TPU v7x, 32 devices: a whole 2x2x4 slice. The times are simulated.
32 devices in a mesh: img: 4 (over y, x), row: 4 (over z), col: 2 (over core).
Axes of the slice: x: 2, y: 2, z: 4, core: 2. Of those that a mesh axis runs over, the one named last changes fastest.
Arguments:
- features: bfloat16 [4, 96, 64, 2048], P('img', 'row', 'col'), may hold values from -6 to 6
- region_boxes: int32 [4, 8, 4], P('img'), may hold values from 0 to 96, as said below
- labels: int32 [4, 96, 64], P('img', 'row', 'col'), may hold values from 0 to 149
- branch_projection_weight: bfloat16 [4, 2048, 512], replicated, may hold values from -0.125 to 0.125
- branch_gain: float32 [4, 512], replicated, may hold values from 0.5 to 1.5
- branch_bias: float32 [4, 512], replicated, may hold values from -3 to 3
- conv_w: bfloat16 [4096, 9, 512], P(('row', 'col')), may hold values from -0.03125 to 0.03125
- conv_gain: float32 [512], replicated, may hold values from 0.5 to 1.5
- conv_bias: float32 [512], replicated, may hold values from -3 to 3
- class_w: bfloat16 [512, 150], replicated, may hold values from -0.75 to 0.75
- class_bias: float32 [150], replicated, may hold values from -4 to 4
Outputs:
- logits: float32 [4, 96, 64, 150], P('img', 'row', 'col')
- feature_grad: float32 [4, 96, 64, 2048], P('img', 'row', 'col')
- branch_w_grad: float32 [4, 2048, 512], P(None, ('row', 'col'))
- branch_gain_grad: float32 [4, 512], replicated
- branch_bias_grad: float32 [4, 512], replicated
- conv_w_grad: float32 [4096, 9, 512], P(('row', 'col'))
- conv_gain_grad: float32 [512], replicated
- conv_bias_grad: float32 [512], replicated
- class_w_grad: float32 [512, 150], replicated
- class_bias_grad: float32 [150], replicated
Inputs may be any that keep to these rules, and one draw needn't show every extreme that they name: `region_boxes`: in every canvas the 8 boxes (y0, x0, y1, x1, ends excluded) tile the 96 x 64 canvas exactly; each is at least 2 cells high and 2 wide.
All inputs are finite; a program needn't handle non-finite values.
Results may differ from a plain program's by a relative error of at most 0.012.
Values may be sent and summed in bfloat16 or wider, within the bound.
No kernel may reach another device: no remote copies, remote signals or barrier semaphores. Data moves between devices by JAX's collectives and lax.ppermute only.
A program may use at most 448 MiB of HBM per device.

v0:
```python
import jax
import jax.numpy as jnp
from jax import lax
from jax.sharding import PartitionSpec as P

bin_scales = (1, 2, 3, 6)
norm_eps = 1e-05
highest_precision = lax.Precision.HIGHEST
tap_offsets = ((-1, -1), (-1, 0), (-1, 1), (0, -1), (0, 0), (0, 1), (1, -1), (1, 0), (1, 1))
contract_first = (((0,), (0,)), ((), ()))
contract_last = (((1,), (1,)), ((), ()))


def extended(cells, sides, width):
    for axis, dim in sides:
        count = lax.axis_size(axis)
        ends = count - 1
        head = lax.slice_in_dim(cells, 0, width, axis=dim)
        tail = lax.slice_in_dim(cells, cells.shape[dim] - width, cells.shape[dim], axis=dim)
        cells = jnp.concatenate(
            [
                lax.ppermute(tail, axis, [(i, (i + 1) % count) for i in range(ends)]),
                cells,
                lax.ppermute(head, axis, [((i + 1) % count, i) for i in range(ends)]),
            ],
            axis=dim,
        )
    return cells


def region_index(canvas_box, row_cells, col_cells):
    upper = canvas_box[:, 0][:, None, None]
    leftmost = canvas_box[:, 1][:, None, None]
    lower = canvas_box[:, 2][:, None, None]
    rightmost = canvas_box[:, 3][:, None, None]
    inside = (row_cells[None, :, None] >= upper) & (row_cells[None, :, None] < lower)
    inside = (
        inside & (col_cells[None, None, :] >= leftmost) & (col_cells[None, None, :] < rightmost)
    )
    number = jnp.arange(1, canvas_box.shape[0] + 1, dtype=jnp.int32)[:, None, None]
    return jnp.sum(inside.astype(jnp.int32) * number, axis=0) - 1


def axis_tables(first, last, cells, bin_scale):
    extent = last - first
    across = jnp.arange(bin_scale, dtype=jnp.int32)
    lo_edge = first[:, None] + across[None, :] * extent[:, None] // bin_scale
    hi_edge = (
        first[:, None] + ((across[None, :] + 1) * extent[:, None] + bin_scale - 1) // bin_scale
    )
    member = (
        (cells[None, None, :] >= lo_edge[:, :, None]) & (cells[None, None, :] < hi_edge[:, :, None])
    ).astype(jnp.float32)
    numer = (cells[None, :] - first[:, None]) * (bin_scale - 1)
    denom = extent[:, None] - 1
    lower_bin = numer // denom
    fraction = (numer - lower_bin * denom).astype(jnp.float32) / denom.astype(jnp.float32)
    upper_bin = jnp.minimum(lower_bin + 1, bin_scale - 1)
    inside = ((cells[None, :] >= first[:, None]) & (cells[None, :] < last[:, None])).astype(
        jnp.float32
    )
    weight = (across[None, :, None] == lower_bin[:, None, :]).astype(jnp.float32) * (
        1.0 - fraction
    )[:, None, :]
    weight = (
        weight
        + (across[None, :, None] == upper_bin[:, None, :]).astype(jnp.float32)
        * fraction[:, None, :]
    )
    weight = weight * inside[:, None, :]
    return (member, (hi_edge - lo_edge).astype(jnp.float32), weight)


def bin_tables(canvas_box, row_cells, col_cells, bin_scale):
    member_y, size_y, weight_y = axis_tables(
        canvas_box[:, 0], canvas_box[:, 2], row_cells, bin_scale
    )
    member_x, size_x, weight_x = axis_tables(
        canvas_box[:, 1], canvas_box[:, 3], col_cells, bin_scale
    )
    bins = canvas_box.shape[0] * bin_scale * bin_scale
    cells = row_cells.shape[0] * col_cells.shape[0]
    average_pooling = (member_y[:, :, None, :, None] * member_x[:, None, :, None, :]).reshape(
        bins, cells
    )
    sizes = (size_y[:, :, None] * size_x[:, None, :]).reshape(bins)
    spread = (weight_y[:, :, None, :, None] * weight_x[:, None, :, None, :]).reshape(bins, cells)
    return (average_pooling, sizes, spread)


def silu_slope(value):
    sigmoid_value = jax.nn.sigmoid(value)
    return sigmoid_value * (1.0 + value * (1.0 - sigmoid_value))


def on_device(
    features,
    region_boxes,
    labels,
    branch_projection_weight,
    branch_gain,
    branch_bias,
    conv_w,
    conv_gain,
    conv_bias,
    class_w,
    class_bias,
):
    tile_h = features.shape[1]
    tile_w = features.shape[2]
    channels_in = features.shape[3]
    pixels = tile_h * tile_w
    img_count = lax.axis_size("img")
    col_count = lax.axis_size("col")
    groups = lax.axis_size("row") * col_count
    width_mid = conv_w.shape[2]
    block_rows = conv_w.shape[0]
    cat_width = block_rows * groups
    branch_width = branch_projection_weight.shape[2]
    regions = region_boxes.shape[1]
    all_cells = img_count * tile_h * lax.axis_size("row") * tile_w * col_count
    top_row = lax.axis_index("row") * tile_h
    left_col = lax.axis_index("col") * tile_w
    row_cells = top_row + jnp.arange(tile_h, dtype=jnp.int32)
    col_cells = left_col + jnp.arange(tile_w, dtype=jnp.int32)
    canvas_box = region_boxes[0]
    feature_rows = features[0].reshape(pixels, channels_in)
    tables = [bin_tables(canvas_box, row_cells, col_cells, bin_scale) for bin_scale in bin_scales]
    average_pooling = jnp.concatenate([entry[0] for entry in tables], axis=0)
    sizes = jnp.concatenate([entry[1] for entry in tables], axis=0)
    limits = [0]
    for bin_scale in bin_scales:
        limits.append(limits[-1] + regions * bin_scale * bin_scale)
    local_sums = jnp.dot(
        average_pooling.astype(jnp.bfloat16), feature_rows, preferred_element_type=jnp.float32
    )
    bin_sum = lax.psum(local_sums, ("row", "col"))
    pooled_features = (bin_sum / sizes[:, None]).astype(jnp.bfloat16)
    pre_list = [
        jnp.dot(
            pooled_features[limits[branch_position] : limits[branch_position + 1]],
            branch_projection_weight[branch_position],
            preferred_element_type=jnp.float32,
        )
        for branch_position in range(4)
    ]
    first_sum = jnp.stack(
        [jnp.sum(branch_preactivation, axis=0) for branch_preactivation in pre_list]
    )
    second_sum = jnp.stack(
        [
            jnp.sum(branch_preactivation * branch_preactivation, axis=0)
            for branch_preactivation in pre_list
        ]
    )
    first_sum, second_sum = lax.psum((first_sum, second_sum), "img")
    normed_list, before_list, inverse_list, upsampled = ([], [], [], [])
    for branch_position, bin_scale in enumerate(bin_scales):
        members = img_count * regions * bin_scale * bin_scale
        center = first_sum[branch_position] / members
        variance = second_sum[branch_position] / members - center * center
        inverse = lax.rsqrt(variance + norm_eps)
        normed = (pre_list[branch_position] - center) * inverse
        before = branch_gain[branch_position] * normed + branch_bias[branch_position]
        spread_up = lax.dot_general(
            tables[branch_position][2],
            jax.nn.silu(before),
            contract_first,
            precision=highest_precision,
        )
        normed_list.append(normed)
        before_list.append(before)
        inverse_list.append(inverse)
        upsampled.append(spread_up.astype(jnp.bfloat16))
    joined = jnp.concatenate([feature_rows] + upsampled, axis=1)
    padded = extended(joined.reshape(1, tile_h, tile_w, cat_width), (("row", 1), ("col", 2)), 1)[0]

    def masks_at(top, left):
        region_rim = region_index(
            canvas_box,
            top - 1 + jnp.arange(tile_h + 2, dtype=jnp.int32),
            left - 1 + jnp.arange(tile_w + 2, dtype=jnp.int32),
        )
        region_core = region_rim[1:-1, 1:-1]
        return jnp.stack(
            [
                (
                    region_rim[
                        1 + shift_y : 1 + shift_y + tile_h, 1 + shift_x : 1 + shift_x + tile_w
                    ]
                    == region_core
                ).reshape(pixels)
                for shift_y, shift_x in tap_offsets
            ]
        ).astype(jnp.bfloat16)

    masks = masks_at(top_row, left_col)

    def windows_with(taken, tile_masks):
        amount = taken.shape[2]
        windows = [
            taken[1 + shift_y : 1 + shift_y + tile_h, 1 + shift_x : 1 + shift_x + tile_w].reshape(
                pixels, amount
            )
            * tile_masks[tap_index][:, None]
            for tap_index, (shift_y, shift_x) in enumerate(tap_offsets)
        ]
        return jnp.stack(windows, axis=2).reshape(pixels, amount * 9)

    def tap_windows(source):
        return windows_with(source, masks)

    shard_piece = lax.all_gather(conv_w, ("row", "col"), axis=0, tiled=True)
    amount = shard_piece.shape[0]
    hidden = jnp.dot(
        tap_windows(padded),
        shard_piece.reshape(amount * 9, width_mid),
        preferred_element_type=jnp.float32,
    )
    moment_one = jnp.sum(hidden, axis=0)
    moment_two = jnp.sum(hidden * hidden, axis=0)
    moment_one, moment_two = lax.psum((moment_one, moment_two), ("img", "row", "col"))
    center_mid = moment_one / all_cells
    variance_mid = moment_two / all_cells - center_mid * center_mid
    inverse_mid = lax.rsqrt(variance_mid + norm_eps)
    normed_mid = (hidden - center_mid) * inverse_mid
    before_mid = conv_gain * normed_mid + conv_bias
    act_mid = jax.nn.silu(before_mid).astype(jnp.bfloat16)
    logits = jnp.dot(act_mid, class_w, preferred_element_type=jnp.float32) + class_bias
    classes = class_w.shape[1]
    onehot = (
        labels[0].reshape(pixels)[:, None] == jnp.arange(classes, dtype=jnp.int32)[None, :]
    ).astype(jnp.float32)
    grad_logits = (jax.nn.softmax(logits, axis=-1) - onehot).astype(jnp.bfloat16)
    class_term = lax.dot_general(
        act_mid, grad_logits, contract_first, preferred_element_type=jnp.float32
    )
    bias_term = jnp.sum(grad_logits.astype(jnp.float32), axis=0)
    grad_before = lax.dot_general(
        grad_logits, class_w, contract_last, preferred_element_type=jnp.float32
    ) * silu_slope(before_mid)
    gain_term = jnp.sum(grad_before * normed_mid, axis=0)
    shift_term = jnp.sum(grad_before, axis=0)
    class_w_grad, class_bias_grad, conv_gain_grad, conv_bias_grad = lax.psum(
        (class_term, bias_term, gain_term, shift_term), ("img", "row", "col")
    )
    grad_hidden = (
        conv_gain
        * inverse_mid
        * (grad_before - conv_bias_grad / all_cells - normed_mid * conv_gain_grad / all_cells)
    ).astype(jnp.bfloat16)
    grad_pad = extended(
        grad_hidden.reshape(1, tile_h, tile_w, width_mid), (("row", 1), ("col", 2)), 1
    )[0]
    shifted = jnp.stack(
        [
            grad_pad[
                1 - shift_y : 1 - shift_y + tile_h, 1 - shift_x : 1 - shift_x + tile_w
            ].reshape(pixels, width_mid)
            * masks[8 - tap_index][:, None]
            for tap_index, (shift_y, shift_x) in enumerate(tap_offsets)
        ],
        axis=1,
    ).reshape(pixels, 9 * width_mid)
    shard_piece = lax.all_gather(conv_w, ("row", "col"), axis=0, tiled=True)
    grad_joined = lax.dot_general(
        shifted,
        shard_piece.reshape(shard_piece.shape[0], 9 * width_mid),
        contract_last,
        preferred_element_type=jnp.float32,
    )
    bin_parts = []
    for branch_position in range(4):
        lower_channel = channels_in + branch_position * branch_width
        grad_up = grad_joined[:, lower_channel : lower_channel + branch_width]
        bin_parts.append(jnp.dot(tables[branch_position][2], grad_up, precision=highest_precision))
    grad_bins = lax.psum(jnp.concatenate(bin_parts, axis=0), ("row", "col"))
    grad_act_list, gain_terms, shift_terms = ([], [], [])
    for branch_position in range(4):
        grad_act = grad_bins[limits[branch_position] : limits[branch_position + 1]] * silu_slope(
            before_list[branch_position]
        )
        grad_act_list.append(grad_act)
        gain_terms.append(jnp.sum(grad_act * normed_list[branch_position], axis=0))
        shift_terms.append(jnp.sum(grad_act, axis=0))
    branch_gain_grad, branch_bias_grad = lax.psum(
        (jnp.stack(gain_terms), jnp.stack(shift_terms)), "img"
    )
    block = channels_in // groups
    group_index = lax.axis_index(("row", "col"))
    grad_pool_list, weight_terms = ([], [])
    for branch_position, bin_scale in enumerate(bin_scales):
        members = img_count * regions * bin_scale * bin_scale
        grad_pre = (
            branch_gain[branch_position]
            * inverse_list[branch_position]
            * (
                grad_act_list[branch_position]
                - branch_bias_grad[branch_position] / members
                - normed_list[branch_position] * branch_gain_grad[branch_position] / members
            )
        ).astype(jnp.bfloat16)
        grad_pool_list.append(
            lax.dot_general(
                grad_pre,
                branch_projection_weight[branch_position],
                contract_last,
                preferred_element_type=jnp.float32,
            )
        )
        pooled_part = lax.dynamic_slice_in_dim(
            pooled_features[limits[branch_position] : limits[branch_position + 1]],
            group_index * block,
            block,
            1,
        )
        weight_terms.append(
            lax.dot_general(
                pooled_part, grad_pre, contract_first, preferred_element_type=jnp.float32
            )
        )
    weight_terms = jnp.stack(weight_terms)
    grad_sizes = jnp.concatenate(grad_pool_list, axis=0) / sizes[:, None]
    grad_pool = lax.dot_general(
        average_pooling, grad_sizes, contract_first, precision=highest_precision
    )
    feature_grad = (grad_joined[:, :channels_in] + grad_pool).reshape(
        1, tile_h, tile_w, channels_in
    )
    columns = tap_windows(padded)
    conv_share = lax.psum_scatter(
        lax.dot_general(
            columns, grad_hidden, contract_first, preferred_element_type=jnp.float32
        ).reshape(block_rows * lax.axis_size(("row", "col")), 9, width_mid),
        ("row", "col"),
        scatter_dimension=0,
        tiled=True,
    )
    conv_w_grad, branch_w_grad = (
        lax.psum(conv_share.astype(jnp.bfloat16), "img").astype(jnp.float32),
        lax.psum(weight_terms.astype(jnp.bfloat16), "img").astype(jnp.float32),
    )
    return (
        logits.reshape(1, tile_h, tile_w, classes),
        feature_grad,
        branch_w_grad,
        branch_gain_grad,
        branch_bias_grad,
        conv_w_grad,
        conv_gain_grad,
        conv_bias_grad,
        class_w_grad,
        class_bias_grad,
    )


def solution(mesh):
    return jax.shard_map(
        on_device,
        mesh=mesh,
        in_specs=(
            P("img", "row", "col", None),
            P("img", None, None),
            P("img", "row", "col"),
            P(),
            P(),
            P(),
            P(("row", "col"), None, None),
            P(),
            P(),
            P(),
            P(),
        ),
        out_specs=(
            P("img", "row", "col", None),
            P("img", "row", "col", None),
            P(None, ("row", "col"), None),
            P(),
            P(),
            P(("row", "col"), None, None),
            P(),
            P(),
            P(),
            P(),
        ),
        check_vma=False,
    )
```

profile of v0, /device:TPU:0, one launch (start us, length us, event | category | flops | bytes accessed | tf_op | source)
XLA Modules:
  0.0 2010.0 jit_solution(4138477172162444139)
XLA Ops:
  10.0 2.1 broadcast_multiply_fusion.1
  12.1 2.5 mul.1429
  15.7 5.0 fusion.48
  24.6 2.1 broadcast_multiply_fusion
  26.7 2.5 mul.1527
  29.4 4.1 constant_dynamic-update-slice_fusion.8
  33.5 69.4 %all-reduce.10.cloned.1.call-done = f32[400,2048]{1,0:T(8,128)} async-done(((f32[400,2048]{1,0:T(8,128)}), f32[400,2048]{1,0:T(8,128)}) %all-reduce.10.cloned.1.call-update) | async-done | bytes 3276816 | tf_op jit(solution)/shard_map/psum | solution.py:137
  102.9 2.4 divide_convert_fusion
  105.3 2.6 fusion.201
  107.9 2.1 fusion.199
  110.0 2.5 fusion.197
  112.4 2.8 fusion.195
  115.3 16.3 all-reduce.3
  132.4 1.4 convolution_convert_fusion
  134.8 1.4 convolution_convert_fusion.3
  137.2 1.4 convolution_convert_fusion.2
  139.7 2.8 convolution_convert_fusion.1
  145.8 4.6 collective-permute-start
  150.6 12.7 collective-permute-done.1
  163.3 2.4 pad_maximum_fusion.4
  167.5 3.1 collective-permute-start.2
  172.6 6.8 maximum_bitcast_fusion
  179.4 18.9 fusion.202
  198.3 7.6 constant_dynamic-update-slice_fusion.17
  206.0 5.4 constant_dynamic-update-slice_fusion.16
  211.4 5.3 constant_dynamic-update-slice_fusion.15
  216.7 8.1 constant_dynamic-update-slice_fusion.14
  224.8 5.4 constant_dynamic-update-slice_fusion.13
  230.3 5.6 constant_dynamic-update-slice_fusion.12
  235.8 7.9 constant_dynamic-update-slice_fusion.11
  243.8 5.4 constant_dynamic-update-slice_fusion.10
  249.2 5.4 constant_dynamic-update-slice_fusion.9
  254.6 180.2 %all-gather.2.cloned.1.call-done = bf16[4096,9,512]{2,0,1:T(8,128)(2,1)} async-done(((bf16[512,9,512]{2,0,1:T(8,128)(2,1)}), bf16[4096,9,512]{2,0,1:T(8,128)(2,1)}) %all-gather.2.cloned.1.call-update) | async-done | bytes 37748752 | tf_op jit(solution)/shard_map/all_gather | solution.py:213
  434.8 38.5 %bitcast_reduce_fusion = (f32[512]{0:T(512)S(1)}, f32[512]{0:T(512)S(1)}, f32[768,512,1]{1,0,2:T(8,128)S(1)}) fusion(bf16[768,4096,9]{1,0,2:T(8,128)(2,1)} %constant_dynamic-update-slice_fusion.9, bf16[4096,9,512]{2,0,1:T(8,128)(2,1)} %all-gather.2.cloned.1.call-done), kind=kOutput, calls=%fused_computation.59 | convolution fusion | flops 28992208896 | bytes 95948800 | tf_op jit(solution)/shard_map/dot_general | solution.py:215
  473.3 39.1 %all-reduce.1 = (f32[512]{0:T(512)S(1)}, f32[512]{0:T(512)S(1)}) all-reduce(f32[512]{0:T(512)S(1)} %get-tuple-element.25, f32[512]{0:T(512)S(1)} %get-tuple-element.24), channel_id=1, replica_groups=mesh['img'=4,'row'=4,'col'=2] {'img','row','col'}, use_global_device_ids=true, to_apply=%region_15.18 | all-reduce | flops 1024 | bytes 8192 | tf_op jit(solution)/shard_map/psum | solution.py:222
  514.3 2.1 fusion.193
  516.5 40.2 %all-reduce = (f32[512]{0:T(512)S(1)}, f32[512]{0:T(512)S(1)}, f32[150]{0:T(256)}) all-reduce(f32[512]{0:T(512)S(1)} %get-tuple-element.23, f32[512]{0:T(512)S(1)} %get-tuple-element.22, f32[150]{0:T(256)S(1)} %get-tuple-element.74), channel_id=1, replica_groups=mesh['img'=4,'row'=4,'col'=2] {'img','row','col'}, use_global_device_ids=true, to_apply=%region_21.24 | all-reduce | flops 1174 | bytes 9392 | tf_op jit(solution)/shard_map/psum | solution.py:244
  557.2 1.9 multiply_convert_fusion
  560.5 4.5 collective-permute-start.4
  565.0 1.6 collective-permute-done.4
  568.0 3.0 collective-permute-start.6
  571.0 113.5 %copy.62 = bf16[768,4096,9]{0,2,1:T(8,128)(2,1)} copy(bf16[768,4096,9]{1,0,2:T(8,128)(2,1)} %constant_dynamic-update-slice_fusion.9) | data formatting | bytes 113246208 | tf_op jit(solution)/shard_map/stack | solution.py:208
  684.5 100.8 %reshape.2561 = bf16[768,36864]{0,1:T(8,128)(2,1)} reshape(bf16[768,4096,9]{0,2,1:T(8,128)(2,1)} %copy.62) | data formatting | bytes 113246208 | tf_op jit(solution)/shard_map/reshape | solution.py:208
  785.3 97.8 %dot_general.115 = bf16[4096,9,768]{2,1,0:T(8,128)(2,1)} reshape(bf16[36864,768]{1,0:T(8,128)(2,1)} %bitcast.245) | data formatting | bytes 113246208 | tf_op jit(solution)/shard_map/dot_general | solution.py:332
  895.1 37.6 %convolution_bitcast_fusion = f32[768,4096]{1,0:T(8,128)} fusion(bf16[768,9,512]{2,0,1:T(8,128)(2,1)} %constant_dynamic-update-slice_fusion.18, bf16[4096,9,512]{2,0,1:T(8,128)(2,1)} %all-gather.2.cloned.1.call-done), kind=kOutput, calls=%fused_computation.3 | convolution fusion | flops 28991029248 | bytes 57409536 | tf_op jit(solution)/shard_map/dot_general | solution.py:266
  932.6 3.1 fusion.33
  935.7 2.5 fusion.35
  938.2 2.4 fusion.37
  940.6 2.3 fusion.39
  943.9 68.8 %fusion = f32[4096,9,512]{2,0,1:T(8,128)} fusion(bf16[4096,9,768]{2,1,0:T(8,128)(2,1)} %dot_general.115, bf16[768,512]{1,0:T(8,128)(2,1)S(1)} %multiply_convert_fusion), kind=kOutput, calls=%fused_computation | convolution fusion | flops 28991029248 | bytes 132907008 | tf_op jit(solution)/shard_map/dot_general | solution.py:332
  1016.4 1.4 fusion.194
  1017.8 17.0 all-reduce.2
  1037.4 696.1 %reduce-scatter.2.cloned.1.call-done = f32[512,9,512]{2,0,1:T(8,128)} async-done(((f32[4096,9,512]{2,0,1:T(8,128)}), f32[512,9,512]{2,0,1:T(8,128)}) %reduce-scatter.2.cloned.1.call-update) | async-done | bytes 9437200 | tf_op jit(solution)/shard_map/reduce_scatter | solution.py:331
  1733.5 6.5 convert_element_type.281
  1742.6 2.9 fusion.8
  1745.5 2.3 fusion.12
  1747.8 2.3 fusion.16
  1750.1 2.2 fusion.20
  1752.4 14.2 slice_add_fusion
  1766.6 102.1 %all-reduce.16.cloned.1.call-done = (bf16[4,256,512]{2,1,0:T(8,128)(2,1)}, bf16[512,9,512]{2,0,1:T(8,128)(2,1)}) async-done(((bf16[4,256,512]{2,1,0:T(8,128)(2,1)}, bf16[512,9,512]{2,0,1:T(8,128)(2,1)}), (bf16[4,256,512]{2,1,0:T(8,128)(2,1)}, bf16[512,9,512]{2,0,1:T(8,128)(2,1)})) %all-reduce.16.cloned.1.call-update) | async-done | bytes 5767184 | tf_op jit(solution)/shard_map/psum | solution.py:341
  1868.7 2.8 convert_element_type.280
  1871.5 7.4 convert_element_type.282
  1878.9 122.0 %all-reduce.14.cloned.1.call-done = f32[512,150]{0,1:T(8,128)} async-done(((f32[512,150]{0,1:T(8,128)}), f32[512,150]{0,1:T(8,128)}) %all-reduce.14.cloned.1.call-update) | async-done | bytes 307216 | tf_op jit(solution)/shard_map/psum | solution.py:244
  2001.0 1.7 copy.94
  (371 shorter events, 44.8 us)
Async XLA Ops:
  7.2 505.7 %copy-start = (bf16[512,150]{0,1:T(8,128)(2,1)S(1)}, bf16[512,150]{0,1:T(8,128)(2,1)}, u32[]{:S(2)}) copy-start(bf16[512,150]{0,1:T(8,128)(2,1)} %param.24) | copy-start | bytes 460804
  7.2 95.7 %all-reduce.10.cloned.1.call-start = ((), (), s32[]{:S(2)}) async-start(), calls=%async_computation.1 | async-start | bytes 6553600 | tf_op jit(solution)/shard_map/psum | solution.py:137
  20.8 414.0 %all-gather.2.cloned.1.call-start = ((), (), s32[]{:S(2)}) async-start(), calls=%async_computation.2 | async-start | bytes 42467328 | tf_op jit(solution)/shard_map/all_gather | solution.py:213
  21.6 991.5 %all-reduce.12.cloned.1.call-start = ((), (), s32[]{:S(2)}) async-start(), calls=%async_computation.3 | async-start | bytes 1638400 | tf_op jit(solution)/shard_map/psum | solution.py:277
  22.7 109.6 %copy-start.24 = (f32[8,768]{1,0:T(8,128)}, f32[8,768]{1,0:T(8,128)S(1)}, u32[]{:S(2)}) copy-start(f32[8,768]{1,0:T(8,128)S(1)} %mul.1384) | copy-start | bytes 73732
  23.3 109.1 %copy-start.50 = (f32[1,512]{1,0:T(1,128)}, f32[1,512]{1,0:T(1,128)S(1)}, u32[]{:S(2)}) copy-start(f32[1,512]{1,0:T(1,128)S(1)} %slice.327) | copy-start | bytes 6148
  24.1 110.7 %copy-start.18 = (f32[32,768]{1,0:T(8,128)}, f32[32,768]{1,0:T(8,128)S(1)}, u32[]{:S(2)}) copy-start(f32[32,768]{1,0:T(8,128)S(1)} %mul.1471) | copy-start | bytes 294916
  24.5 112.7 %copy-start.12 = (f32[72,768]{1,0:T(8,128)}, f32[72,768]{1,0:T(8,128)S(1)}, u32[]{:S(2)}) copy-start(f32[72,768]{1,0:T(8,128)S(1)} %mul.1499) | copy-start | bytes 663556
  29.2 110.5 %copy-start.8 = (f32[288,768]{1,0:T(8,128)}, f32[288,768]{1,0:T(8,128)S(1)}, u32[]{:S(2)}) copy-start(f32[288,768]{1,0:T(8,128)S(1)} %mul.1527) | copy-start | bytes 2654212
  29.3 78.6 %copy-start.80 = (f32[400]{0:T(512)}, f32[400]{0:T(512)S(1)}, u32[]{:S(2)}) copy-start(f32[400]{0:T(512)S(1)} %pad_maximum_fusion.12) | copy-start | bytes 4804
  29.4 103.0 %copy-start.52 = (f32[1,512]{1,0:T(1,128)}, f32[1,512]{1,0:T(1,128)S(1)}, u32[]{:S(2)}) copy-start(f32[1,512]{1,0:T(1,128)S(1)} %get-tuple-element.141) | copy-start | bytes 6148
  29.4 105.4 %copy-start.48 = (f32[1,512]{1,0:T(1,128)}, f32[1,512]{1,0:T(1,128)S(1)}, u32[]{:S(2)}) copy-start(f32[1,512]{1,0:T(1,128)S(1)} %get-tuple-element.140) | copy-start | bytes 6148
  29.4 107.8 %copy-start.46 = (f32[1,512]{1,0:T(1,128)}, f32[1,512]{1,0:T(1,128)S(1)}, u32[]{:S(2)}) copy-start(f32[1,512]{1,0:T(1,128)S(1)} %get-tuple-element.142) | copy-start | bytes 6148
  29.4 110.3 %copy-start.82 = (f32[1,512]{1,0:T(1,128)}, f32[1,512]{1,0:T(1,128)S(1)}, u32[]{:S(2)}) copy-start(f32[1,512]{1,0:T(1,128)S(1)} %get-tuple-element.139) | copy-start | bytes 6148
  107.9 24.5 %copy-start.22 = (f32[8,512]{1,0:T(8,128)}, f32[8,512]{1,0:T(8,128)S(1)}, u32[]{:S(2)}) copy-start(f32[8,512]{1,0:T(8,128)S(1)} %get-tuple-element.214) | copy-start | bytes 49156
  109.9 24.9 %copy-start.20 = (f32[32,512]{1,0:T(8,128)}, f32[32,512]{1,0:T(8,128)S(1)}, u32[]{:S(2)}) copy-start(f32[32,512]{1,0:T(8,128)S(1)} %get-tuple-element.213) | copy-start | bytes 196612
  112.4 24.8 %copy-start.14 = (f32[72,512]{1,0:T(8,128)}, f32[72,512]{1,0:T(8,128)S(1)}, u32[]{:S(2)}) copy-start(f32[72,512]{1,0:T(8,128)S(1)} %get-tuple-element.212) | copy-start | bytes 442372
  115.3 28.2 %copy-start.10 = (f32[288,512]{1,0:T(8,128)}, f32[288,512]{1,0:T(8,128)S(1)}, u32[]{:S(2)}) copy-start(f32[288,512]{1,0:T(8,128)S(1)} %get-tuple-element.211) | copy-start | bytes 1769476
  132.3 11.1 copy-start.38
  142.5 29.0 %copy-start.73 = (s32[1,24,32]{2,1,0:T(8,128)S(1)}, s32[1,24,32]{2,1,0:T(8,128)}, u32[]{:S(2)}) copy-start(s32[1,24,32]{2,1,0:T(8,128)} %param.17) | copy-start | bytes 9220
  144.5 18.7 collective-permute-start.1
  145.8 17.4 collective-permute-start
  166.0 5.8 collective-permute-start.3
  167.5 4.7 collective-permute-start.2
  171.6 26.7 %copy-start.54 = (bf16[768]{0:T(1024)(128)(2,1)}, bf16[768]{0:T(1024)(128)(2,1)S(1)}, u32[]{:S(2)}) copy-start(bf16[768]{0:T(1024)(128)(2,1)S(1)} %get-tuple-element.46) | copy-start | bytes 4612
  171.6 34.4 %copy-start.56 = (bf16[768]{0:T(1024)(128)(2,1)}, bf16[768]{0:T(1024)(128)(2,1)S(1)}, u32[]{:S(2)}) copy-start(bf16[768]{0:T(1024)(128)(2,1)S(1)} %get-tuple-element.45) | copy-start | bytes 4612
  171.7 39.7 %copy-start.58 = (bf16[768]{0:T(1024)(128)(2,1)}, bf16[768]{0:T(1024)(128)(2,1)S(1)}, u32[]{:S(2)}) copy-start(bf16[768]{0:T(1024)(128)(2,1)S(1)} %get-tuple-element.44) | copy-start | bytes 4612
  171.7 45.1 %copy-start.60 = (bf16[768]{0:T(1024)(128)(2,1)}, bf16[768]{0:T(1024)(128)(2,1)S(1)}, u32[]{:S(2)}) copy-start(bf16[768]{0:T(1024)(128)(2,1)S(1)} %get-tuple-element.43) | copy-start | bytes 4612
  171.7 53.1 %copy-start.62 = (bf16[768]{0:T(1024)(128)(2,1)}, bf16[768]{0:T(1024)(128)(2,1)S(1)}, u32[]{:S(2)}) copy-start(bf16[768]{0:T(1024)(128)(2,1)S(1)} %get-tuple-element.42) | copy-start | bytes 4612
  171.7 58.6 %copy-start.64 = (bf16[768]{0:T(1024)(128)(2,1)}, bf16[768]{0:T(1024)(128)(2,1)S(1)}, u32[]{:S(2)}) copy-start(bf16[768]{0:T(1024)(128)(2,1)S(1)} %get-tuple-element.41) | copy-start | bytes 4612
  171.7 64.1 %copy-start.66 = (bf16[768]{0:T(1024)(128)(2,1)}, bf16[768]{0:T(1024)(128)(2,1)S(1)}, u32[]{:S(2)}) copy-start(bf16[768]{0:T(1024)(128)(2,1)S(1)} %get-tuple-element.40) | copy-start | bytes 4612
  171.7 72.1 %copy-start.68 = (bf16[768]{0:T(1024)(128)(2,1)}, bf16[768]{0:T(1024)(128)(2,1)S(1)}, u32[]{:S(2)}) copy-start(bf16[768]{0:T(1024)(128)(2,1)S(1)} %get-tuple-element.39) | copy-start | bytes 4612
  171.7 77.5 %copy-start.70 = (bf16[768]{0:T(1024)(128)(2,1)}, bf16[768]{0:T(1024)(128)(2,1)S(1)}, u32[]{:S(2)}) copy-start(bf16[768]{0:T(1024)(128)(2,1)S(1)} %get-tuple-element.38) | copy-start | bytes 4612
  198.3 13.0 slice-start.8
  211.4 13.4 slice-start.6
  216.7 13.5 slice-start.4
  230.3 13.5 slice-start.2
  235.8 13.4 slice-start
  254.6 257.8 %copy-start.79 = (f32[512]{0:T(512)S(1)}, f32[512]{0:T(512)}, u32[]{:S(2)}) copy-start(f32[512]{0:T(512)} %param.22) | copy-start | bytes 6148
  254.6 257.8 %copy-start.89 = (f32[512]{0:T(512)S(1)}, f32[512]{0:T(512)}, u32[]{:S(2)}) copy-start(f32[512]{0:T(512)} %param.23) | copy-start | bytes 6148
  254.6 258.3 %copy-start.91 = (f32[150]{0:T(256)S(1)}, f32[150]{0:T(256)}, u32[]{:S(2)}) copy-start(f32[150]{0:T(256)} %param.25) | copy-start | bytes 1804
  556.7 127.8 %copy-start.88 = (f32[512]{0:T(512)}, f32[512]{0:T(512)S(1)}, u32[]{:S(2)}) copy-start(f32[512]{0:T(512)S(1)} %get-tuple-element.233) | copy-start | bytes 6148
  559.2 5.9 collective-permute-start.5
  560.5 6.1 collective-permute-start.4
  566.7 316.5 %collective-permute-start.7 = (bf16[1,26,1,512]{3,2,1,0:T(2,128)(2,1)S(1)}, bf16[1,26,1,512]{3,2,1,0:T(2,128)(2,1)S(1)}, u32[]{:S(2)}, u32[]{:S(2)}) collective-permute-start(bf16[1,26,1,512]{3,2,1,0:T(2,128)(2,1)S(1)} %get-tuple-element.107), channel_id=1, source_target_pairs={{1,0},{3,2},{5,4},{7,6},{9,8},{11,10},{13,12},{15,14},{17,16},{19,... | collective-permute-start | bytes 79880 | tf_op jit(solution)/shard_map/ppermute | solution.py:24
  568.0 315.2 %collective-permute-start.6 = (bf16[1,26,1,512]{3,2,1,0:T(2,128)(2,1)S(1)}, bf16[1,26,1,512]{3,2,1,0:T(2,128)(2,1)S(1)}, u32[]{:S(2)}, u32[]{:S(2)}) collective-permute-start(bf16[1,26,1,512]{3,2,1,0:T(2,128)(2,1)S(1)} %get-tuple-element.106), channel_id=1, source_target_pairs={{0,1},{2,3},{4,5},{6,7},{8,9},{10,11},{12,13},{14,15},{16,17},{18,... | collective-permute-start | bytes 79880 | tf_op jit(solution)/shard_map/ppermute | solution.py:22
  895.1 37.6 %copy-start.9 = (f32[288,768]{1,0:T(8,128)S(1)}, f32[288,768]{1,0:T(8,128)}, u32[]{:S(2)}) copy-start(f32[288,768]{1,0:T(8,128)} %copy-done.8) | copy-start | bytes 2654212
  895.1 40.6 %copy-start.13 = (f32[72,768]{1,0:T(8,128)S(1)}, f32[72,768]{1,0:T(8,128)}, u32[]{:S(2)}) copy-start(f32[72,768]{1,0:T(8,128)} %copy-done.12) | copy-start | bytes 663556
  895.1 43.1 %copy-start.19 = (f32[32,768]{1,0:T(8,128)S(1)}, f32[32,768]{1,0:T(8,128)}, u32[]{:S(2)}) copy-start(f32[32,768]{1,0:T(8,128)} %copy-done.18) | copy-start | bytes 294916
  943.8 789.7 %reduce-scatter.2.cloned.1.call-start = ((), (), s32[]{:S(2)}) async-start(), calls=%async_computation.4 | async-start | bytes 84934656 | tf_op jit(solution)/shard_map/reduce_scatter | solution.py:331
  1012.8 22.0 %copy-start.84 = (f32[1,512]{1,0:T(1,128)S(1)}, f32[1,512]{1,0:T(1,128)}, u32[]{:S(2)}) copy-start(f32[1,512]{1,0:T(1,128)} %get-tuple-element.110) | copy-start | bytes 6148
  1012.8 22.0 %slice-start.13 = ((bf16[400,2048]{1,0:T(8,128)(2,1)}), bf16[8,2048]{1,0:T(8,128)(2,1)S(1)}, s32[]{:S(2)}) async-start(bf16[400,2048]{1,0:T(8,128)(2,1)} %copy-done.7), calls=%async_computation.20 | async-start | bytes 65536 | tf_op jit(solution)/shard_map/slice | solution.py:141
  1012.9 22.3 %copy-start.76 = (f32[1,512]{1,0:T(1,128)S(1)}, f32[1,512]{1,0:T(1,128)}, u32[]{:S(2)}) copy-start(f32[1,512]{1,0:T(1,128)} %get-tuple-element.112) | copy-start | bytes 6148
  1012.9 22.3 %slice-start.12 = ((bf16[400,2048]{1,0:T(8,128)(2,1)}), bf16[32,2048]{1,0:T(8,128)(2,1)S(1)}, s32[]{:S(2)}) async-start(bf16[400,2048]{1,0:T(8,128)(2,1)} %copy-done.7), calls=%async_computation.19 | async-start | bytes 262144 | tf_op jit(solution)/shard_map/slice | solution.py:141
  1012.9 22.6 %copy-start.75 = (f32[1,512]{1,0:T(1,128)S(1)}, f32[1,512]{1,0:T(1,128)}, u32[]{:S(2)}) copy-start(f32[1,512]{1,0:T(1,128)} %get-tuple-element.114) | copy-start | bytes 6148
  1012.9 22.6 %slice-start.11 = ((bf16[400,2048]{1,0:T(8,128)(2,1)}), bf16[72,2048]{1,0:T(8,128)(2,1)S(1)}, s32[]{:S(2)}) async-start(bf16[400,2048]{1,0:T(8,128)(2,1)} %copy-done.7), calls=%async_computation.18 | async-start | bytes 589824 | tf_op jit(solution)/shard_map/slice | solution.py:141
  1012.9 22.9 %copy-start.74 = (f32[1,512]{1,0:T(1,128)S(1)}, f32[1,512]{1,0:T(1,128)}, u32[]{:S(2)}) copy-start(f32[1,512]{1,0:T(1,128)} %get-tuple-element.68) | copy-start | bytes 6148
  1012.9 23.1 %slice-start.10 = ((bf16[400,2048]{1,0:T(8,128)(2,1)}), bf16[288,2048]{1,0:T(8,128)(2,1)S(1)}, s32[]{:S(2)}) async-start(bf16[400,2048]{1,0:T(8,128)(2,1)} %copy-done.7), calls=%async_computation.17 | async-start | bytes 2359296 | tf_op jit(solution)/shard_map/slice | solution.py:141
  1012.9 855.7 %all-reduce.16.cloned.1.call-start = ((), (), s32[]{:S(2)}) async-start(), calls=%async_computation.6 | async-start | bytes 11534336 | tf_op jit(solution)/shard_map/psum | solution.py:341
  1034.8 705.2 %copy-start.86 = (f32[4,512]{1,0:T(4,128)}, f32[4,512]{1,0:T(4,128)S(1)}, u32[]{:S(2)}) copy-start(f32[4,512]{1,0:T(4,128)S(1)} %get-tuple-element.230) | copy-start | bytes 24580
  1034.8 705.2 %copy-start.87 = (f32[4,512]{1,0:T(4,128)}, f32[4,512]{1,0:T(4,128)S(1)}, u32[]{:S(2)}) copy-start(f32[4,512]{1,0:T(4,128)S(1)} %get-tuple-element.231) | copy-start | bytes 24580
  1037.4 702.9 %copy-start.4 = (f32[768,150]{0,1:T(8,128)S(1)}, f32[768,150]{0,1:T(8,128)}, u32[]{:S(2)}) copy-start(f32[768,150]{0,1:T(8,128)} %copy-done.3) | copy-start | bytes 1382404
  1740.1 260.9 %all-reduce.14.cloned.1.call-start = ((), (), s32[]{:S(2)}) async-start(), calls=%async_computation.5 | async-start | bytes 622592 | tf_op jit(solution)/shard_map/psum | solution.py:244
  1871.5 131.2 %copy-start.1 = (bf16[512,150]{0,1:T(8,128)(2,1)S(1)}, bf16[512,150]{0,1:T(8,128)(2,1)}, u32[]{:S(2)}) copy-start(bf16[512,150]{0,1:T(8,128)(2,1)} %param.24) | copy-start | bytes 460804
  (58 other events, 255.3 us)
Sparse Core Ops, SparseCore 0:
  20.9 81.9 all-reduce.9
  104.6 330.1 all-gather.1
  944.0 58.4 all-reduce.11
  1013.0 720.4 reduce-scatter.1
  1740.2 128.4 all-reduce.15
  1875.3 125.5 all-reduce.13
where the time goes:
time: 2030 us; the launch traced here: 2010 us
  waiting for transfers between devices  1180 us (58%)
  local copies, waits for them, and re-layouts  356 us (18%)
  matrix products  206 us (10%)
  other arithmetic  114 us (6%)
  blocking collectives  113 us (6%)
  starting transfers between devices  20.9 us (1%)
    reduce_scatter x1, waiting for transfers between devices, on_device(): lax.psum_scatter(lax.dot_general(columns, grad_hidden, contract_first, pr...  696 us
    all_gather x1, waiting for transfers between devices, on_device(): shard_piece = lax.all_gather(conv_w, ('row', 'col'), axis=0, tiled=True)  180 us
    psum x1, waiting for transfers between devices, on_device(): lax.psum((class_term, bias_term, gain_term, shift_term), ('img', 'row', '...  122 us
    another operation x1, local copies, waits for them, and re-layouts, windows_with(): return jnp.stack(windows, axis=2).reshape(pixels, amount * 9)  113 us
    psum x1, waiting for transfers between devices, on_device(): lax.psum(weight_terms.astype(jnp.bfloat16), 'img').astype(jnp.float32)  102 us
    reshape x1, local copies, waits for them, and re-layouts, windows_with(): return jnp.stack(windows, axis=2).reshape(pixels, amount * 9)  101 us
    dot_general x1, local copies, waits for them, and re-layouts, on_device(): lax.dot_general(columns, grad_hidden, contract_first, preferred_element_t...  97.8 us
    psum x1, waiting for transfers between devices, on_device(): bin_sum = lax.psum(local_sums, ('row', 'col'))  69.4 us
  transfers between devices with their start and end apart: 14, of which 7 were waited for; matrix products, arithmetic and copies ran while one was open for 27% of the time, Pallas kernels for 0%

commit v1 on v0

v1 whole, which is shorter than its diff:
```python
import jax
import jax.numpy as jnp
import numpy as np
from jax import lax
from jax.experimental import pallas as pl
from jax.experimental.pallas import tpu as pltpu
from jax.sharding import PartitionSpec as P

bin_scales = (1, 2, 3, 6)
norm_eps = 1e-05
tap_offsets = ((-1, -1), (-1, 0), (-1, 1), (0, -1), (0, 0), (0, 1), (1, -1), (1, 0), (1, 1))
contract_first = (((0,), (0,)), ((), ()))
contract_last = (((1,), (1,)), ((), ()))
bf16 = jnp.bfloat16
f32 = jnp.float32


def dot(a, b, dims=(((1,), (0,)), ((), ()))):
    return lax.dot_general(a, b, dims, preferred_element_type=f32)


def swap(value, axis, step):
    count = lax.axis_size(axis)
    return lax.ppermute(value, axis, [(i, i ^ step) for i in range(count)])


def butterfly(value, axes):
    for axis in axes:
        step = 1
        while step < lax.axis_size(axis):
            value = value + swap(value, axis, step)
            step *= 2
    return value


def bin_constants(regions):
    rows = []
    for position, scale in enumerate(bin_scales):
        for r in range(regions):
            for i in range(scale):
                for j in range(scale):
                    rows.append((position, scale, r, i, j))
    return np.asarray(rows, np.int32)


def of_bin_boxes(canvas_box, table):
    pick = jnp.asarray(table[:, 2:3] == np.arange(canvas_box.shape[0])[None, :], jnp.int32)
    return jnp.sum(pick[:, :, None] * canvas_box[None], axis=1)


def members(edges, cells_y, cells_x):
    lo_y, hi_y, lo_x, hi_x = (edge[:, None] for edge in edges)
    y, x = cells_y[None, :], cells_x[None, :]
    return ((y >= lo_y) & (y < hi_y) & (x >= lo_x) & (x < hi_x)).astype(bf16)


def axis_weight(cells, first, last, scale, index):
    extent = (last - first - 1).astype(f32)[:, None]
    place = ((cells[None, :] - first[:, None]) * (scale - 1)[:, None]).astype(f32)
    away = jnp.abs(place - index.astype(f32)[:, None] * extent) / extent
    inside = (cells[None, :] >= first[:, None]) & (cells[None, :] < last[:, None])
    return jnp.where(inside, jnp.maximum(1.0 - away, 0.0), 0.0)


def spreads(boxes, table, cells_y, cells_x):
    scale, i, j = (jnp.asarray(table[:, k]) for k in (1, 3, 4))
    weight_y = axis_weight(cells_y, boxes[:, 0], boxes[:, 2], scale, i)
    weight_x = axis_weight(cells_x, boxes[:, 1], boxes[:, 3], scale, j)
    return (weight_y * weight_x).astype(bf16)


def grid_cells(rows, cols):
    y = jnp.broadcast_to(rows[:, None], (rows.shape[0], cols.shape[0])).reshape(-1)
    x = jnp.broadcast_to(cols[None, :], (rows.shape[0], cols.shape[0])).reshape(-1)
    return y, x


def row_masks(canvas_box, rows, cols):
    y, x = rows[:, None], cols[None, :]
    up, left, down, right = (canvas_box[:, k][:, None, None] for k in range(4))
    inside = (y >= up) & (y < down) & (x >= left) & (x < right)
    upper = jnp.any(inside & (y > up), axis=0)
    lower = jnp.any(inside & (y + 1 < down), axis=0)
    return upper.reshape(-1), lower.reshape(-1)


def shift_lines(box_ref, first, x_ref, o_ref, width, reverse):
    cells, block = x_ref.shape
    order = (2, 1, 0) if reverse else (0, 1, 2)
    left_at, mid_at, right_at = (place * block for place in order)

    def line(at, carry):
        y = first + at
        here = pl.ds(pl.multiple_of(at * width, width), width)
        x = lax.broadcasted_iota(jnp.int32, (width, block), 0)
        no_left = x == 0
        no_right = x == width - 1
        for r in range(box_ref.shape[0]):
            inside = (y >= box_ref[r, 0]) & (y < box_ref[r, 2])
            no_left = no_left | (x == jnp.where(inside, box_ref[r, 1], -1))
            no_right = no_right | (x == jnp.where(inside, box_ref[r, 3] - 1, -1))
        own = x_ref[here, :]
        wide = own.astype(f32)
        left = jnp.where(no_left, 0.0, pltpu.roll(wide, 1, 0))
        right = jnp.where(no_right, 0.0, pltpu.roll(wide, width - 1, 0))
        o_ref[here, left_at : left_at + block] = left.astype(bf16)
        o_ref[here, mid_at : mid_at + block] = own
        o_ref[here, right_at : right_at + block] = right.astype(bf16)
        return carry

    lax.fori_loop(0, cells // width, line, 0)


def shifted(x, canvas_box, first_line, width, reverse=False, places=None, out_blocks=1, into=None):
    blocks, cells, block = x.shape
    total = cells // width
    lines = max(k for k in range(1, total + 1) if total % k == 0 and k * width <= 2048)
    if places is None:
        places, out_blocks = jnp.arange(blocks, dtype=jnp.int32), blocks

    def body(place_ref, first_ref, box_ref, x_ref, *rest):
        first = first_ref[0] + pl.program_id(1) * lines
        shift_lines(box_ref, first, x_ref.at[0], rest[-1].at[0], width, reverse)

    extra = [] if into is None else [into]
    return pl.pallas_call(
        body,
        grid_spec=pltpu.PrefetchScalarGridSpec(
            num_scalar_prefetch=2,
            grid=(blocks, total // lines),
            in_specs=[
                pl.BlockSpec(memory_space=pltpu.SMEM),
                pl.BlockSpec((1, width * lines, block), lambda b, i, at, first: (b, i, 0)),
            ]
            + [pl.BlockSpec(memory_space=pl.ANY)] * len(extra),
            out_specs=pl.BlockSpec(
                (1, width * lines, 3 * block), lambda b, i, at, first: (at[b], i, 0)
            ),
        ),
        out_shape=jax.ShapeDtypeStruct((out_blocks, cells, 3 * block), bf16),
        input_output_aliases={4: 0} if extra else {},
        compiler_params=pltpu.CompilerParams(vmem_limit_bytes=40 << 20),
        cost_estimate=pl.CostEstimate(
            flops=0, bytes_accessed=8 * blocks * cells * block, transcendentals=0
        ),
    )(places, jnp.reshape(first_line, (1,)).astype(jnp.int32), canvas_box, x, *extra)


def silu_slope(value):
    sigmoid_value = jax.nn.sigmoid(value)
    return sigmoid_value * (1.0 + value * (1.0 - sigmoid_value))


def choose(options, index):
    value = options[0]
    for k in range(1, len(options)):
        value = jnp.where(index == k, options[k], value)
    return value


def table_at(values, index):
    return choose([jnp.int32(value) for value in values], index)


def tie(*arrays):
    return list(lax.optimization_barrier(tuple(arrays)))


class Rows:
    def __init__(self, own):
        self.count = lax.axis_size("row")
        self.row = lax.axis_index("row")
        self.right = self.left = own
        self.arrived = {}
        self.step = 0

    def kinds(self, k):
        return [(abs(z - (z ^ k)), int((z ^ k) > z)) for z in range(self.count)]

    def more(self):
        return self.step < self.count - 1

    def send(self):
        self.step += 1
        step, count = self.step, self.count
        to_right = [(z, z + 1) for z in range(step - 1, count - 1)]
        to_left = [(z, z - 1) for z in range(1, count - step + 1)]
        if len(dict(to_right + to_left)) == len(to_right + to_left):
            senders = [z for z, _ in to_right]
            chosen = choose([self.left, self.right], sum(self.row == z for z in senders))
            both = lax.ppermute(chosen, "row", to_right + to_left)
            return [both]
        return [
            lax.ppermute(self.right, "row", to_right),
            lax.ppermute(self.left, "row", to_left),
        ]

    def receive(self, results):
        self.right, self.left = results[0], results[-1]
        self.arrived[self.step] = (self.right, self.left)

    def ready(self, k):
        return max(step for step, _ in self.kinds(k)) <= self.step

    def slot(self, k):
        each = self.kinds(k)
        options = sorted(set(each))
        which = table_at([options.index(kind) for kind in each], self.row)
        return choose([self.arrived[step][side] for step, side in options], which)


def place_images(pieces, kind=bf16):
    me = lax.axis_index("img")
    first = pieces[0]
    width = first.shape[1]
    shape = (first.shape[0], len(pieces) * width) + first.shape[2:]
    joined = jnp.zeros(shape, kind)
    for step, piece in enumerate(pieces):
        joined = lax.dynamic_update_slice_in_dim(
            joined, piece.astype(kind), (me ^ step) * width, 1
        )
    return joined


class Chain:
    def __init__(self, value, axes):
        self.value = value
        self.todo = []
        for axis in axes:
            step = 1
            while step < lax.axis_size(axis):
                self.todo.append((axis, step))
                step *= 2

    def send(self):
        return [swap(self.value, *self.todo[0])] if self.todo else []

    def receive(self, got):
        if got:
            self.value = self.value + got[0]
            self.todo = self.todo[1:]


def sum_images(x, chain, hooks):
    count = lax.axis_size("img")
    me = lax.axis_index("img")

    def fly(index, *flights):
        sent = chain.send()
        more = hooks.get(index, lambda: [])()
        got = tie(*flights, *sent, *more)
        chain.receive(got[len(flights) : len(flights) + len(sent)])
        return got[: len(flights)], got[len(flights) + len(sent) :]

    if count != 4:
        total, kept = fly(0, lax.psum(x, "img"))
        while chain.todo:
            fly(9)
        return total[0].astype(f32), kept
    quarter = x.shape[1] // 4
    half = quarter // 2

    def piece(j, side):
        at = (me ^ j) * quarter + side * half
        return lax.dynamic_slice_in_dim(x, at, half, 1)

    def add(a, b):
        return (a.astype(f32) + b.astype(f32)).astype(bf16)

    (a_in, b_in), kept = fly(
        0,
        swap(jnp.concatenate([piece(1, 0), piece(3, 0)], axis=1), "img", 1),
        swap(jnp.concatenate([piece(2, 1), piece(3, 1)], axis=1), "img", 2),
    )
    a_own, a_far = add(piece(0, 0), a_in[:, :half]), add(piece(2, 0), a_in[:, half:])
    b_own, b_far = add(piece(0, 1), b_in[:, :half]), add(piece(1, 1), b_in[:, half:])
    (a_two, b_one), _ = fly(1, swap(a_far, "img", 2), swap(b_far, "img", 1))
    a_own, b_own = add(a_own, a_two), add(b_own, b_one)
    (a_next, b_next), _ = fly(2, swap(a_own, "img", 1), swap(b_own, "img", 2))
    (a_rest, b_rest), _ = fly(
        3,
        swap(jnp.concatenate([a_own, a_next], axis=1), "img", 2),
        swap(jnp.concatenate([b_own, b_next], axis=1), "img", 1),
    )
    while chain.todo:
        fly(9)
    parts = [
        (a_own, b_own),
        (a_next, b_rest[:, :half]),
        (a_rest[:, :half], b_next),
        (a_rest[:, half:], b_rest[:, half:]),
    ]
    return place_images([jnp.concatenate(part, axis=1) for part in parts], f32), kept


def join_cols(mine, others, axis):
    col = lax.axis_index("col")
    pieces = [mine] + list(others)
    return jnp.concatenate([choose(pieces, col ^ c) for c in range(len(pieces))], axis=axis)


def row_halo(strip):
    count = lax.axis_size("row")
    above = lax.ppermute(strip[:, -1:], "row", [(i, i + 1) for i in range(count - 1)])
    below = lax.ppermute(strip[:, :1], "row", [(i + 1, i) for i in range(count - 1)])
    return jnp.concatenate([above, strip, below], axis=1)


def on_device(
    features,
    region_boxes,
    labels,
    branch_projection_weight,
    branch_gain,
    branch_bias,
    conv_w,
    conv_gain,
    conv_bias,
    class_w,
    class_bias,
):
    _, tile_h, tile_w, channels_in = features.shape
    pixels = tile_h * tile_w
    images, row_count, col_count = (lax.axis_size(axis) for axis in ("img", "row", "col"))
    img, row, col = (lax.axis_index(axis) for axis in ("img", "row", "col"))
    groups = row_count * col_count
    block, taps, mid = conv_w.shape
    branch_width = branch_projection_weight.shape[2]
    feature_rows = channels_in // (block * col_count)
    regions = region_boxes.shape[1]
    height, width = row_count * tile_h, col_count * tile_w
    all_cells = images * height * width
    canvas_box = region_boxes[0]
    table = bin_constants(regions)
    bins = table.shape[0]
    limits = [0]
    for scale in bin_scales:
        limits.append(limits[-1] + regions * scale * scale)
    scale_rows = [
        jnp.asarray((table[:, 0] == position).astype(np.float32)) for position in range(4)
    ]

    weight = jnp.transpose(conv_w, (1, 0, 2))
    share = block // images
    rows = Rows(lax.dynamic_slice_in_dim(weight, img * share, share, 1))

    def by_line(nine):
        return [nine[3 * a : 3 * a + 3] for a in range(3)]

    weights = [by_line(weight)]
    waiting = {"cross": None, "close": None, "next": 1}

    def weight_phase(more=(), hold=()):
        flights, plan = [], []
        if rows.more():
            sent = rows.send()
            plan.append(("rows", len(sent)))
            flights += sent
        if waiting["close"] is not None:
            _, one, two = waiting["close"]
            half = share // 2
            plan.append(("close", 2))
            flights += [swap(one[:, :half], "img", 2), swap(two[:, half:], "img", 1)]
        if waiting["cross"] is not None:
            part = waiting["cross"]
            if images == 4:
                plan.append(("cross", 2))
                flights += [swap(part, "img", 1), swap(part, "img", 2)]
            else:
                plan.append(("all", images - 1))
                flights += [swap(part, "img", step) for step in range(1, images)]
        got = tie(*flights, *more, *hold)
        at = 0
        closed, crossed = waiting["close"], waiting["cross"]
        waiting["close"] = waiting["cross"] = None
        for what, count in plan:
            part = got[at : at + count]
            at += count
            if what == "rows":
                rows.receive(part)
            elif what == "close":
                pieces = closed + [jnp.concatenate(part, axis=1)]
                weights.append(
                    [place_images([piece[3 * a : 3 * a + 3] for piece in pieces]) for a in range(3)]
                )
            elif what == "cross":
                waiting["close"] = [crossed] + list(part)
            else:
                pieces = [crossed] + list(part)
                weights.append(
                    [place_images([piece[3 * a : 3 * a + 3] for piece in pieces]) for a in range(3)]
                )
        if waiting["next"] < row_count and rows.ready(waiting["next"]):
            waiting["cross"] = rows.slot(waiting["next"])
            waiting["next"] += 1
        return got[at : at + len(more)], got[at + len(more) :]

    weight_phase()

    tile = features[0].reshape(pixels, channels_in)

    def channels_of(c):
        at = [(r * col_count + c) * block for r in range(feature_rows)]
        return jnp.stack([tile[:, k : k + block] for k in at])

    by_col = [channels_of(c) for c in range(col_count)]
    sent = [
        choose(by_col, col ^ step).reshape(feature_rows, tile_h, tile_w, block)
        for step in range(col_count)
    ]
    strip = join_cols(
        sent[0], [swap(sent[step], "col", step) for step in range(1, col_count)], 2
    )
    strip_ext = row_halo(strip)

    boxes = of_bin_boxes(canvas_box, table)
    scale, bin_i, bin_j = (jnp.asarray(table[:, k]) for k in (1, 3, 4))
    extent_y, extent_x = boxes[:, 2] - boxes[:, 0], boxes[:, 3] - boxes[:, 1]
    edges = (
        boxes[:, 0] + lax.div(bin_i * extent_y, scale),
        boxes[:, 0] + lax.div((bin_i + 1) * extent_y + scale - 1, scale),
        boxes[:, 1] + lax.div(bin_j * extent_x, scale),
        boxes[:, 1] + lax.div((bin_j + 1) * extent_x + scale - 1, scale),
    )
    sizes = ((edges[1] - edges[0]) * (edges[3] - edges[2])).astype(f32)
    top, left = row * tile_h, col * tile_w
    tile_y, tile_x = grid_cells(
        top + jnp.arange(tile_h, dtype=jnp.int32), left + jnp.arange(tile_w, dtype=jnp.int32)
    )
    pooling = members(edges, tile_y, tile_x)
    local_means = dot(pooling, tile) / sizes[:, None]
    local_low = local_means.astype(bf16)
    pre_local = jnp.concatenate(
        [
            dot(
                branch_projection_weight[position],
                local_low[limits[position] : limits[position + 1]],
                (((0,), (1,)), ((), ())),
            )
            for position in range(4)
        ],
        axis=1,
    )
    pre = lax.psum_scatter(pre_local, ("row", "col"), scatter_dimension=0, tiled=True)
    part = branch_width // groups
    group = row * col_count + col

    def by_scale(value):
        return jnp.stack([jnp.sum(value * line[None], axis=1) for line in scale_rows])

    def to_bins(value):
        return sum(value[k][:, None] * scale_rows[k][None] for k in range(4))

    def branch_part(value):
        return to_bins(lax.dynamic_slice_in_dim(value, group * part, part, 1))

    counts = np.asarray([images * regions * s * s for s in bin_scales], np.float32)[:, None]
    moments = butterfly(jnp.concatenate([by_scale(pre), by_scale(pre * pre)], axis=0), ("img",))
    center = moments[:4] / counts
    inverse = lax.rsqrt(moments[4:] / counts - center * center + norm_eps)
    gain_part = branch_part(branch_gain)
    inverse_bins = to_bins(inverse)
    normed = (pre - to_bins(center)) * inverse_bins
    before = gain_part * normed + branch_part(branch_bias)
    _, (act_part,) = weight_phase(hold=[jax.nn.silu(before).astype(bf16)])
    act_branch = lax.all_gather(
        act_part, ("row", "col"), axis=0, tiled=True
    )

    def block_rows_of(r):
        first = (r * col_count + col) * block - channels_in
        position = lax.div(first, branch_width)
        taken = lax.dynamic_slice_in_dim(
            act_branch, jnp.maximum(lax.rem(first, branch_width), 0), block, 0
        )
        keep = jnp.asarray(table[:, 0]) == position
        return jnp.where(keep[None], taken, jnp.zeros((), bf16)), keep

    strip_cols = jnp.arange(width, dtype=jnp.int32)
    strip_cells = tile_h * width
    ext_cells = strip_cells + 2 * width

    def ext_spread(source):
        lines = source * tile_h - 1 + jnp.arange(tile_h + 2, dtype=jnp.int32)
        return spreads(boxes, table, *grid_cells(lines, strip_cols))

    def up_blocks(spread, r):
        return dot(spread, block_rows_of(r)[0], (((0,), (1,)), ((), ()))).astype(bf16)

    spread_ext = ext_spread(row)
    ups = jnp.stack([up_blocks(spread_ext, r) for r in range(feature_rows, row_count)])
    cat_blocks = strip_ext.reshape(feature_rows, ext_cells, block)
    slots_of = row ^ jnp.arange(row_count, dtype=jnp.int32)
    cat_wide = shifted(
        cat_blocks, canvas_box, top - 1, width, places=slots_of[:feature_rows],
        out_blocks=row_count,
    )
    cat_wide = shifted(
        ups, canvas_box, top - 1, width, places=slots_of[feature_rows:],
        out_blocks=row_count, into=cat_wide,
    )
    upper, lower = row_masks(canvas_box, jnp.arange(height, dtype=jnp.int32), strip_cols)

    def strip_of(cells, source):
        return lax.dynamic_slice_in_dim(cells, source * strip_cells, strip_cells, 0)

    keeps = [strip_of(upper, row)[:, None], None, strip_of(lower, row)[:, None]]

    (cat_moves,) = weight_phase(hold=[cat_blocks])[1]

    def moved(step, begin, end):
        to = jnp.minimum(row ^ step, feature_rows - 1)
        taken = lax.dynamic_index_in_dim(cat_moves, to, 0, keepdims=False)[begin:end]
        pairs = [(i, i ^ step) for i in range(row_count) if (i ^ step) < feature_rows]
        return lax.ppermute(taken, "row", pairs) if step else taken

    half = ext_cells // 2
    moves = []
    for step in [2, 1] + list(range(3, row_count)):
        moves += [(step, 0, half), (step, half, ext_cells)]
    landed = {(0, 0): moved(0, 0, half), (0, half): moved(0, half, ext_cells)}

    def take_moves(count):
        taken = moves[:count]
        del moves[:count]
        return taken

    def land(taken, got):
        for (step, begin, _), array in zip(taken, got):
            landed[(step, begin)] = array

    hidden_strip = 0.0
    for slot in range(row_count):
        while len(weights) <= slot:
            taken = take_moves(1 if len(moves) == 2 * (row_count - 1) else 2)
            got, hold = weight_phase(
                more=[moved(*move) for move in taken], hold=[hidden_strip] if slot else []
            )
            land(taken, got)
            if hold:
                hidden_strip = hold[0]
        for a in (1, 0, 2):
            term = dot(
                cat_wide[slot, a * width : a * width + strip_cells],
                weights[slot][a].reshape(3 * block, mid),
            )
            hidden_strip = hidden_strip + (
                term if a == 1 else jnp.where(keeps[a], term, 0.0)
            )
    own_means = lax.psum_scatter(
        local_means.astype(bf16), ("row", "col"), scatter_dimension=1, tiled=True
    )
    hidden_strip, own_means = tie(hidden_strip, own_means)
    hidden_strip = hidden_strip.reshape(tile_h, width, mid)

    def cells_of(step):
        return lax.dynamic_slice_in_dim(hidden_strip, (col ^ step) * tile_w, tile_w, 1)

    hidden = cells_of(0)
    for step in range(1, col_count):
        hidden = hidden + swap(cells_of(step), "col", step)
    hidden = hidden.reshape(pixels, mid)

    everywhere = ("col", "img", "row")
    mid_moments = butterfly(
        jnp.stack([jnp.sum(hidden, axis=0), jnp.sum(hidden * hidden, axis=0)]), everywhere
    )
    center_mid = mid_moments[0] / all_cells
    inverse_mid = lax.rsqrt(mid_moments[1] / all_cells - center_mid * center_mid + norm_eps)
    normed_mid = (hidden - center_mid) * inverse_mid
    before_mid = conv_gain * normed_mid + conv_bias
    act_mid = jax.nn.silu(before_mid).astype(bf16)
    logits = dot(act_mid, class_w) + class_bias
    classes = class_w.shape[1]
    onehot = (
        labels[0].reshape(pixels)[:, None] == jnp.arange(classes, dtype=jnp.int32)[None, :]
    ).astype(f32)
    grad_logits = (jax.nn.softmax(logits, axis=-1) - onehot).astype(bf16)
    grad_before = dot(grad_logits, class_w, contract_last) * silu_slope(before_mid)
    mid_grads = butterfly(
        jnp.stack([jnp.sum(grad_before * normed_mid, axis=0), jnp.sum(grad_before, axis=0)]),
        everywhere,
    )
    conv_gain_grad, conv_bias_grad = mid_grads[0], mid_grads[1]
    class_chain = Chain(
        jnp.concatenate(
            [
                dot(act_mid, grad_logits, contract_first),
                jnp.sum(grad_logits.astype(f32), axis=0, keepdims=True),
            ],
            axis=0,
        ),
        everywhere,
    )
    grad_hidden = (
        conv_gain
        * inverse_mid
        * (grad_before - conv_bias_grad / all_cells - normed_mid * conv_gain_grad / all_cells)
    ).astype(bf16)

    grad_tile = grad_hidden.reshape(tile_h, tile_w, mid)
    grad_strip = join_cols(
        grad_tile, [swap(grad_tile, "col", step) for step in range(1, col_count)], 1
    )
    hops = Rows(grad_tile)
    grad_ext = row_halo(grad_strip[None]).reshape(1, ext_cells, mid)
    own_wide = shifted(grad_ext, canvas_box, top - 1, width, reverse=True)[0]

    def input_grads(slot):
        sums = []
        for a in range(3):
            sums.append(
                sum(
                    dot(
                        own_wide[a * width : a * width + strip_cells, j * mid : (j + 1) * mid],
                        weights[slot][2 - a][j],
                        contract_last,
                    )
                    for j in range(3)
                )
            )
        total = sums[1] + jnp.where(keeps[0], sums[0], 0.0) + jnp.where(keeps[2], sums[2], 0.0)
        return total.astype(bf16)

    conv_sums = [0.0] * taps

    def weight_grads(slot, strip):
        source = row ^ slot
        ext = jnp.where(
            row < feature_rows,
            jnp.concatenate([landed[(slot, 0)], landed[(slot, half)]], axis=0),
            up_blocks(ext_spread(source), row),
        )
        if slot == 0:
            wide = own_wide[width : width + strip_cells]
        else:
            wide = shifted(
                strip.reshape(1, strip_cells, mid), canvas_box, source * tile_h, width,
                reverse=True,
            )[0]
        masks = [strip_of(upper, source), None, strip_of(lower, source)]
        for a in range(3):
            side = ext[a * width : a * width + strip_cells]
            if a != 1:
                side = jnp.where(masks[a][:, None], side, jnp.zeros((), bf16))
            for j in range(3):
                conv_sums[3 * a + j] = conv_sums[3 * a + j] + dot(
                    side, wide[:, j * mid : (j + 1) * mid], contract_first
                )

    cat_grads, strips, swapping, asked = [], {0: grad_strip}, None, 1
    while len(strips) < row_count:
        flights, plan = [], []
        if hops.more():
            sent = hops.send()
            plan.append(("hops", len(sent)))
            flights += sent
        if swapping is not None:
            plan.append(("swap", col_count - 1))
            flights += [swap(swapping[1], "col", step) for step in range(1, col_count)]
        taken = take_moves(1)
        plan.append(("moves", len(taken)))
        flights += [moved(*move) for move in taken]
        sent = class_chain.send()
        plan.append(("class", len(sent)))
        flights += sent
        held = [input_grads(len(cat_grads))] if len(cat_grads) < row_count else []
        if len(cat_grads) + 1 < row_count and len(cat_grads) > 0:
            held.append(input_grads(len(cat_grads) + 1))
        got = tie(*flights, *held)
        cat_grads += got[len(flights) :]
        at = 0
        swapped, swapping = swapping, None
        for what, count in plan:
            part = got[at : at + count]
            at += count
            if what == "hops":
                hops.receive(part)
            elif what == "swap":
                strips[swapped[0]] = join_cols(swapped[1], part, 1)
            elif what == "moves":
                land(taken, part)
            else:
                class_chain.receive(part)
        if asked < row_count and hops.ready(asked):
            swapping = (asked, hops.slot(asked))
            asked += 1
    while moves:
        taken = take_moves(2)
        land(taken, [moved(*move) for move in taken])
    while len(cat_grads) < row_count:
        cat_grads.append(input_grads(len(cat_grads)))
    by_row = [choose(cat_grads, row ^ r) for r in range(row_count)]
    for slot in range(row_count):
        weight_grads(slot, strips[slot])
    conv_term = jnp.stack(conv_sums).astype(bf16)
    spread_strip = lax.slice_in_dim(spread_ext, width, width + strip_cells, axis=1)
    grad_bins_local = jnp.zeros((branch_width, bins), f32)
    for r in range(feature_rows, row_count):
        first = (r * col_count + col) * block - channels_in
        keep = jnp.asarray(table[:, 0]) == lax.div(first, branch_width)
        terms = dot(by_row[r], spread_strip, (((0,), (1,)), ((), ())))
        terms = jnp.where(keep[None], terms, 0.0)
        at = lax.rem(first, branch_width)
        old = lax.dynamic_slice_in_dim(grad_bins_local, at, block, 0)
        grad_bins_local = lax.dynamic_update_slice_in_dim(grad_bins_local, old + terms, at, 0)
    grad_bins = lax.psum_scatter(
        grad_bins_local, ("row", "col"), scatter_dimension=0, tiled=True
    )
    grad_act = grad_bins * silu_slope(before)
    branch_sums = butterfly(
        jnp.concatenate([by_scale(grad_act * normed), by_scale(grad_act)], axis=0), ("img",)
    )
    grad_pre = (
        gain_part
        * inverse_bins
        * (
            grad_act
            - to_bins(branch_sums[4:] / counts)
            - normed * to_bins(branch_sums[:4] / counts)
        )
    ).astype(bf16)
    conv_w_grad, (grad_pre, branch_sums) = sum_images(
        conv_term, class_chain, {0: lambda: [grad_pre, branch_sums]}
    )
    class_w_grad, class_bias_grad = class_chain.value[:mid], class_chain.value[mid]
    gathered = lax.all_gather(
        jnp.concatenate([grad_pre.astype(f32), branch_sums.T], axis=1),
        ("row", "col"), axis=0, tiled=True,
    )
    grad_pre = gathered[:, :bins].astype(bf16)
    branch_all = gathered[:, bins:].T
    branch_gain_grad, branch_bias_grad = branch_all[:4], branch_all[4:]

    weight_terms, bin_grads = [], []
    for position in range(4):
        span = slice(limits[position], limits[position + 1])
        weight_terms.append(
            dot(own_means[span], grad_pre[:, span], (((0,), (1,)), ((), ())))
        )
        bin_grads.append(
            dot(grad_pre[:, span], branch_projection_weight[position], (((0,), (1,)), ((), ())))
        )
    bin_grads = (jnp.concatenate(bin_grads, axis=0) / sizes[:, None]).astype(bf16)
    grad_pool = dot(pooling, bin_grads, contract_first)

    own_features = [
        by_row[r].reshape(tile_h, width, block) for r in range(feature_rows)
    ]

    def feature_grads_of(step):
        return jnp.stack(
            [
                choose(
                    [one[:, c * tile_w : (c + 1) * tile_w] for c in range(col_count)], col ^ step
                ).reshape(pixels, block)
                for one in own_features
            ]
        )

    by_step = [feature_grads_of(0)] + [
        swap(feature_grads_of(step), "col", step) for step in range(1, col_count)
    ]
    by_block = [choose(by_step, col ^ c) for c in range(col_count)]
    joined = jnp.concatenate(
        [by_block[c][r] for r in range(feature_rows) for c in range(col_count)], axis=1
    )
    feature_grad = (joined.astype(f32) + grad_pool).reshape(1, tile_h, tile_w, channels_in)

    branch_w_grad = lax.psum(jnp.stack(weight_terms).astype(bf16), "img").astype(f32)
    conv_w_grad = jnp.transpose(conv_w_grad, (1, 0, 2))
    return (
        logits.reshape(1, tile_h, tile_w, classes),
        feature_grad,
        branch_w_grad,
        branch_gain_grad,
        branch_bias_grad,
        conv_w_grad,
        conv_gain_grad,
        conv_bias_grad,
        class_w_grad,
        class_bias_grad,
    )


def solution(mesh):
    return jax.shard_map(
        on_device,
        mesh=mesh,
        in_specs=(
            P("img", "row", "col", None),
            P("img", None, None),
            P("img", "row", "col"),
            P(),
            P(),
            P(),
            P(("row", "col"), None, None),
            P(),
            P(),
            P(),
            P(),
        ),
        out_specs=(
            P("img", "row", "col", None),
            P("img", "row", "col", None),
            P(None, ("row", "col"), None),
            P(),
            P(),
            P(("row", "col"), None, None),
            P(),
            P(),
            P(),
            P(),
        ),
        check_vma=False,
    )
```

time: 2030 us -> 790 us (0.39)
  waiting for transfers between devices: 1180 us -> 197 us
  local copies, waits for them, and re-layouts: 356 us -> 92.5 us
  blocking collectives: 113 us -> 33.7 us
  starting transfers between devices: 20.9 us -> 83.8 us
  matrix products: 206 us -> 254 us
  other arithmetic: 114 us -> 73.9 us
  Pallas kernels: 0 us -> 28.5 us
    reduce_scatter x1, waiting for transfers between devices: 696 us -> 0.01 us  [on_device(): lax.psum_scatter(local_means.astype(bf16), ('row', 'col'), scatter_dimens...]
    psum x4 -> x1, waiting for transfers between devices: 294 us -> 19.7 us  [on_device(): lax.psum(jnp.stack(weight_terms).astype(bf16), 'img').astype(f32)]
    all_gather x1 -> x0, waiting for transfers between devices: 180 us -> none  [on_device(): shard_piece = lax.all_gather(conv_w, ('row', 'col'), axis=0, tiled=True)]
    ppermute x8 -> x66, waiting for transfers between devices: 14.3 us -> 177 us  [the longest x46 104 us: swap(): return lax.ppermute(value, axis, [(i, i ^ step) for i in range(count)])]
    psum x4 -> x0, blocking collectives: 113 us -> none  [the longest x1 40.2 us: on_device(): lax.psum((class_term, bias_term, gain_term, shift_term), ('img', 'row', '...]
    another operation x11 -> x9, local copies, waits for them, and re-layouts: 114 us -> 4.63 us  [the longest x1 113 us: windows_with(): return jnp.stack(windows, axis=2).reshape(pixels, amount * 9)]
    reshape x1 -> x2, local copies, waits for them, and re-layouts: 101 us -> 0.18 us  [row_masks(): return (upper.reshape(-1), lower.reshape(-1))]
    dot_general x1 -> x0, local copies, waits for them, and re-layouts: 97.8 us -> none  [on_device(): lax.dot_general(columns, grad_hidden, contract_first, preferred_element_t...]
  transfers between devices with their start and end apart: 14 -> 70, of which waited for: 7 -> 25; matrix products, arithmetic and copies ran while one was open for 27% -> 47% of each run, Pallas kernels for 0% -> 4%
where the time goes in v1:
time: 790 us; the launch traced here: 781 us
  matrix products  254 us (32%)
  waiting for transfers between devices  197 us (25%)
  local copies, waits for them, and re-layouts  92.5 us (12%)
  starting transfers between devices  83.8 us (11%)
  other arithmetic  73.9 us (9%)
  blocking collectives  33.7 us (4%)
  Pallas kernels  28.5 us (4%)
  between operations  17.5 us (2%)
    dot_general x109, matrix products, dot(): return lax.dot_general(a, b, dims, preferred_element_type=f32)  254 us
    ppermute x46, waiting for transfers between devices, swap(): return lax.ppermute(value, axis, [(i, i ^ step) for i in range(count)])  104 us
    ppermute x46, starting transfers between devices, swap(): return lax.ppermute(value, axis, [(i, i ^ step) for i in range(count)])  39.3 us
    pallas_call x6, Pallas kernels, shifted(): pl.pallas_call(body, grid_spec=pltpu.PrefetchScalarGridSpec(num_scalar_pr...  28.5 us
    dynamic_update_slice x18, local copies, waits for them, and re-layouts, place_images(): lax.dynamic_update_slice_in_dim(joined, piece.astype(kind), (me ^ step) *...  24.6 us
    ppermute x6, waiting for transfers between devices, moved(): return lax.ppermute(taken, 'row', pairs) if step else taken  24.3 us
    select_n x16, other arithmetic, choose(): value = jnp.where(index == k, options[k], value)  20.5 us
    psum x1, waiting for transfers between devices, on_device(): lax.psum(jnp.stack(weight_terms).astype(bf16), 'img').astype(f32)  19.7 us
  transfers between devices with their start and end apart: 70, of which 25 were waited for; matrix products, arithmetic and copies ran while one was open for 47% of the time, Pallas kernels for 4%

profile of v1, /device:TPU:0, one launch (start us, length us, event | category | flops | bytes accessed | tf_op | source)
XLA Modules:
  0.0 780.8 jit_solution(10141267698985037379)
XLA Ops:
  10.0 3.9 divide_convert_fusion
  14.0 3.0 fusion.108
  24.3 5.9 collective-permute-start
  41.6 4.6 fusion.310
  46.2 18.4 %collective-permute-done = bf16[9,128,512]{2,1,0:T(8,128)(2,1)} collective-permute-done((bf16[9,128,512]{2,1,0:T(8,128)(2,1)}, bf16[9,128,512]{2,1,0:T(8,128)(2,1)}, u32[]{:S(2)}, u32[]{:S(2)}) %collective-permute-start) | collective-permute-done | bytes 1179680 | tf_op jit(solution)/shard_map/ppermute | solution.py:194
  64.6 4.4 collective-permute-done.1
  92.4 6.8 collective-permute-done.6
  102.8 2.8 collective-permute-start.14
  110.6 10.2 %collective-permute-done.15 = bf16[2,1,64,512]{3,2,1,0:T(8,128)(2,1)S(1)} collective-permute-done((bf16[2,1,64,512]{3,2,1,0:T(8,128)(2,1)S(1)}, bf16[2,1,64,512]{3,2,1,0:T(8,128)(2,1)S(1)}, u32[]{:S(2)}, u32[]{:S(2)}) %collective-permute-start.15) | collective-permute-done | bytes 131104 | tf_op jit(solution)/shard_map/ppermute | solution.py:305
  121.2 8.3 %shard_map.474.rest_0_ = bf16[4,1664,1536]{2,1,0:T(8,128)(2,1)} custom-call(s32[2]{0:T(128)S(1)} %get-tuple-element.341.place_ref, s32[1]{0:T(128)} %bitcast.45.first_ref, s32[8,4]{1,0:T(8,128)S(1)} %copy.91.box_ref, bf16[2,1664,512]{2,1,0:T(8,128)(2,1)S(1)} %bitcast.484), custom_call_target="tpu_custom_call" | custom-call | bytes 13631488 | tf_op jit(solution)/shard_map/pallas_call | solution.py:126
  129.6 3.2 broadcast_select_fusion.6
  135.5 16.6 %all_gather.6 = bf16[512,400]{1,0:T(8,128)(2,1)S(1)} all-gather(bf16[64,400]{1,0:T(8,128)(2,1)S(1)} %copy.89), channel_id=1, replica_groups=mesh['img'=4,'row'=4,'col'=2] {'row','col'}, dimensions={0}, use_global_device_ids=true | all-gather | bytes 460800 | tf_op jit(solution)/shard_map/all_gather | solution.py:466
  167.6 8.2 %shard_map.475 = bf16[4,1664,1536]{2,1,0:T(8,128)(2,1)} custom-call(s32[2]{0:T(128)S(1)} %get-tuple-element.342.place_ref, s32[1]{0:T(128)} %bitcast.45.first_ref, s32[8,4]{1,0:T(8,128)S(1)} %copy.91.box_ref, bf16[2,1664,512]{2,1,0:T(8,128)(2,1)S(1)} %pad_maximum_fusion.1.x_ref, ...), custom_call_target="tpu_custom_call", output_to_operand_aliasing={{}: (4, {})} | custom-call | bytes 13631488 | tf_op jit(solution)/shard_map/pallas_call | solution.py:126
  175.8 4.9 fusion.25
  180.8 3.1 slice_dynamic-update-slice_fusion.31
  185.1 2.9 slice_dynamic-update-slice_fusion.30
  188.0 4.4 fusion.41
  201.3 5.9 fusion.8
  207.2 3.1 dynamic-slice_bitcast_fusion.2
  217.5 5.7 fusion.40
  223.1 5.0 fusion.38
  234.8 5.7 fusion.37
  242.0 5.7 collective-permute-start.24
  247.7 24.3 %collective-permute-done.20 = bf16[832,512]{1,0:T(8,128)(2,1)} collective-permute-done((bf16[832,512]{1,0:T(8,128)(2,1)}, bf16[832,512]{1,0:T(8,128)(2,1)}, u32[]{:S(2)}, u32[]{:S(2)}) %collective-permute-start.20) | collective-permute-done | bytes 852000 | tf_op jit(solution)/shard_map/ppermute | solution.py:515
  272.2 4.3 fusion.5
  276.6 4.3 fusion.29
  284.7 6.5 add_add_fusion.1
  298.3 4.3 fusion.31
  302.6 5.8 add_add_fusion
  311.1 3.7 collective-permute-done.25
  314.9 3.5 fusion.306
  327.0 3.6 collective-permute-done.29
  330.7 4.4 collective-permute-done.30
  340.2 3.4 multiply_convert_fusion.3
  352.7 3.9 collective-permute-start.38
  358.1 3.1 collective-permute-start.35
  361.2 5.8 fusion.48
  367.0 28.3 %collective-permute-done.35 = f32[2,512]{1,0:T(2,128)S(1)} collective-permute-done((f32[2,512]{1,0:T(2,128)S(1)}, f32[2,512]{1,0:T(2,128)S(1)}, u32[]{:S(2)}, u32[]{:S(2)}) %collective-permute-start.35) | collective-permute-done | bytes 4128 | tf_op jit(solution)/shard_map/ppermute | solution.py:24
  397.2 5.6 maximum_select_fusion.2
  410.0 5.2 collective-permute-start.36
  416.6 3.3 shard_map.476
  420.0 3.7 fusion.251
  443.9 3.9 fusion.255
  459.4 4.1 fusion.176
  480.7 3.9 convolution_add_fusion.11
  490.4 3.8 convolution_add_fusion.17
  509.4 2.9 fusion.44
  512.4 6.1 maximum_select_fusion.1
  552.6 13.3 %collective-permute-done.48 = bf16[24,32,512]{2,1,0:T(8,128)(2,1)S(1)} collective-permute-done((bf16[24,32,512]{2,1,0:T(8,128)(2,1)S(1)}, bf16[24,32,512]{2,1,0:T(8,128)(2,1)S(1)}, u32[]{:S(2)}, u32[]{:S(2)}) %collective-permute-start.48) | collective-permute-done | bytes 786464 | tf_op jit(solution)/shard_map/ppermute | solution.py:191
  575.4 2.9 shard_map.478
  594.5 4.1 maximum_select_fusion.3
  601.9 3.1 shard_map.479
  628.5 21.2 %collective-permute-done.58 = f32[8,64]{1,0:T(8,128)S(1)} collective-permute-done((f32[8,64]{1,0:T(8,128)S(1)}, f32[8,64]{1,0:T(8,128)S(1)}, u32[]{:S(2)}, u32[]{:S(2)}) %collective-permute-start.58) | collective-permute-done | bytes 2080 | tf_op jit(solution)/shard_map/ppermute | solution.py:24
  653.9 17.1 %all_gather.7 = f32[512,408]{1,0:T(8,128)S(1)} all-gather(f32[64,408]{1,0:T(8,128)S(1)} %copy.101), channel_id=1, replica_groups=mesh['img'=4,'row'=4,'col'=2] {'row','col'}, dimensions={0}, use_global_device_ids=true | all-gather | bytes 940032 | tf_op jit(solution)/shard_map/all_gather | solution.py:727
  674.7 2.9 add_convert_fusion.3
  681.8 3.1 fusion.57
  684.9 3.3 fusion.53
  688.2 5.1 collective-permute-done.60
  693.6 3.2 add_convert_fusion
  703.8 13.4 %collective-permute-done.62 = bf16[9,64,512]{2,1,0:T(8,128)(2,1)} collective-permute-done((bf16[9,64,512]{2,1,0:T(8,128)(2,1)}, bf16[9,64,512]{2,1,0:T(8,128)(2,1)}, u32[]{:S(2)}, u32[]{:S(2)}) %collective-permute-start.62) | collective-permute-done | bytes 589856 | tf_op jit(solution)/shard_map/ppermute | solution.py:24
  726.7 6.9 convert_add_fusion
  733.6 4.9 broadcast_in_dim.407
  738.6 3.0 convert_dynamic-update-slice_fusion.3
  741.5 19.7 %all-reduce.2.cloned.1.call-done = bf16[4,256,512]{2,1,0:T(8,128)(2,1)} async-done(((bf16[4,256,512]{2,1,0:T(8,128)(2,1)}), bf16[4,256,512]{2,1,0:T(8,128)(2,1)}) %all-reduce.2.cloned.1.call-update) | async-done | bytes 1048592 | tf_op jit(solution)/shard_map/psum | solution.py:770
  (777 shorter events, 341.4 us)
Async XLA Ops:
  7.2 79.6 %reduce-scatter.10.cloned.1.call-start = ((), (), s32[]{:S(2)}) async-start(), calls=%async_computation.5 | async-start | bytes 1179648
  21.9 286.5 %reduce-scatter.8.cloned.1.call-start = ((), (), s32[]{:S(2)}) async-start(), calls=%async_computation.3 | async-start | bytes 1843200 | tf_op jit(solution)/shard_map/reduce_scatter | solution.py:550
  24.3 40.3 %collective-permute-start = (bf16[9,128,512]{2,1,0:T(8,128)(2,1)}, bf16[9,128,512]{2,1,0:T(8,128)(2,1)}, u32[]{:S(2)}, u32[]{:S(2)}) collective-permute-start(bf16[9,128,512]{2,1,0:T(8,128)(2,1)} %dynamic-slice_bitcast_fusion), channel_id=1, source_target_pairs={{0,2},{2,4},{4,6},{1,3},{3,5},{5,7},{8,10},{10,12},{12,14},{9,11},... | collective-permute-start | bytes 3538952 | tf_op jit(solution)/shard_map/ppermute | solution.py:194
  30.3 38.8 %collective-permute-start.1 = (bf16[9,128,512]{2,1,0:T(8,128)(2,1)}, bf16[9,128,512]{2,1,0:T(8,128)(2,1)}, u32[]{:S(2)}, u32[]{:S(2)}) collective-permute-start(bf16[9,128,512]{2,1,0:T(8,128)(2,1)} %dynamic-slice_bitcast_fusion), channel_id=1, source_target_pairs={{2,0},{4,2},{6,4},{3,1},{5,3},{7,5},{10,8},{12,10},{14,12},{11,9},... | collective-permute-start | bytes 3538952 | tf_op jit(solution)/shard_map/ppermute | solution.py:195
  35.1 55.0 %collective-permute-start.13 = (bf16[2,24,32,512]{3,2,1,0:T(8,128)(2,1)}, bf16[2,24,32,512]{3,2,1,0:T(8,128)(2,1)}, u32[]{:S(2)}, u32[]{:S(2)}) collective-permute-start(bf16[2,24,32,512]{3,2,1,0:T(8,128)(2,1)} %broadcast_select_fusion.3), channel_id=1, source_target_pairs={{0,1},{1,0},{2,3},{3,2},{4,5},{5,4},{6,7},{7,6},{8,9},{9,8},{10,11... | collective-permute-start | bytes 4718600 | tf_op jit(solution)/shard_map/ppermute | solution.py:24
  35.1 587.8 %reduce-scatter.12.cloned.1.call-start = ((), (), s32[]{:S(2)}) async-start(), calls=%async_computation.6 | async-start | bytes 1179648
  71.5 58.0 %collective-permute-start.4 = (bf16[9,128,512]{2,1,0:T(8,128)(2,1)}, bf16[9,128,512]{2,1,0:T(8,128)(2,1)}, u32[]{:S(2)}, u32[]{:S(2)}) collective-permute-start(bf16[9,128,512]{2,1,0:T(8,128)(2,1)} %broadcast_select_fusion.7), channel_id=1, source_target_pairs={{0,8},{8,0},{16,24},{24,16},{1,9},{9,1},{17,25},{25,17},{2,10},{10... | collective-permute-start | bytes 3538952 | tf_op jit(solution)/shard_map/ppermute | solution.py:24
  73.0 56.5 %collective-permute-start.5 = (bf16[9,128,512]{2,1,0:T(8,128)(2,1)}, bf16[9,128,512]{2,1,0:T(8,128)(2,1)}, u32[]{:S(2)}, u32[]{:S(2)}) collective-permute-start(bf16[9,128,512]{2,1,0:T(8,128)(2,1)} %broadcast_select_fusion.7), channel_id=1, source_target_pairs={{0,16},{8,24},{16,0},{24,8},{1,17},{9,25},{17,1},{25,9},{2,18},{10... | collective-permute-start | bytes 3538952 | tf_op jit(solution)/shard_map/ppermute | solution.py:24
  74.5 55.0 %collective-permute-start.2 = (bf16[9,128,512]{2,1,0:T(8,128)(2,1)}, bf16[9,128,512]{2,1,0:T(8,128)(2,1)}, u32[]{:S(2)}, u32[]{:S(2)}) collective-permute-start(bf16[9,128,512]{2,1,0:T(8,128)(2,1)} %collective-permute-done), channel_id=1, source_target_pairs={{2,4},{4,6},{3,5},{5,7},{10,12},{12,14},{11,13},{13,15},{18,20},{2... | collective-permute-start | bytes 3538952 | tf_op jit(solution)/shard_map/ppermute | solution.py:194
  76.1 53.3 %collective-permute-start.3 = (bf16[9,128,512]{2,1,0:T(8,128)(2,1)}, bf16[9,128,512]{2,1,0:T(8,128)(2,1)}, u32[]{:S(2)}, u32[]{:S(2)}) collective-permute-start(bf16[9,128,512]{2,1,0:T(8,128)(2,1)} %collective-permute-done.1), channel_id=1, source_target_pairs={{2,0},{4,2},{3,1},{5,3},{10,8},{12,10},{11,9},{13,11},{18,16},{20,... | collective-permute-start | bytes 3538952 | tf_op jit(solution)/shard_map/ppermute | solution.py:195
  90.0 9.2 %collective-permute-start.6 = (f32[8,64]{1,0:T(8,128)}, f32[8,64]{1,0:T(8,128)S(1)}, u32[]{:S(2)}, u32[]{:S(2)}) collective-permute-start(f32[8,64]{1,0:T(8,128)} %concatenate.92), channel_id=1, source_target_pairs={{0,8},{8,0},{16,24},{24,16},{1,9},{9,1},{17,25},{25,17},{2,10},{10... | collective-permute-start | bytes 6152 | tf_op jit(solution)/shard_map/ppermute | solution.py:24
  102.8 5.4 collective-permute-start.14
  108.2 12.6 %collective-permute-start.15 = (bf16[2,1,64,512]{3,2,1,0:T(8,128)(2,1)S(1)}, bf16[2,1,64,512]{3,2,1,0:T(8,128)(2,1)S(1)}, u32[]{:S(2)}, u32[]{:S(2)}) collective-permute-start(bf16[2,1,64,512]{3,2,1,0:T(8,128)(2,1)S(1)} %get-tuple-element.224), channel_id=1, source_target_pairs={{2,0},{4,2},{6,4},{3,1},{5,3},{7,5},{10,8},{12,10},{14,12},{11,9},... | collective-permute-start | bytes 393224 | tf_op jit(solution)/shard_map/ppermute | solution.py:305
  132.8 59.7 %collective-permute-start.11 = (bf16[9,128,512]{2,1,0:T(8,128)(2,1)}, bf16[9,128,512]{2,1,0:T(8,128)(2,1)}, u32[]{:S(2)}, u32[]{:S(2)}) collective-permute-start(bf16[9,128,512]{2,1,0:T(8,128)(2,1)} %get-tuple-element.229), channel_id=1, source_target_pairs={{0,8},{8,0},{16,24},{24,16},{1,9},{9,1},{17,25},{25,17},{2,10},{10... | collective-permute-start | bytes 3538952 | tf_op jit(solution)/shard_map/ppermute | solution.py:24
  134.0 58.5 %collective-permute-start.12 = (bf16[9,128,512]{2,1,0:T(8,128)(2,1)}, bf16[9,128,512]{2,1,0:T(8,128)(2,1)}, u32[]{:S(2)}, u32[]{:S(2)}) collective-permute-start(bf16[9,128,512]{2,1,0:T(8,128)(2,1)} %get-tuple-element.229), channel_id=1, source_target_pairs={{0,16},{8,24},{16,0},{24,8},{1,17},{9,25},{17,1},{25,9},{2,18},{10... | collective-permute-start | bytes 3538952 | tf_op jit(solution)/shard_map/ppermute | solution.py:24
  157.9 34.6 %collective-permute-start.8 = (bf16[9,128,512]{2,1,0:T(8,128)(2,1)}, bf16[9,128,512]{2,1,0:T(8,128)(2,1)}, u32[]{:S(2)}, u32[]{:S(2)}) collective-permute-start(bf16[9,128,512]{2,1,0:T(8,128)(2,1)} %get-tuple-element.230), channel_id=1, source_target_pairs={{4,6},{2,0},{5,7},{3,1},{12,14},{10,8},{13,15},{11,9},{20,22},{18,... | collective-permute-start | bytes 3538952 | tf_op jit(solution)/shard_map/ppermute | solution.py:191
  161.6 30.8 %collective-permute-start.10 = (bf16[9,64,512]{2,1,0:T(8,128)(2,1)}, bf16[9,64,512]{2,1,0:T(8,128)(2,1)}, u32[]{:S(2)}, u32[]{:S(2)}) collective-permute-start(bf16[9,64,512]{2,1,0:T(8,128)(2,1)} %slice.833), channel_id=1, source_target_pairs={{0,8},{8,0},{16,24},{24,16},{1,9},{9,1},{17,25},{25,17},{2,10},{10... | collective-permute-start | bytes 1769480 | tf_op jit(solution)/shard_map/ppermute | solution.py:24
  164.3 28.2 %collective-permute-start.9 = (bf16[9,64,512]{2,1,0:T(8,128)(2,1)}, bf16[9,64,512]{2,1,0:T(8,128)(2,1)}, u32[]{:S(2)}, u32[]{:S(2)}) collective-permute-start(bf16[9,64,512]{2,1,0:T(8,128)(2,1)} %slice.832), channel_id=1, source_target_pairs={{0,16},{8,24},{16,0},{24,8},{1,17},{9,25},{17,1},{25,9},{2,18},{10... | collective-permute-start | bytes 1769480 | tf_op jit(solution)/shard_map/ppermute | solution.py:24
  195.3 76.6 %collective-permute-start.18 = (bf16[9,128,512]{2,1,0:T(8,128)(2,1)}, bf16[9,128,512]{2,1,0:T(8,128)(2,1)}, u32[]{:S(2)}, u32[]{:S(2)}) collective-permute-start(bf16[9,128,512]{2,1,0:T(8,128)(2,1)} %select_select_fusion), channel_id=1, source_target_pairs={{0,8},{8,0},{16,24},{24,16},{1,9},{9,1},{17,25},{25,17},{2,10},{10... | collective-permute-start | bytes 3538952 | tf_op jit(solution)/shard_map/ppermute | solution.py:24
  196.6 75.4 %collective-permute-start.19 = (bf16[9,128,512]{2,1,0:T(8,128)(2,1)}, bf16[9,128,512]{2,1,0:T(8,128)(2,1)}, u32[]{:S(2)}, u32[]{:S(2)}) collective-permute-start(bf16[9,128,512]{2,1,0:T(8,128)(2,1)} %select_select_fusion), channel_id=1, source_target_pairs={{0,16},{8,24},{16,0},{24,8},{1,17},{9,25},{17,1},{25,9},{2,18},{10... | collective-permute-start | bytes 3538952 | tf_op jit(solution)/shard_map/ppermute | solution.py:24
  210.3 61.6 %collective-permute-start.20 = (bf16[832,512]{1,0:T(8,128)(2,1)}, bf16[832,512]{1,0:T(8,128)(2,1)}, u32[]{:S(2)}, u32[]{:S(2)}) collective-permute-start(bf16[832,512]{1,0:T(8,128)(2,1)} %get-tuple-element.216), channel_id=1, source_target_pairs={{4,0},{6,2},{5,1},{7,3},{12,8},{14,10},{13,9},{15,11},{20,16},{22,... | collective-permute-start | bytes 2555912 | tf_op jit(solution)/shard_map/ppermute | solution.py:515
  213.7 26.9 %collective-permute-start.16 = (bf16[9,64,512]{2,1,0:T(8,128)(2,1)}, bf16[9,64,512]{2,1,0:T(8,128)(2,1)S(1)}, u32[]{:S(2)}, u32[]{:S(2)}) collective-permute-start(bf16[9,64,512]{2,1,0:T(8,128)(2,1)} %slice.840), channel_id=1, source_target_pairs={{0,16},{8,24},{16,0},{24,8},{1,17},{9,25},{17,1},{25,9},{2,18},{10... | collective-permute-start | bytes 1769480 | tf_op jit(solution)/shard_map/ppermute | solution.py:24
  215.3 26.6 %collective-permute-start.17 = (bf16[9,64,512]{2,1,0:T(8,128)(2,1)S(1)}, bf16[9,64,512]{2,1,0:T(8,128)(2,1)S(1)}, u32[]{:S(2)}, u32[]{:S(2)}) collective-permute-start(bf16[9,64,512]{2,1,0:T(8,128)(2,1)S(1)} %slice.841), channel_id=1, source_target_pairs={{0,8},{8,0},{16,24},{24,16},{1,9},{9,1},{17,25},{25,17},{2,10},{10... | collective-permute-start | bytes 1769480 | tf_op jit(solution)/shard_map/ppermute | solution.py:24
  240.5 53.4 %collective-permute-start.23 = (bf16[832,512]{1,0:T(8,128)(2,1)}, bf16[832,512]{1,0:T(8,128)(2,1)}, u32[]{:S(2)}, u32[]{:S(2)}) collective-permute-start(bf16[832,512]{1,0:T(8,128)(2,1)} %get-tuple-element.220), channel_id=1, source_target_pairs={{4,0},{6,2},{5,1},{7,3},{12,8},{14,10},{13,9},{15,11},{20,16},{22,... | collective-permute-start | bytes 2555912 | tf_op jit(solution)/shard_map/ppermute | solution.py:515
  242.0 52.0 %collective-permute-start.24 = (bf16[832,512]{1,0:T(8,128)(2,1)S(1)}, bf16[832,512]{1,0:T(8,128)(2,1)}, u32[]{:S(2)}, u32[]{:S(2)}) collective-permute-start(bf16[832,512]{1,0:T(8,128)(2,1)S(1)} %copy-done.46), channel_id=1, source_target_pairs={{0,2},{2,0},{1,3},{3,1},{8,10},{10,8},{9,11},{11,9},{16,18},{18,16... | collective-permute-start | bytes 2555912 | tf_op jit(solution)/shard_map/ppermute | solution.py:515
  282.0 12.0 %collective-permute-start.21 = (bf16[9,64,512]{2,1,0:T(8,128)(2,1)S(1)}, bf16[9,64,512]{2,1,0:T(8,128)(2,1)S(1)}, u32[]{:S(2)}, u32[]{:S(2)}) collective-permute-start(bf16[9,64,512]{2,1,0:T(8,128)(2,1)S(1)} %slice.873), channel_id=1, source_target_pairs={{0,16},{8,24},{16,0},{24,8},{1,17},{9,25},{17,1},{25,9},{2,18},{10... | collective-permute-start | bytes 1769480 | tf_op jit(solution)/shard_map/ppermute | solution.py:24
  283.8 11.5 %collective-permute-start.22 = (bf16[9,64,512]{2,1,0:T(8,128)(2,1)S(1)}, bf16[9,64,512]{2,1,0:T(8,128)(2,1)S(1)}, u32[]{:S(2)}, u32[]{:S(2)}) collective-permute-start(bf16[9,64,512]{2,1,0:T(8,128)(2,1)S(1)} %slice.874), channel_id=1, source_target_pairs={{0,8},{8,0},{16,24},{24,16},{1,9},{9,1},{17,25},{25,17},{2,10},{10... | collective-permute-start | bytes 1769480 | tf_op jit(solution)/shard_map/ppermute | solution.py:24
  311.1 3.8 collective-permute-start.25
  319.7 3.7 collective-permute-start.27
  323.3 3.7 collective-permute-start.28
  330.6 4.5 collective-permute-start.30
  343.6 3.7 collective-permute-start.32
  351.0 7.1 collective-permute-start.34
  352.7 99.3 %collective-permute-start.38 = (bf16[832,512]{1,0:T(8,128)(2,1)}, bf16[832,512]{1,0:T(8,128)(2,1)}, u32[]{:S(2)}, u32[]{:S(2)}) collective-permute-start(bf16[832,512]{1,0:T(8,128)(2,1)} %get-tuple-element.219), channel_id=1, source_target_pairs={{0,2},{2,0},{1,3},{3,1},{8,10},{10,8},{9,11},{11,9},{16,18},{18,16... | collective-permute-start | bytes 2555912 | tf_op jit(solution)/shard_map/ppermute | solution.py:515
  356.6 167.3 %collective-permute-start.46 = (bf16[832,512]{1,0:T(8,128)(2,1)}, bf16[832,512]{1,0:T(8,128)(2,1)}, u32[]{:S(2)}, u32[]{:S(2)}) collective-permute-start(bf16[832,512]{1,0:T(8,128)(2,1)} %get-tuple-element.214), channel_id=1, source_target_pairs={{4,2},{6,0},{5,3},{7,1},{12,10},{14,8},{13,11},{15,9},{20,18},{22,... | collective-permute-start | bytes 2555912 | tf_op jit(solution)/shard_map/ppermute | solution.py:515
  358.1 37.2 %collective-permute-start.35 = (f32[2,512]{1,0:T(2,128)S(1)}, f32[2,512]{1,0:T(2,128)S(1)}, u32[]{:S(2)}, u32[]{:S(2)}) collective-permute-start(f32[2,512]{1,0:T(2,128)S(1)} %add.753), channel_id=1, source_target_pairs={{0,4},{2,6},{4,0},{6,2},{1,5},{3,7},{5,1},{7,3},{8,12},{10,14},{12... | collective-permute-start | bytes 12296 | tf_op jit(solution)/shard_map/ppermute | solution.py:24
  397.2 7.2 collective-permute-start.40
  406.1 3.9 collective-permute-start.41
  407.4 7.7 collective-permute-start.42
  409.5 42.5 %collective-permute-start.39 = (f32[513,150]{0,1:T(8,128)}, f32[513,150]{0,1:T(8,128)}, u32[]{:S(2)}, u32[]{:S(2)}) collective-permute-start(f32[513,150]{0,1:T(8,128)} %pad_maximum_fusion.18), channel_id=1, source_target_pairs={{0,1},{1,0},{2,3},{3,2},{4,5},{5,4},{6,7},{7,6},{8,9},{9,8},{10,11... | collective-permute-start | bytes 923408 | tf_op jit(solution)/shard_map/ppermute | solution.py:24
  410.0 42.0 %collective-permute-start.36 = (bf16[24,32,512]{2,1,0:T(8,128)(2,1)}, bf16[24,32,512]{2,1,0:T(8,128)(2,1)}, u32[]{:S(2)}, u32[]{:S(2)}) collective-permute-start(bf16[24,32,512]{2,1,0:T(8,128)(2,1)} %bitcast.92), channel_id=1, source_target_pairs={{0,2},{2,4},{4,6},{1,3},{3,5},{5,7},{8,10},{10,12},{12,14},{9,11},... | collective-permute-start | bytes 2359304 | tf_op jit(solution)/shard_map/ppermute | solution.py:194
  415.1 36.8 %collective-permute-start.37 = (bf16[24,32,512]{2,1,0:T(8,128)(2,1)}, bf16[24,32,512]{2,1,0:T(8,128)(2,1)}, u32[]{:S(2)}, u32[]{:S(2)}) collective-permute-start(bf16[24,32,512]{2,1,0:T(8,128)(2,1)} %bitcast.92), channel_id=1, source_target_pairs={{2,0},{4,2},{6,4},{3,1},{5,3},{7,5},{10,8},{12,10},{14,12},{11,9},... | collective-permute-start | bytes 2359304 | tf_op jit(solution)/shard_map/ppermute | solution.py:195
  452.0 73.2 %collective-permute-start.43 = (bf16[24,32,512]{2,1,0:T(8,128)(2,1)}, bf16[24,32,512]{2,1,0:T(8,128)(2,1)}, u32[]{:S(2)}, u32[]{:S(2)}) collective-permute-start(bf16[24,32,512]{2,1,0:T(8,128)(2,1)} %collective-permute-done.36), channel_id=1, source_target_pairs={{2,4},{4,6},{3,5},{5,7},{10,12},{12,14},{11,13},{13,15},{18,20},{2... | collective-permute-start | bytes 2359304 | tf_op jit(solution)/shard_map/ppermute | solution.py:194
  455.6 69.6 %collective-permute-start.44 = (bf16[24,32,512]{2,1,0:T(8,128)(2,1)}, bf16[24,32,512]{2,1,0:T(8,128)(2,1)}, u32[]{:S(2)}, u32[]{:S(2)}) collective-permute-start(bf16[24,32,512]{2,1,0:T(8,128)(2,1)} %collective-permute-done.37), channel_id=1, source_target_pairs={{2,0},{4,2},{3,1},{5,3},{10,8},{12,10},{11,9},{13,11},{18,16},{20,... | collective-permute-start | bytes 2359304 | tf_op jit(solution)/shard_map/ppermute | solution.py:195
  503.6 21.6 %collective-permute-start.47 = (f32[513,150]{0,1:T(8,128)S(1)}, f32[513,150]{0,1:T(8,128)S(1)}, u32[]{:S(2)}, u32[]{:S(2)}) collective-permute-start(f32[513,150]{0,1:T(8,128)S(1)} %fusion.305), channel_id=1, source_target_pairs={{0,8},{8,0},{16,24},{24,16},{1,9},{9,1},{17,25},{25,17},{2,10},{10... | collective-permute-start | bytes 923408 | tf_op jit(solution)/shard_map/ppermute | solution.py:24
  504.5 20.7 %collective-permute-start.45 = (bf16[24,32,512]{2,1,0:T(8,128)(2,1)}, bf16[24,32,512]{2,1,0:T(8,128)(2,1)S(1)}, u32[]{:S(2)}, u32[]{:S(2)}) collective-permute-start(bf16[24,32,512]{2,1,0:T(8,128)(2,1)} %broadcast_select_fusion.10), channel_id=1, source_target_pairs={{0,1},{1,0},{2,3},{3,2},{4,5},{5,4},{6,7},{7,6},{8,9},{9,8},{10,11... | collective-permute-start | bytes 2359304 | tf_op jit(solution)/shard_map/ppermute | solution.py:24
  523.9 28.7 %collective-permute-start.50 = (bf16[832,512]{1,0:T(8,128)(2,1)S(1)}, bf16[832,512]{1,0:T(8,128)(2,1)S(1)}, u32[]{:S(2)}, u32[]{:S(2)}) collective-permute-start(bf16[832,512]{1,0:T(8,128)(2,1)S(1)} %copy-done.45), channel_id=1, source_target_pairs={{4,2},{6,0},{5,3},{7,1},{12,10},{14,8},{13,11},{15,9},{20,18},{22,... | collective-permute-start | bytes 2555912 | tf_op jit(solution)/shard_map/ppermute | solution.py:515
  525.3 27.3 %collective-permute-start.51 = (f32[513,150]{0,1:T(8,128)S(1)}, f32[513,150]{0,1:T(8,128)S(1)}, u32[]{:S(2)}, u32[]{:S(2)}) collective-permute-start(f32[513,150]{0,1:T(8,128)S(1)} %add.781), channel_id=1, source_target_pairs={{0,16},{8,24},{16,0},{24,8},{1,17},{9,25},{17,1},{25,9},{2,18},{10... | collective-permute-start | bytes 923408 | tf_op jit(solution)/shard_map/ppermute | solution.py:24
  528.1 37.8 %collective-permute-start.48 = (bf16[24,32,512]{2,1,0:T(8,128)(2,1)S(1)}, bf16[24,32,512]{2,1,0:T(8,128)(2,1)S(1)}, u32[]{:S(2)}, u32[]{:S(2)}) collective-permute-start(bf16[24,32,512]{2,1,0:T(8,128)(2,1)S(1)} %get-tuple-element.246), channel_id=1, source_target_pairs={{4,6},{2,0},{5,7},{3,1},{12,14},{10,8},{13,15},{11,9},{20,22},{18,... | collective-permute-start | bytes 2359304 | tf_op jit(solution)/shard_map/ppermute | solution.py:191
  529.4 36.5 %collective-permute-start.49 = (bf16[24,32,512]{2,1,0:T(8,128)(2,1)S(1)}, bf16[24,32,512]{2,1,0:T(8,128)(2,1)S(1)}, u32[]{:S(2)}, u32[]{:S(2)}) collective-permute-start(bf16[24,32,512]{2,1,0:T(8,128)(2,1)S(1)} %get-tuple-element.245), channel_id=1, source_target_pairs={{0,1},{1,0},{2,3},{3,2},{4,5},{5,4},{6,7},{7,6},{8,9},{9,8},{10,11... | collective-permute-start | bytes 2359304 | tf_op jit(solution)/shard_map/ppermute | solution.py:24
  570.4 190.8 %all-reduce.2.cloned.1.call-start = ((), (), s32[]{:S(2)}) async-start(), calls=%async_computation.4 | async-start | bytes 2097152 | tf_op jit(solution)/shard_map/psum | solution.py:770
  571.7 29.1 %collective-permute-start.54 = (f32[513,150]{0,1:T(8,128)S(1)}, f32[513,150]{0,1:T(8,128)S(1)}, u32[]{:S(2)}, u32[]{:S(2)}) collective-permute-start(f32[513,150]{0,1:T(8,128)S(1)} %add.802), channel_id=1, source_target_pairs={{0,2},{2,0},{4,6},{6,4},{1,3},{3,1},{5,7},{7,5},{8,10},{10,8},{12,... | collective-permute-start | bytes 923408 | tf_op jit(solution)/shard_map/ppermute | solution.py:24
  575.0 25.8 %collective-permute-start.53 = (bf16[24,32,512]{2,1,0:T(8,128)(2,1)S(1)}, bf16[24,32,512]{2,1,0:T(8,128)(2,1)S(1)}, u32[]{:S(2)}, u32[]{:S(2)}) collective-permute-start(bf16[24,32,512]{2,1,0:T(8,128)(2,1)S(1)} %select_select_fusion.3), channel_id=1, source_target_pairs={{0,1},{1,0},{2,3},{3,2},{4,5},{5,4},{6,7},{7,6},{8,9},{9,8},{10,11... | collective-permute-start | bytes 2359304 | tf_op jit(solution)/shard_map/ppermute | solution.py:24
  593.3 29.2 %collective-permute-start.52 = (bf16[2,768,512]{2,1,0:T(8,128)(2,1)S(1)}, bf16[2,768,512]{2,1,0:T(8,128)(2,1)S(1)}, u32[]{:S(2)}, u32[]{:S(2)}) collective-permute-start(bf16[2,768,512]{2,1,0:T(8,128)(2,1)S(1)} %pad_maximum_fusion.5), channel_id=1, source_target_pairs={{0,1},{1,0},{2,3},{3,2},{4,5},{5,4},{6,7},{7,6},{8,9},{9,8},{10,11... | collective-permute-start | bytes 4718600 | tf_op jit(solution)/shard_map/ppermute | solution.py:24
  601.6 52.1 %collective-permute-start.57 = (f32[513,150]{0,1:T(8,128)}, f32[513,150]{0,1:T(8,128)}, u32[]{:S(2)}, u32[]{:S(2)}) collective-permute-start(f32[513,150]{0,1:T(8,128)} %add.832), channel_id=1, source_target_pairs={{0,4},{2,6},{4,0},{6,2},{1,5},{3,7},{5,1},{7,3},{8,12},{10,14},{12... | collective-permute-start | bytes 923408 | tf_op jit(solution)/shard_map/ppermute | solution.py:24
  618.8 34.9 %collective-permute-start.56 = (bf16[9,128,512]{2,1,0:T(8,128)(2,1)}, bf16[9,128,512]{2,1,0:T(8,128)(2,1)}, u32[]{:S(2)}, u32[]{:S(2)}) collective-permute-start(bf16[9,128,512]{2,1,0:T(8,128)(2,1)} %pad_maximum_fusion.15), channel_id=1, source_target_pairs={{0,16},{8,24},{16,0},{24,8},{1,17},{9,25},{17,1},{25,9},{2,18},{10... | collective-permute-start | bytes 3538952 | tf_op jit(solution)/shard_map/ppermute | solution.py:24
  621.2 32.5 %collective-permute-start.55 = (bf16[9,128,512]{2,1,0:T(8,128)(2,1)}, bf16[9,128,512]{2,1,0:T(8,128)(2,1)}, u32[]{:S(2)}, u32[]{:S(2)}) collective-permute-start(bf16[9,128,512]{2,1,0:T(8,128)(2,1)} %pad_maximum_fusion.14), channel_id=1, source_target_pairs={{0,8},{8,0},{16,24},{24,16},{1,9},{9,1},{17,25},{25,17},{2,10},{10... | collective-permute-start | bytes 3538952 | tf_op jit(solution)/shard_map/ppermute | solution.py:24
  626.4 23.2 %collective-permute-start.58 = (f32[8,64]{1,0:T(8,128)S(1)}, f32[8,64]{1,0:T(8,128)S(1)}, u32[]{:S(2)}, u32[]{:S(2)}) collective-permute-start(f32[8,64]{1,0:T(8,128)S(1)} %concatenate.111), channel_id=1, source_target_pairs={{0,8},{8,0},{16,24},{24,16},{1,9},{9,1},{17,25},{25,17},{2,10},{10... | collective-permute-start | bytes 6152 | tf_op jit(solution)/shard_map/ppermute | solution.py:24
  677.5 15.8 %collective-permute-start.60 = (bf16[9,64,512]{2,1,0:T(8,128)(2,1)}, bf16[9,64,512]{2,1,0:T(8,128)(2,1)S(1)}, u32[]{:S(2)}, u32[]{:S(2)}) collective-permute-start(bf16[9,64,512]{2,1,0:T(8,128)(2,1)} %get-tuple-element.203), channel_id=1, source_target_pairs={{0,16},{8,24},{16,0},{24,8},{1,17},{9,25},{17,1},{25,9},{2,18},{10... | collective-permute-start | bytes 1769480 | tf_op jit(solution)/shard_map/ppermute | solution.py:24
  678.3 15.3 %collective-permute-start.61 = (bf16[9,64,512]{2,1,0:T(8,128)(2,1)S(1)}, bf16[9,64,512]{2,1,0:T(8,128)(2,1)S(1)}, u32[]{:S(2)}, u32[]{:S(2)}) collective-permute-start(bf16[9,64,512]{2,1,0:T(8,128)(2,1)S(1)} %get-tuple-element.202), channel_id=1, source_target_pairs={{0,8},{8,0},{16,24},{24,16},{1,9},{9,1},{17,25},{25,17},{2,10},{10... | collective-permute-start | bytes 1769480 | tf_op jit(solution)/shard_map/ppermute | solution.py:24
  696.8 20.4 %collective-permute-start.62 = (bf16[9,64,512]{2,1,0:T(8,128)(2,1)}, bf16[9,64,512]{2,1,0:T(8,128)(2,1)}, u32[]{:S(2)}, u32[]{:S(2)}) collective-permute-start(bf16[9,64,512]{2,1,0:T(8,128)(2,1)} %get-tuple-element.201), channel_id=1, source_target_pairs={{0,8},{8,0},{16,24},{24,16},{1,9},{9,1},{17,25},{25,17},{2,10},{10... | collective-permute-start | bytes 1769480 | tf_op jit(solution)/shard_map/ppermute | solution.py:24
  698.0 20.3 %collective-permute-start.63 = (bf16[9,64,512]{2,1,0:T(8,128)(2,1)}, bf16[9,64,512]{2,1,0:T(8,128)(2,1)}, u32[]{:S(2)}, u32[]{:S(2)}) collective-permute-start(bf16[9,64,512]{2,1,0:T(8,128)(2,1)} %get-tuple-element.200), channel_id=1, source_target_pairs={{0,16},{8,24},{16,0},{24,8},{1,17},{9,25},{17,1},{25,9},{2,18},{10... | collective-permute-start | bytes 1769480 | tf_op jit(solution)/shard_map/ppermute | solution.py:24
  720.7 43.3 %collective-permute-start.65 = (bf16[9,128,512]{2,1,0:T(8,128)(2,1)}, bf16[9,128,512]{2,1,0:T(8,128)(2,1)}, u32[]{:S(2)}, u32[]{:S(2)}) collective-permute-start(bf16[9,128,512]{2,1,0:T(8,128)(2,1)} %pad_maximum_fusion.13), channel_id=1, source_target_pairs={{0,8},{8,0},{16,24},{24,16},{1,9},{9,1},{17,25},{25,17},{2,10},{10... | collective-permute-start | bytes 3538952 | tf_op jit(solution)/shard_map/ppermute | solution.py:24
  723.9 40.2 %collective-permute-start.64 = (bf16[9,128,512]{2,1,0:T(8,128)(2,1)}, bf16[9,128,512]{2,1,0:T(8,128)(2,1)}, u32[]{:S(2)}, u32[]{:S(2)}) collective-permute-start(bf16[9,128,512]{2,1,0:T(8,128)(2,1)} %pad_maximum_fusion.10), channel_id=1, source_target_pairs={{0,16},{8,24},{16,0},{24,8},{1,17},{9,25},{17,1},{25,9},{2,18},{10... | collective-permute-start | bytes 3538952 | tf_op jit(solution)/shard_map/ppermute | solution.py:24
  (199 other events, 2014.8 us)
Sparse Core Ops, SparseCore 0:
  22.0 38.9 reduce-scatter.9
  63.9 32.7 reduce-scatter.7
  570.5 33.6 reduce-scatter.11
  701.0 60.2 all-reduce.1

commit v2 on v1

--- a/solution.py
+++ b/solution.py
@@ -82,6 +82,9 @@
     upper = jnp.any(inside & (y > up), axis=0)
     lower = jnp.any(inside & (y + 1 < down), axis=0)
     return upper.reshape(-1), lower.reshape(-1)
+
+
+small_cost = pl.CostEstimate(flops=1024, bytes_accessed=1024, transcendentals=0)
 
 
 def shift_lines(box_ref, first, x_ref, o_ref, width, reverse):
@@ -139,11 +142,95 @@
         ),
         out_shape=jax.ShapeDtypeStruct((out_blocks, cells, 3 * block), bf16),
         input_output_aliases={4: 0} if extra else {},
-        compiler_params=pltpu.CompilerParams(vmem_limit_bytes=40 << 20),
-        cost_estimate=pl.CostEstimate(
-            flops=0, bytes_accessed=8 * blocks * cells * block, transcendentals=0
-        ),
+        compiler_params=pltpu.CompilerParams(vmem_limit_bytes=52 << 20),
+        cost_estimate=small_cost,
     )(places, jnp.reshape(first_line, (1,)).astype(jnp.int32), canvas_box, x, *extra)
+
+
+def chunk_of(cells, width):
+    total = cells // width
+    return max(k for k in range(1, total + 1) if total % k == 0 and k * width <= 1024) * width
+
+
+def conv_slot(wide, slot, weight, keeps, total, width):
+    _, ext, deep = wide.shape
+    _, block, mid = weight[0].shape
+    cells = keeps.shape[1]
+    chunk = chunk_of(cells, width)
+
+    def body(x_ref, *rest):
+        w_refs, keep_ref, o_ref = rest[:3], rest[3], rest[-1]
+        begin = pl.program_id(0) * chunk
+        value = 0.0 if total is None else rest[4][...]
+        for a in range(3):
+            term = jnp.dot(
+                x_ref[0, pl.ds(pl.multiple_of(begin + a * width, width), chunk), :],
+                w_refs[a][...].reshape(3 * block, mid),
+                preferred_element_type=f32,
+            )
+            value = value + (term if a == 1 else keep_ref[a] * term)
+        o_ref[...] = value
+
+    extra = [] if total is None else [total]
+    once = pl.Buffered(1)
+    one = pl.BlockSpec((3, block, mid), lambda c: (0, 0, 0), pipeline_mode=once)
+    return pl.pallas_call(
+        body,
+        grid=(cells // chunk,),
+        in_specs=[
+            pl.BlockSpec((1, ext, deep), lambda c: (slot, 0, 0), pipeline_mode=once),
+            one, one, one,
+            pl.BlockSpec((3, chunk, 1), lambda c: (0, c, 0)),
+        ]
+        + [pl.BlockSpec((chunk, mid), lambda c: (c, 0))] * len(extra),
+        out_specs=pl.BlockSpec((chunk, mid), lambda c: (c, 0)),
+        out_shape=jax.ShapeDtypeStruct((cells, mid), f32),
+        input_output_aliases={5: 0} if extra else {},
+        compiler_params=pltpu.CompilerParams(vmem_limit_bytes=32 << 20),
+        cost_estimate=small_cost,
+    )(wide, *weight, keeps, *extra)
+
+
+def grad_slot(wide, weight, keeps, width, marker=None):
+    ext, deep = wide.shape
+    _, block, mid = weight[0].shape
+    cells = keeps.shape[1]
+    chunk = chunk_of(cells, width)
+
+    def body(x_ref, *rest):
+        w_refs, keep_ref, o_ref = rest[:3], rest[3], rest[-1]
+        begin = pl.program_id(0) * chunk
+        value = 0.0
+        for a in range(3):
+            rows = pl.ds(pl.multiple_of(begin + a * width, width), chunk)
+            term = 0.0
+            for j in range(3):
+                term = term + lax.dot_general(
+                    x_ref[rows, j * mid : (j + 1) * mid],
+                    w_refs[2 - a][j],
+                    contract_last,
+                    preferred_element_type=f32,
+                )
+            value = value + (term if a == 1 else keep_ref[a] * term)
+        o_ref[...] = value.astype(bf16)
+
+    extra = [] if marker is None else [marker]
+    once = pl.Buffered(1)
+    one = pl.BlockSpec((3, block, mid), lambda c: (0, 0, 0), pipeline_mode=once)
+    return pl.pallas_call(
+        body,
+        grid=(cells // chunk,),
+        in_specs=[
+            pl.BlockSpec((ext, deep), lambda c: (0, 0), pipeline_mode=once),
+            one, one, one,
+            pl.BlockSpec((3, chunk, 1), lambda c: (0, c, 0)),
+        ]
+        + [pl.BlockSpec(memory_space=pl.ANY)] * len(extra),
+        out_specs=pl.BlockSpec((chunk, block), lambda c: (c, 0)),
+        out_shape=jax.ShapeDtypeStruct((cells, block), bf16),
+        compiler_params=pltpu.CompilerParams(vmem_limit_bytes=32 << 20),
+        cost_estimate=small_cost,
+    )(wide, *weight, keeps, *extra)
 
 
 def silu_slope(value):
@@ -185,11 +272,6 @@
         step, count = self.step, self.count
         to_right = [(z, z + 1) for z in range(step - 1, count - 1)]
         to_left = [(z, z - 1) for z in range(1, count - step + 1)]
-        if len(dict(to_right + to_left)) == len(to_right + to_left):
-            senders = [z for z, _ in to_right]
-            chosen = choose([self.left, self.right], sum(self.row == z for z in senders))
-            both = lax.ppermute(chosen, "row", to_right + to_left)
-            return [both]
         return [
             lax.ppermute(self.right, "row", to_right),
             lax.ppermute(self.left, "row", to_left),
@@ -241,56 +323,70 @@
             self.todo = self.todo[1:]
 
 
-def sum_images(x, chain, hooks):
-    count = lax.axis_size("img")
-    me = lax.axis_index("img")
-
-    def fly(index, *flights):
-        sent = chain.send()
-        more = hooks.get(index, lambda: [])()
-        got = tie(*flights, *sent, *more)
-        chain.receive(got[len(flights) : len(flights) + len(sent)])
-        return got[: len(flights)], got[len(flights) + len(sent) :]
-
-    if count != 4:
-        total, kept = fly(0, lax.psum(x, "img"))
-        while chain.todo:
-            fly(9)
-        return total[0].astype(f32), kept
-    quarter = x.shape[1] // 4
-    half = quarter // 2
-
-    def piece(j, side):
-        at = (me ^ j) * quarter + side * half
-        return lax.dynamic_slice_in_dim(x, at, half, 1)
-
-    def add(a, b):
-        return (a.astype(f32) + b.astype(f32)).astype(bf16)
-
-    (a_in, b_in), kept = fly(
-        0,
-        swap(jnp.concatenate([piece(1, 0), piece(3, 0)], axis=1), "img", 1),
-        swap(jnp.concatenate([piece(2, 1), piece(3, 1)], axis=1), "img", 2),
-    )
-    a_own, a_far = add(piece(0, 0), a_in[:, :half]), add(piece(2, 0), a_in[:, half:])
-    b_own, b_far = add(piece(0, 1), b_in[:, :half]), add(piece(1, 1), b_in[:, half:])
-    (a_two, b_one), _ = fly(1, swap(a_far, "img", 2), swap(b_far, "img", 1))
-    a_own, b_own = add(a_own, a_two), add(b_own, b_one)
-    (a_next, b_next), _ = fly(2, swap(a_own, "img", 1), swap(b_own, "img", 2))
-    (a_rest, b_rest), _ = fly(
-        3,
-        swap(jnp.concatenate([a_own, a_next], axis=1), "img", 2),
-        swap(jnp.concatenate([b_own, b_next], axis=1), "img", 1),
-    )
-    while chain.todo:
-        fly(9)
-    parts = [
-        (a_own, b_own),
-        (a_next, b_rest[:, :half]),
-        (a_rest[:, :half], b_next),
-        (a_rest[:, half:], b_rest[:, half:]),
-    ]
-    return place_images([jnp.concatenate(part, axis=1) for part in parts], f32), kept
+def mark(*arrays):
+    tiny = jnp.zeros((8, 128), f32)
+    *arrays, tiny = tie(*arrays, tiny)
+    return arrays, swap(tiny, "col", 1)
+
+
+def add_low(a, b):
+    return (a.astype(f32) + b.astype(f32)).astype(bf16)
+
+
+class ImageSum:
+    def __init__(self, x):
+        self.x = x
+        self.me = lax.axis_index("img")
+        self.half = x.shape[1] // 8
+
+    def piece(self, j, side):
+        at = (self.me ^ j) * 2 * self.half + side * self.half
+        return lax.dynamic_slice_in_dim(self.x, at, self.half, 1)
+
+    def first_sends(self):
+        return [
+            jnp.concatenate([self.piece(1, 0), self.piece(3, 0)], axis=1),
+            jnp.concatenate([self.piece(2, 1), self.piece(3, 1)], axis=1),
+        ]
+
+    def first(self, sends):
+        return [swap(sends[0], "img", 1), swap(sends[1], "img", 2)]
+
+    def second_sends(self, got):
+        half = self.half
+        self.own = [add_low(self.piece(0, k), got[k][:, :half]) for k in range(2)]
+        return [
+            add_low(self.piece(2, 0), got[0][:, half:]),
+            add_low(self.piece(1, 1), got[1][:, half:]),
+        ]
+
+    def second(self, sends):
+        return [swap(sends[0], "img", 2), swap(sends[1], "img", 1)]
+
+    def reduced(self, got):
+        self.own = [add_low(a, b) for a, b in zip(self.own, got)]
+        return self.own
+
+    def third(self, own):
+        self.own = own
+        return [swap(own[0], "img", 1), swap(own[1], "img", 2)]
+
+    def fourth_sends(self, got):
+        self.next = got
+        return [jnp.concatenate([own, near], axis=1) for own, near in zip(self.own, got)]
+
+    def fourth(self, sends):
+        return [swap(sends[0], "img", 2), swap(sends[1], "img", 1)]
+
+    def gathered(self, got):
+        half = self.half
+        parts = [
+            (self.own[0], self.own[1]),
+            (self.next[0], got[1][:, :half]),
+            (got[0][:, :half], self.next[1]),
+            (got[0][:, half:], got[1][:, half:]),
+        ]
+        return place_images([jnp.concatenate(part, axis=1) for part in parts], f32)
 
 
 def join_cols(mine, others, axis):
@@ -299,11 +395,11 @@
     return jnp.concatenate([choose(pieces, col ^ c) for c in range(len(pieces))], axis=axis)
 
 
-def row_halo(strip):
+def row_halo(lines):
     count = lax.axis_size("row")
-    above = lax.ppermute(strip[:, -1:], "row", [(i, i + 1) for i in range(count - 1)])
-    below = lax.ppermute(strip[:, :1], "row", [(i + 1, i) for i in range(count - 1)])
-    return jnp.concatenate([above, strip, below], axis=1)
+    above = lax.ppermute(lines[-1:], "row", [(i, i + 1) for i in range(count - 1)])
+    below = lax.ppermute(lines[:1], "row", [(i + 1, i) for i in range(count - 1)])
+    return jnp.concatenate([above, lines, below], axis=0)
 
 
 def on_device(
@@ -342,76 +438,86 @@
 
     weight = jnp.transpose(conv_w, (1, 0, 2))
     share = block // images
-    rows = Rows(lax.dynamic_slice_in_dim(weight, img * share, share, 1))
+    own_share, tile = tie(
+        lax.dynamic_slice_in_dim(weight, img * share, share, 1),
+        features[0].reshape(pixels, channels_in),
+    )
+    rows = Rows(own_share)
 
     def by_line(nine):
         return [nine[3 * a : 3 * a + 3] for a in range(3)]
 
     weights = [by_line(weight)]
-    waiting = {"cross": None, "close": None, "next": 1}
+    waiting = {"next": 1, "send": [], "plan": [], "slot": None, "place": []}
+
+    def weight_plan(before=()):
+        plan, send = [], [[], []]
+        if waiting["slot"] is not None:
+            pieces = waiting["slot"]
+            half = share // 2
+            send[0].append(pieces[2][:, half:])
+            send[1].append(pieces[1][:, :half])
+            plan.append(("close", pieces))
+        if waiting["next"] < row_count and rows.ready(waiting["next"]):
+            part = rows.slot(waiting["next"])
+            waiting["next"] += 1
+            send[0].append(part)
+            send[1].append(part)
+            plan.append(("cross", part))
+        send = [jnp.concatenate(arrays, axis=1) for arrays in send if arrays]
+        placed = waiting["place"] if plan else []
+        got, waiting["mark"] = mark(*send, *before, *placed)
+        waiting["send"], waiting["plan"] = got[: len(send)], plan
+        end = len(got) - len(placed)
+        place_now(got[end:] if plan else waiting["place"])
+        return got[len(send) : end]
+
+    def lines_of(pieces):
+        return [place_images([piece[3 * a : 3 * a + 3] for piece in pieces]) for a in range(3)]
+
+    def place_now(pieces):
+        if pieces:
+            weights.append(lines_of(pieces))
+        waiting["place"] = []
 
     def weight_phase(more=(), hold=()):
-        flights, plan = [], []
-        if rows.more():
-            sent = rows.send()
-            plan.append(("rows", len(sent)))
-            flights += sent
-        if waiting["close"] is not None:
-            _, one, two = waiting["close"]
-            half = share // 2
-            plan.append(("close", 2))
-            flights += [swap(one[:, :half], "img", 2), swap(two[:, half:], "img", 1)]
-        if waiting["cross"] is not None:
-            part = waiting["cross"]
-            if images == 4:
-                plan.append(("cross", 2))
-                flights += [swap(part, "img", 1), swap(part, "img", 2)]
+        flights = [swap(send, "img", k + 1) for k, send in enumerate(waiting["send"])]
+        count = len(flights)
+        hop = waiting["hop"]
+        flights += hop
+        got = tie(*flights, *more, *hold)
+        if hop:
+            rows.receive(got[count : len(flights)])
+        waiting["hop"] = rows.send() if rows.more() else []
+        waiting["slot"] = None
+        at = 0
+        for what, kept in waiting["plan"]:
+            size = share // 2 if what == "close" else share
+            part = [array[:, at : at + size] for array in got[:count]]
+            at += size
+            if what == "close":
+                far = jnp.concatenate([part[1], part[0]], axis=1)
+                waiting["place"] = kept + [far]
             else:
-                plan.append(("all", images - 1))
-                flights += [swap(part, "img", step) for step in range(1, images)]
-        got = tie(*flights, *more, *hold)
-        at = 0
-        closed, crossed = waiting["close"], waiting["cross"]
-        waiting["close"] = waiting["cross"] = None
-        for what, count in plan:
-            part = got[at : at + count]
-            at += count
-            if what == "rows":
-                rows.receive(part)
-            elif what == "close":
-                pieces = closed + [jnp.concatenate(part, axis=1)]
-                weights.append(
-                    [place_images([piece[3 * a : 3 * a + 3] for piece in pieces]) for a in range(3)]
-                )
-            elif what == "cross":
-                waiting["close"] = [crossed] + list(part)
-            else:
-                pieces = [crossed] + list(part)
-                weights.append(
-                    [place_images([piece[3 * a : 3 * a + 3] for piece in pieces]) for a in range(3)]
-                )
-        if waiting["next"] < row_count and rows.ready(waiting["next"]):
-            waiting["cross"] = rows.slot(waiting["next"])
-            waiting["next"] += 1
+                waiting["slot"] = [kept] + part
+        at = len(flights)
         return got[at : at + len(more)], got[at + len(more) :]
 
-    weight_phase()
-
-    tile = features[0].reshape(pixels, channels_in)
+    waiting["hop"] = rows.send()
+
+    tile_ext = row_halo(tile.reshape(tile_h, tile_w, channels_in))
 
     def channels_of(c):
         at = [(r * col_count + c) * block for r in range(feature_rows)]
-        return jnp.stack([tile[:, k : k + block] for k in at])
+        return jnp.stack([tile_ext[..., k : k + block] for k in at])
 
     by_col = [channels_of(c) for c in range(col_count)]
-    sent = [
-        choose(by_col, col ^ step).reshape(feature_rows, tile_h, tile_w, block)
-        for step in range(col_count)
-    ]
-    strip = join_cols(
+    sent = [choose(by_col, col ^ step) for step in range(col_count)]
+    strip_ext = join_cols(
         sent[0], [swap(sent[step], "col", step) for step in range(1, col_count)], 2
     )
-    strip_ext = row_halo(strip)
+    weight_phase()
+    (strip_ext,) = weight_plan([strip_ext])
 
     boxes = of_bin_boxes(canvas_box, table)
     scale, bin_i, bin_j = (jnp.asarray(table[:, k]) for k in (1, 3, 4))
@@ -442,6 +548,13 @@
         axis=1,
     )
     pre = lax.psum_scatter(pre_local, ("row", "col"), scatter_dimension=0, tiled=True)
+    cat_blocks = strip_ext.reshape(feature_rows, -1, block)
+    slots_of = row ^ jnp.arange(row_count, dtype=jnp.int32)
+    cat_wide = shifted(
+        cat_blocks, canvas_box, top - 1, width, places=slots_of[:feature_rows],
+        out_blocks=row_count,
+    )
+    _, (pre, cat_wide) = weight_phase(hold=[pre, cat_wide])
     part = branch_width // groups
     group = row * col_count + col
 
@@ -456,15 +569,16 @@
 
     counts = np.asarray([images * regions * s * s for s in bin_scales], np.float32)[:, None]
     moments = butterfly(jnp.concatenate([by_scale(pre), by_scale(pre * pre)], axis=0), ("img",))
+    moments, cat_wide = weight_plan([moments, cat_wide])
     center = moments[:4] / counts
     inverse = lax.rsqrt(moments[4:] / counts - center * center + norm_eps)
     gain_part = branch_part(branch_gain)
     inverse_bins = to_bins(inverse)
     normed = (pre - to_bins(center)) * inverse_bins
     before = gain_part * normed + branch_part(branch_bias)
-    _, (act_part,) = weight_phase(hold=[jax.nn.silu(before).astype(bf16)])
     act_branch = lax.all_gather(
-        act_part, ("row", "col"), axis=0, tiled=True
+        (jax.nn.silu(before) + waiting["mark"][0, 0]).astype(bf16),
+        ("row", "col"), axis=0, tiled=True,
     )
 
     def block_rows_of(r):
@@ -489,12 +603,6 @@
 
     spread_ext = ext_spread(row)
     ups = jnp.stack([up_blocks(spread_ext, r) for r in range(feature_rows, row_count)])
-    cat_blocks = strip_ext.reshape(feature_rows, ext_cells, block)
-    slots_of = row ^ jnp.arange(row_count, dtype=jnp.int32)
-    cat_wide = shifted(
-        cat_blocks, canvas_box, top - 1, width, places=slots_of[:feature_rows],
-        out_blocks=row_count,
-    )
     cat_wide = shifted(
         ups, canvas_box, top - 1, width, places=slots_of[feature_rows:],
         out_blocks=row_count, into=cat_wide,
@@ -504,53 +612,32 @@
     def strip_of(cells, source):
         return lax.dynamic_slice_in_dim(cells, source * strip_cells, strip_cells, 0)
 
-    keeps = [strip_of(upper, row)[:, None], None, strip_of(lower, row)[:, None]]
-
-    (cat_moves,) = weight_phase(hold=[cat_blocks])[1]
-
-    def moved(step, begin, end):
-        to = jnp.minimum(row ^ step, feature_rows - 1)
-        taken = lax.dynamic_index_in_dim(cat_moves, to, 0, keepdims=False)[begin:end]
-        pairs = [(i, i ^ step) for i in range(row_count) if (i ^ step) < feature_rows]
-        return lax.ppermute(taken, "row", pairs) if step else taken
-
-    half = ext_cells // 2
-    moves = []
-    for step in [2, 1] + list(range(3, row_count)):
-        moves += [(step, 0, half), (step, half, ext_cells)]
-    landed = {(0, 0): moved(0, 0, half), (0, half): moved(0, half, ext_cells)}
-
-    def take_moves(count):
-        taken = moves[:count]
-        del moves[:count]
-        return taken
-
-    def land(taken, got):
-        for (step, begin, _), array in zip(taken, got):
-            landed[(step, begin)] = array
-
-    hidden_strip = 0.0
-    for slot in range(row_count):
+    keeps = jnp.stack(
+        [strip_of(upper, row), jnp.ones((strip_cells,), bool), strip_of(lower, row)]
+    ).astype(f32)[:, :, None]
+
+    depth = row_count // 2
+    place = lax.rem(row, depth)
+    _, (cat_wide, cat_blocks) = weight_phase(hold=[cat_wide, cat_blocks])
+
+    def moved(step):
+        return lax.dynamic_index_in_dim(cat_blocks, place ^ step, 0, keepdims=False)
+
+    own_ext, *sends, cat_wide = weight_plan([moved(step) for step in range(depth)] + [cat_wide])
+    feature_exts = {0: own_ext}
+    hidden_strip = conv_slot(cat_wide, 0, weights[0], keeps, None, width)
+    for slot in range(1, row_count):
         while len(weights) <= slot:
-            taken = take_moves(1 if len(moves) == 2 * (row_count - 1) else 2)
-            got, hold = weight_phase(
-                more=[moved(*move) for move in taken], hold=[hidden_strip] if slot else []
-            )
-            land(taken, got)
-            if hold:
-                hidden_strip = hold[0]
-        for a in (1, 0, 2):
-            term = dot(
-                cat_wide[slot, a * width : a * width + strip_cells],
-                weights[slot][a].reshape(3 * block, mid),
-            )
-            hidden_strip = hidden_strip + (
-                term if a == 1 else jnp.where(keeps[a], term, 0.0)
-            )
-    own_means = lax.psum_scatter(
-        local_means.astype(bf16), ("row", "col"), scatter_dimension=1, tiled=True
-    )
-    hidden_strip, own_means = tie(hidden_strip, own_means)
+            step = len(feature_exts)
+            more = [swap(sends[step - 1], "row", step)] if step < depth else []
+            got, hold = weight_phase(more=more, hold=[hidden_strip])
+            if got:
+                feature_exts[step] = got[0]
+            (hidden_strip,) = weight_plan(hold)
+        hidden_strip = conv_slot(cat_wide, slot, weights[slot], keeps, hidden_strip, width)
+    for step in range(1, depth):
+        if step not in feature_exts:
+            feature_exts[step] = swap(sends[step - 1], "row", step)
     hidden_strip = hidden_strip.reshape(tile_h, width, mid)
 
     def cells_of(step):
@@ -582,6 +669,7 @@
         everywhere,
     )
     conv_gain_grad, conv_bias_grad = mid_grads[0], mid_grads[1]
+    background = ("col", "row", "img")
     class_chain = Chain(
         jnp.concatenate(
             [
@@ -590,7 +678,7 @@
             ],
             axis=0,
         ),
-        everywhere,
+        background,
     )
     grad_hidden = (
         conv_gain
@@ -598,102 +686,90 @@
         * (grad_before - conv_bias_grad / all_cells - normed_mid * conv_gain_grad / all_cells)
     ).astype(bf16)
 
+    def pair_strip(mine):
+        return [swap(mine, "col", step) for step in range(1, col_count)]
+
+    grad_hidden, mean_moves = tie(grad_hidden, local_means.astype(bf16))
+    own_means = lax.psum_scatter(mean_moves, ("row", "col"), scatter_dimension=1, tiled=True)
     grad_tile = grad_hidden.reshape(tile_h, tile_w, mid)
-    grad_strip = join_cols(
-        grad_tile, [swap(grad_tile, "col", step) for step in range(1, col_count)], 1
-    )
-    hops = Rows(grad_tile)
-    grad_ext = row_halo(grad_strip[None]).reshape(1, ext_cells, mid)
+    hops = [swap(grad_tile, "row", step) for step in range(1, depth)]
+    grad_ext = row_halo(grad_tile)
+    grad_ext = join_cols(grad_ext, pair_strip(grad_ext), 1)
+    grad_strip = grad_ext[1:-1]
+    grad_ext = grad_ext.reshape(1, ext_cells, mid)
     own_wide = shifted(grad_ext, canvas_box, top - 1, width, reverse=True)[0]
 
-    def input_grads(slot):
-        sums = []
+    def input_grads(slot, marker=None):
+        return grad_slot(own_wide, weights[slot], keeps, width, marker)
+
+    low_zero = jnp.zeros((), bf16)
+    lower_half = row < depth
+    up_exts = [choose([ups[r] for r in range(depth)], place)] + [
+        up_blocks(ext_spread(row ^ step), feature_rows + place) for step in range(1, depth)
+    ]
+    exts = [
+        (
+            jnp.where(lower_half, up_exts[step], feature_exts[step]),
+            jnp.where(lower_half, feature_exts[step], up_exts[step]),
+        )
+        for step in range(depth)
+    ]
+    sides = []
+    for kind in range(2):
+        lines = []
         for a in range(3):
-            sums.append(
-                sum(
-                    dot(
-                        own_wide[a * width : a * width + strip_cells, j * mid : (j + 1) * mid],
-                        weights[slot][2 - a][j],
-                        contract_last,
-                    )
-                    for j in range(3)
-                )
-            )
-        total = sums[1] + jnp.where(keeps[0], sums[0], 0.0) + jnp.where(keeps[2], sums[2], 0.0)
-        return total.astype(bf16)
-
-    conv_sums = [0.0] * taps
-
-    def weight_grads(slot, strip):
-        source = row ^ slot
-        ext = jnp.where(
-            row < feature_rows,
-            jnp.concatenate([landed[(slot, 0)], landed[(slot, half)]], axis=0),
-            up_blocks(ext_spread(source), row),
+            pieces = []
+            for step in range(depth):
+                piece = exts[step][kind][a * width : a * width + strip_cells]
+                if a != 1:
+                    keep = strip_of((upper, None, lower)[a], row ^ step)
+                    piece = jnp.where(keep[:, None], piece, low_zero)
+                pieces.append(piece)
+            lines.append(jnp.concatenate(pieces, axis=0))
+        sides.append(lines)
+
+    def phase(flights, hold=()):
+        sent = class_chain.send()
+        got = tie(*flights, *sent, *hold)
+        class_chain.receive(got[len(flights) : len(flights) + len(sent)])
+        return got[: len(flights)], got[len(flights) + len(sent) :]
+
+    wides = shifted(
+        grad_strip.reshape(1, strip_cells, mid), canvas_box, top, width, reverse=True,
+        places=jnp.zeros((1,), jnp.int32), out_blocks=depth,
+    )
+    held = [input_grads(slot) for slot in range(depth)]
+    hops, held = phase(hops, held + [wides, *sides[0], *sides[1]])
+    cat_grads, wides = held[:depth], held[depth]
+    sides = [held[depth + 1 : depth + 4], held[depth + 4 :]]
+    for k, tile_there in enumerate(hops):
+        strip = join_cols(tile_there, pair_strip(tile_there), 1)
+        wides = shifted(
+            strip.reshape(1, strip_cells, mid), canvas_box, (row ^ (k + 1)) * tile_h, width,
+            reverse=True, places=jnp.full((1,), k + 1, jnp.int32), out_blocks=depth, into=wides,
         )
-        if slot == 0:
-            wide = own_wide[width : width + strip_cells]
-        else:
-            wide = shifted(
-                strip.reshape(1, strip_cells, mid), canvas_box, source * tile_h, width,
-                reverse=True,
-            )[0]
-        masks = [strip_of(upper, source), None, strip_of(lower, source)]
-        for a in range(3):
-            side = ext[a * width : a * width + strip_cells]
-            if a != 1:
-                side = jnp.where(masks[a][:, None], side, jnp.zeros((), bf16))
-            for j in range(3):
-                conv_sums[3 * a + j] = conv_sums[3 * a + j] + dot(
-                    side, wide[:, j * mid : (j + 1) * mid], contract_first
-                )
-
-    cat_grads, strips, swapping, asked = [], {0: grad_strip}, None, 1
-    while len(strips) < row_count:
-        flights, plan = [], []
-        if hops.more():
-            sent = hops.send()
-            plan.append(("hops", len(sent)))
-            flights += sent
-        if swapping is not None:
-            plan.append(("swap", col_count - 1))
-            flights += [swap(swapping[1], "col", step) for step in range(1, col_count)]
-        taken = take_moves(1)
-        plan.append(("moves", len(taken)))
-        flights += [moved(*move) for move in taken]
-        sent = class_chain.send()
-        plan.append(("class", len(sent)))
-        flights += sent
-        held = [input_grads(len(cat_grads))] if len(cat_grads) < row_count else []
-        if len(cat_grads) + 1 < row_count and len(cat_grads) > 0:
-            held.append(input_grads(len(cat_grads) + 1))
-        got = tie(*flights, *held)
-        cat_grads += got[len(flights) :]
-        at = 0
-        swapped, swapping = swapping, None
-        for what, count in plan:
-            part = got[at : at + count]
-            at += count
-            if what == "hops":
-                hops.receive(part)
-            elif what == "swap":
-                strips[swapped[0]] = join_cols(swapped[1], part, 1)
-            elif what == "moves":
-                land(taken, part)
-            else:
-                class_chain.receive(part)
-        if asked < row_count and hops.ready(asked):
-            swapping = (asked, hops.slot(asked))
-            asked += 1
-    while moves:
-        taken = take_moves(2)
-        land(taken, [moved(*move) for move in taken])
-    while len(cat_grads) < row_count:
-        cat_grads.append(input_grads(len(cat_grads)))
+    wides = wides.reshape(depth * strip_cells, 3 * mid)
+
+    def weight_grads(kind):
+        return jnp.stack(
+            [
+                dot(
+                    sides[kind][a], wides[:, j * mid : (j + 1) * mid], contract_first
+                ).astype(bf16)
+                for a in range(3)
+                for j in range(3)
+            ]
+        )
+
+    away = ImageSum(weight_grads(0))
+    sends, marker = mark(*away.first_sends())
+    flights = away.first(sends)
+    held = [input_grads(slot, marker) for slot in range(depth, row_count)]
+    got, held = phase(flights, held + [own_means, wides])
+    cat_grads += held[:-2]
+    own_means, wides = held[-2:]
+    flights = away.second(away.second_sends(got))
     by_row = [choose(cat_grads, row ^ r) for r in range(row_count)]
-    for slot in range(row_count):
-        weight_grads(slot, strips[slot])
-    conv_term = jnp.stack(conv_sums).astype(bf16)
     spread_strip = lax.slice_in_dim(spread_ext, width, width + strip_cells, axis=1)
     grad_bins_local = jnp.zeros((branch_width, bins), f32)
     for r in range(feature_rows, row_count):
@@ -704,6 +780,10 @@
         at = lax.rem(first, branch_width)
         old = lax.dynamic_slice_in_dim(grad_bins_local, at, block, 0)
         grad_bins_local = lax.dynamic_update_slice_in_dim(grad_bins_local, old + terms, at, 0)
+    wides, grad_bins_local = tie(wides, grad_bins_local)
+    got, (home,) = phase(flights, [weight_grads(1)])
+    home = ImageSum(home)
+    crossing = [swap(jnp.concatenate(away.reduced(got), axis=1), "row", depth)]
     grad_bins = lax.psum_scatter(
         grad_bins_local, ("row", "col"), scatter_dimension=0, tiled=True
     )
@@ -711,6 +791,9 @@
     branch_sums = butterfly(
         jnp.concatenate([by_scale(grad_act * normed), by_scale(grad_act)], axis=0), ("img",)
     )
+    got, (branch_sums,) = phase(home.first(home.first_sends()), [branch_sums])
+    sends, second_mark = mark(*home.second_sends(got))
+    flights = home.second(sends)
     grad_pre = (
         gain_part
         * inverse_bins
@@ -720,18 +803,25 @@
             - normed * to_bins(branch_sums[:4] / counts)
         )
     ).astype(bf16)
-    conv_w_grad, (grad_pre, branch_sums) = sum_images(
-        conv_term, class_chain, {0: lambda: [grad_pre, branch_sums]}
-    )
+    got, _ = phase(flights + crossing)
+    home_own = home.reduced(got[:2])
+    crossed = [got[2][:, : home.half], got[2][:, home.half :]]
+    home_own = [add_low(a, b) for a, b in zip(home_own, crossed)]
+    got, _ = phase(home.third(home_own))
+    sends, fourth_mark = mark(*home.fourth_sends(got))
+    got = home.fourth(sends)
+    while class_chain.todo:
+        phase([])
     class_w_grad, class_bias_grad = class_chain.value[:mid], class_chain.value[mid]
     gathered = lax.all_gather(
-        jnp.concatenate([grad_pre.astype(f32), branch_sums.T], axis=1),
+        jnp.concatenate([grad_pre.astype(f32), branch_sums.T], axis=1) + second_mark[0, 0],
         ("row", "col"), axis=0, tiled=True,
     )
     grad_pre = gathered[:, :bins].astype(bf16)
     branch_all = gathered[:, bins:].T
     branch_gain_grad, branch_bias_grad = branch_all[:4], branch_all[4:]
 
+    late_pre = (gathered[:, :bins] + fourth_mark[0, 0]).astype(bf16)
     weight_terms, bin_grads = [], []
     for position in range(4):
         span = slice(limits[position], limits[position + 1])
@@ -739,7 +829,9 @@
             dot(own_means[span], grad_pre[:, span], (((0,), (1,)), ((), ())))
         )
         bin_grads.append(
-            dot(grad_pre[:, span], branch_projection_weight[position], (((0,), (1,)), ((), ())))
+            dot(
+                late_pre[:, span], branch_projection_weight[position], (((0,), (1,)), ((), ()))
+            )
         )
     bin_grads = (jnp.concatenate(bin_grads, axis=0) / sizes[:, None]).astype(bf16)
     grad_pool = dot(pooling, bin_grads, contract_first)
@@ -767,7 +859,10 @@
     )
     feature_grad = (joined.astype(f32) + grad_pool).reshape(1, tile_h, tile_w, channels_in)
 
-    branch_w_grad = lax.psum(jnp.stack(weight_terms).astype(bf16), "img").astype(f32)
+    branch_w_grad = lax.psum(jnp.stack(weight_terms).astype(bf16), "img")
+    branch_w_grad, *got = tie(branch_w_grad, *got)
+    branch_w_grad = branch_w_grad.astype(f32)
+    conv_w_grad = home.gathered(got)
     conv_w_grad = jnp.transpose(conv_w_grad, (1, 0, 2))
     return (
         logits.reshape(1, tile_h, tile_w, classes),

time: 790 us -> 624 us (0.79)
  matrix products: 254 us -> 80.6 us
  waiting for transfers between devices: 197 us -> 101 us
  Pallas kernels: 28.5 us -> 112 us
  other arithmetic: 73.9 us -> 101 us
  blocking collectives: 33.7 us -> 55.7 us
  starting transfers between devices: 83.8 us -> 67.9 us
  local copies, waits for them, and re-layouts: 92.5 us -> 79.8 us
    dot_general x109 -> x40, matrix products: 254 us -> 80.6 us  [dot(): return lax.dot_general(a, b, dims, preferred_element_type=f32)]
    pallas_call x0 -> x8, Pallas kernels: none -> 77.9 us  [the longest x4 46.2 us: conv_slot(): pl.pallas_call(body, grid=(cells // chunk,), in_specs=[pl.BlockSpec((1, e...]
    ppermute x46 -> x51, waiting for transfers between devices: 104 us -> 50.1 us  [swap(): return lax.ppermute(value, axis, [(i, i ^ step) for i in range(count)])]
    ppermute x12 -> x4, waiting for transfers between devices: 50.1 us -> 3.34 us  [the longest x2 3.33 us: row_halo(): lax.ppermute(lines[:1], 'row', [(i + 1, i) for i in range(count - 1)])]
    concatenate x7 -> x18, other arithmetic: 7.67 us -> 26.1 us  [the longest x6 11.4 us: on_device(): lines.append(jnp.concatenate(pieces, axis=0))]
    ppermute x4 -> x3, waiting for transfers between devices: 18.4 us -> 0.01 us  [send(): lax.ppermute(self.right, 'row', to_right)]
    unnamed x394 -> x293, local copies, waits for them, and re-layouts: 14 us -> 32.3 us
    dynamic_update_slice x18, local copies, waits for them, and re-layouts: 24.6 us -> 7.22 us  [place_images(): lax.dynamic_update_slice_in_dim(joined, piece.astype(kind), (me ^ step) *...]
  transfers between devices with their start and end apart: 70 -> 65, of which waited for: 25 -> 27; matrix products, arithmetic and copies ran while one was open for 47% -> 32% of each run, Pallas kernels for 4% -> 16%
where the time goes in v2:
time: 624 us; the launch traced here: 615 us
  Pallas kernels  112 us (18%)
  other arithmetic  101 us (16%)
  waiting for transfers between devices  101 us (16%)
  matrix products  80.6 us (13%)
  local copies, waits for them, and re-layouts  79.8 us (13%)
  starting transfers between devices  67.9 us (11%)
  blocking collectives  55.7 us (9%)
  between operations  16.8 us (3%)
    dot_general x40, matrix products, dot(): return lax.dot_general(a, b, dims, preferred_element_type=f32)  80.6 us
    ppermute x51, waiting for transfers between devices, swap(): return lax.ppermute(value, axis, [(i, i ^ step) for i in range(count)])  50.1 us
    pallas_call x4, Pallas kernels, conv_slot(): pl.pallas_call(body, grid=(cells // chunk,), in_specs=[pl.BlockSpec((1, e...  46.2 us
    ppermute x51, starting transfers between devices, swap(): return lax.ppermute(value, axis, [(i, i ^ step) for i in range(count)])  41.3 us
    pallas_call x5, Pallas kernels, shifted(): pl.pallas_call(body, grid_spec=pltpu.PrefetchScalarGridSpec(num_scalar_pr...  33.9 us
    unnamed x293, local copies, waits for them, and re-layouts  32.3 us
    pallas_call x4, Pallas kernels, grad_slot(): pl.pallas_call(body, grid=(cells // chunk,), in_specs=[pl.BlockSpec((ext,...  31.7 us
    all_gather x1, blocking collectives, on_device(): lax.all_gather(jnp.concatenate([grad_pre.astype(f32), branch_sums.T], axi...  30.7 us
  transfers between devices with their start and end apart: 65, of which 27 were waited for; matrix products, arithmetic and copies ran while one was open for 32% of the time, Pallas kernels for 16%

profile of v2, /device:TPU:0, one launch (start us, length us, event | category | flops | bytes accessed | tf_op | source)
XLA Modules:
  0.0 614.7 jit_solution(11866398315981348738)
XLA Ops:
  7.3 2.4 dynamic-slice_bitcast_fusion.2
  9.7 5.9 collective-permute-start
  19.9 5.8 collective-permute-start.2
  26.4 3.9 divide_convert_fusion
  30.4 3.0 fusion.138
  40.4 2.8 copy.207
  44.8 3.3 collective-permute-done.3
  55.6 2.4 broadcast_select_fusion.12
  66.2 4.7 fusion.318
  71.1 4.4 reduce-scatter.10.cloned.1.call-done
  76.5 9.0 %shard_map.366.rest_0_ = bf16[4,1664,1536]{2,1,0:T(8,128)(2,1)} custom-call(s32[2]{0:T(128)S(1)} %get-tuple-element.477.place_ref, s32[1]{0:T(128)} %bitcast.22.first_ref, s32[8,4]{1,0:T(8,128)S(1)} %copy.179.box_ref, bf16[2,1664,512]{2,1,0:T(8,128)(2,1)} %bitcast.296), custom_call_target="tpu_custom_call" | custom-call | flops 1024 | bytes 1024 | tf_op jit(solution)/shard_map/pallas_call | solution.py:129
  85.5 5.9 collective-permute-done.8
  110.6 25.0 %all_gather.6 = bf16[512,400]{1,0:T(8,128)(2,1)S(1)} all-gather(bf16[64,400]{1,0:T(8,128)(2,1)S(1)} %get-tuple-element.317), channel_id=1, replica_groups=mesh['img'=4,'row'=4,'col'=2] {'row','col'}, dimensions={0}, use_global_device_ids=true | all-gather | bytes 460800 | tf_op jit(solution)/shard_map/all_gather | solution.py:579
  135.8 3.1 convolution_convert_fusion.1
  138.9 3.1 convolution_convert_fusion.2
  142.0 2.3 pad_maximum_fusion.2.x_ref
  144.3 9.4 %shard_map.367.x_ref = bf16[4,1664,1536]{2,1,0:T(8,128)(2,1)} custom-call(s32[2]{0:T(128)S(1)} %get-tuple-element.476.place_ref, s32[1]{0:T(128)} %bitcast.22.first_ref, s32[8,4]{1,0:T(8,128)S(1)} %copy.179.box_ref, bf16[2,1664,512]{2,1,0:T(8,128)(2,1)} %pad_maximum_fusion.2.x_ref, ...), custom_call_target="tpu_custom_call", output_to_operand_aliasing={{}: (4, {})} | custom-call | flops 1024 | bytes 1024 | tf_op jit(solution)/shard_map/pallas_call | solution.py:129
  167.4 10.2 %shard_map.368.rest_4_ = f32[1536,512]{1,0:T(8,128)S(1)} custom-call(bf16[4,1664,1536]{2,1,0:T(8,128)(2,1)} %shard_map.367.x_ref, bf16[3,512,512]{2,1,0:T(8,128)(2,1)S(1)} %copy-done.28, bf16[3,512,512]{2,1,0:T(8,128)(2,1)S(1)} %copy-done.26, bf16[3,512,512]{2,1,0:T(8,128)(2,1)S(1)} %copy-done.24, f32[3,1536,1]{2,1,0:T(8,128)S(1)} %add_convert_fusion.rest_3_), custom_call_target="tpu_custom_call" | custom-call | flops 1024 | bytes 1024 | tf_op jit(solution)/shard_map/pallas_call | solution.py:177
  181.7 12.0 %shard_map.369.rest_4_ = f32[1536,512]{1,0:T(8,128)S(1)} custom-call(bf16[4,1664,1536]{2,1,0:T(8,128)(2,1)} %shard_map.367.x_ref, bf16[3,512,512]{2,1,0:T(8,128)(2,1)S(1)} %get-tuple-element.418.rest_0_, bf16[3,512,512]{2,1,0:T(8,128)(2,1)S(1)} %get-tuple-element.417.rest_1_, ...), custom_call_target="tpu_custom_call", output_to_operand_aliasing={{}: (5, {})} | custom-call | flops 1024 | bytes 1024 | tf_op jit(solution)/shard_map/pallas_call | solution.py:177
  196.9 6.7 %collective-permute-done.18 = bf16[1664,512]{1,0:T(8,128)(2,1)S(1)} collective-permute-done((bf16[1664,512]{1,0:T(8,128)(2,1)S(1)}, bf16[1664,512]{1,0:T(8,128)(2,1)S(1)}, u32[]{:S(2)}, u32[]{:S(2)}) %collective-permute-start.18) | collective-permute-done | bytes 1703968 | tf_op jit(solution)/shard_map/ppermute | solution.py:24
  207.3 12.0 %shard_map.370.rest_4_ = f32[1536,512]{1,0:T(8,128)S(1)} custom-call(bf16[4,1664,1536]{2,1,0:T(8,128)(2,1)} %shard_map.367.x_ref, bf16[3,512,512]{2,1,0:T(8,128)(2,1)S(1)} %get-tuple-element.409.rest_0_, bf16[3,512,512]{2,1,0:T(8,128)(2,1)S(1)} %get-tuple-element.408.rest_1_, ...), custom_call_target="tpu_custom_call", output_to_operand_aliasing={{}: (5, {})} | custom-call | flops 1024 | bytes 1024 | tf_op jit(solution)/shard_map/pallas_call | solution.py:177
  219.9 12.0 %shard_map.371 = f32[1536,512]{1,0:T(8,128)S(1)} custom-call(bf16[4,1664,1536]{2,1,0:T(8,128)(2,1)} %shard_map.367.x_ref, bf16[3,512,512]{2,1,0:T(8,128)(2,1)S(1)} %get-tuple-element.406.rest_0_, bf16[3,512,512]{2,1,0:T(8,128)(2,1)S(1)} %get-tuple-element.405.rest_1_, ...), custom_call_target="tpu_custom_call", output_to_operand_aliasing={{}: (5, {})} | custom-call | flops 1024 | bytes 1024 | tf_op jit(solution)/shard_map/pallas_call | solution.py:177
  235.0 3.7 collective-permute-done.21
  238.7 3.5 fusion.314
  248.5 3.1 convolution_convert_fusion
  252.3 3.0 collective-permute-done.25
  257.0 2.8 collective-permute-done.26
  277.3 2.3 collective-permute-done.31
  284.2 4.8 collective-permute-start.34
  301.7 5.2 shard_map.372
  307.0 2.4 copy-done.2
  309.4 7.9 %shard_map.373 = bf16[1536,512]{1,0:T(8,128)(2,1)S(1)} custom-call(bf16[1664,1536]{1,0:T(8,128)(2,1)S(1)} %bitcast.267, bf16[3,512,512]{2,1,0:T(8,128)(2,1)S(1)} %copy-done.29, bf16[3,512,512]{2,1,0:T(8,128)(2,1)S(1)} %copy-done.27, bf16[3,512,512]{2,1,0:T(8,128)(2,1)S(1)} %copy-done.25, f32[3,1536,1]{2,1,0:T(8,128)S(1)} %add_convert_fusion.rest_3_), custom_call_target="tpu_custom_call" | custom-call | flops 1024 | bytes 1024 | tf_op jit(solution)/shard_map/pallas_call | solution.py:220
  317.4 7.9 %shard_map.374 = bf16[1536,512]{1,0:T(8,128)(2,1)S(1)} custom-call(bf16[1664,1536]{1,0:T(8,128)(2,1)S(1)} %bitcast.268, bf16[3,512,512]{2,1,0:T(8,128)(2,1)S(1)} %copy-done.19, bf16[3,512,512]{2,1,0:T(8,128)(2,1)S(1)} %copy-done.23, bf16[3,512,512]{2,1,0:T(8,128)(2,1)S(1)} %copy-done.21, f32[3,1536,1]{2,1,0:T(8,128)S(1)} %add_convert_fusion.rest_3_), custom_call_target="tpu_custom_call" | custom-call | flops 1024 | bytes 1024 | tf_op jit(solution)/shard_map/pallas_call | solution.py:220
  326.4 4.9 shard_map.375.rest_0_
  335.2 5.3 shard_map.376
  340.6 3.9 fusion.192
  368.2 3.4 multiply_convert_fusion.1
  372.8 2.4 copy-done.4
  379.5 8.0 %shard_map.377 = bf16[1536,512]{1,0:T(8,128)(2,1)S(1)} custom-call(bf16[1664,1536]{1,0:T(8,128)(2,1)S(1)} %bitcast.269, bf16[3,512,512]{2,1,0:T(8,128)(2,1)S(1)} %copy-done.7, bf16[3,512,512]{2,1,0:T(8,128)(2,1)S(1)} %copy-done.17, bf16[3,512,512]{2,1,0:T(8,128)(2,1)S(1)} %copy-done.15, f32[3,1536,1]{2,1,0:T(8,128)S(1)} %add_convert_fusion.rest_3_, ...), custom_call_target="tpu_custom_call" | custom-call | flops 1024 | bytes 1024 | tf_op jit(solution)/shard_map/pallas_call | solution.py:220
  387.6 7.9 %shard_map.378 = bf16[1536,512]{1,0:T(8,128)(2,1)S(1)} custom-call(bf16[1664,1536]{1,0:T(8,128)(2,1)S(1)} %bitcast.270, bf16[3,512,512]{2,1,0:T(8,128)(2,1)S(1)} %copy-done.9, bf16[3,512,512]{2,1,0:T(8,128)(2,1)S(1)} %copy-done.13, bf16[3,512,512]{2,1,0:T(8,128)(2,1)S(1)} %copy-done.11, f32[3,1536,1]{2,1,0:T(8,128)S(1)} %add_convert_fusion.rest_3_, ...), custom_call_target="tpu_custom_call" | custom-call | flops 1024 | bytes 1024 | tf_op jit(solution)/shard_map/pallas_call | solution.py:220
  396.7 3.2 select_select_fusion.1
  403.0 3.6 add_convert_fusion.13
  417.0 2.6 fusion.246
  419.6 2.6 fusion.228
  422.3 2.6 fusion.210
  424.9 2.6 fusion.240
  427.5 2.6 fusion.222
  430.1 2.6 fusion.204
  432.7 2.6 fusion.234
  435.3 2.8 fusion.216
  438.1 2.6 copy.209
  440.7 4.5 fusion.198
  454.1 2.5 add_convert_fusion.8
  460.9 13.9 %reduce-scatter.12.cloned.1.call-done = f32[64,400]{1,0:T(8,128)} async-done(((f32[512,400]{1,0:T(8,128)}), f32[64,400]{1,0:T(8,128)}) %reduce-scatter.12.cloned.1.call-update) | async-done | bytes 102416 | tf_op jit(solution)/shard_map/reduce_scatter | solution.py:787
  479.0 5.4 collective-permute-done.49
  488.5 3.0 add_convert_fusion.11
  498.1 30.7 %all_gather.7 = f32[512,408]{1,0:T(8,128)S(1)} all-gather(f32[64,408]{1,0:T(8,128)S(1)} %maximum_add_fusion), channel_id=1, replica_groups=mesh['img'=4,'row'=4,'col'=2] {'row','col'}, dimensions={0}, use_global_device_ids=true | all-gather | bytes 940032 | tf_op jit(solution)/shard_map/all_gather | solution.py:816
  531.4 2.9 add_convert_fusion.1
  542.9 11.8 %collective-permute-done.56 = bf16[9,64,512]{2,1,0:T(8,128)(2,1)S(1)} collective-permute-done((bf16[9,64,512]{2,1,0:T(8,128)(2,1)S(1)}, bf16[9,64,512]{2,1,0:T(8,128)(2,1)S(1)}, u32[]{:S(2)}, u32[]{:S(2)}) %collective-permute-start.56) | collective-permute-done | bytes 589856 | tf_op jit(solution)/shard_map/ppermute | solution.py:24
  554.9 2.8 pad_maximum_fusion.20
  567.1 4.8 convert_add_fusion
  571.9 23.8 %all-reduce.2.cloned.1.call-done = bf16[4,256,512]{2,1,0:T(8,128)(2,1)} async-done(((bf16[4,256,512]{2,1,0:T(8,128)(2,1)}), bf16[4,256,512]{2,1,0:T(8,128)(2,1)}) %all-reduce.2.cloned.1.call-update) | async-done | bytes 1048592 | tf_op jit(solution)/shard_map/psum | solution.py:862
  597.3 2.8 convert_element_type.395
  603.3 2.8 convert_dynamic-update-slice_fusion.1
  (624 shorter events, 224.0 us)
Async XLA Ops:
  7.3 68.2 %reduce-scatter.10.cloned.1.call-start = ((), (), s32[]{:S(2)}) async-start(), calls=%async_computation.5 | async-start | bytes 1179648
  9.7 42.8 %collective-permute-start = (bf16[9,128,512]{2,1,0:T(8,128)(2,1)}, bf16[9,128,512]{2,1,0:T(8,128)(2,1)}, u32[]{:S(2)}, u32[]{:S(2)}) collective-permute-start(bf16[9,128,512]{2,1,0:T(8,128)(2,1)} %dynamic-slice_bitcast_fusion.2), channel_id=1, source_target_pairs={{0,2},{2,4},{4,6},{1,3},{3,5},{5,7},{8,10},{10,12},{12,14},{9,11},... | collective-permute-start | bytes 3538952 | tf_op jit(solution)/shard_map/ppermute | solution.py:276
  15.7 36.9 %collective-permute-start.1 = (bf16[9,128,512]{2,1,0:T(8,128)(2,1)}, bf16[9,128,512]{2,1,0:T(8,128)(2,1)}, u32[]{:S(2)}, u32[]{:S(2)}) collective-permute-start(bf16[9,128,512]{2,1,0:T(8,128)(2,1)} %dynamic-slice_bitcast_fusion.2), channel_id=1, source_target_pairs={{2,0},{4,2},{6,4},{3,1},{5,3},{7,5},{10,8},{12,10},{14,12},{11,9},... | collective-permute-start | bytes 3538952 | tf_op jit(solution)/shard_map/ppermute | solution.py:277
  18.6 29.5 %collective-permute-start.3 = (bf16[1,32,2048]{2,1,0:T(8,128)(2,1)}, bf16[1,32,2048]{2,1,0:T(8,128)(2,1)}, u32[]{:S(2)}, u32[]{:S(2)}) collective-permute-start(bf16[1,32,2048]{2,1,0:T(8,128)(2,1)} %get-tuple-element.361), channel_id=1, source_target_pairs={{2,0},{4,2},{6,4},{3,1},{5,3},{7,5},{10,8},{12,10},{14,12},{11,9},... | collective-permute-start | bytes 393224 | tf_op jit(solution)/shard_map/ppermute | solution.py:401
  19.9 28.2 %collective-permute-start.2 = (bf16[1,32,2048]{2,1,0:T(8,128)(2,1)S(1)}, bf16[1,32,2048]{2,1,0:T(8,128)(2,1)}, u32[]{:S(2)}, u32[]{:S(2)}) collective-permute-start(bf16[1,32,2048]{2,1,0:T(8,128)(2,1)S(1)} %get-tuple-element.360), channel_id=1, source_target_pairs={{0,2},{2,4},{4,6},{1,3},{3,5},{5,7},{8,10},{10,12},{12,14},{9,11},... | collective-permute-start | bytes 393224 | tf_op jit(solution)/shard_map/ppermute | solution.py:400
  43.2 353.5 %reduce-scatter.8.cloned.1.call-start = ((), (), s32[]{:S(2)}) async-start(), calls=%async_computation.3 | async-start | bytes 1843200 | tf_op jit(solution)/shard_map/reduce_scatter | solution.py:693
  51.3 6.8 %collective-permute-start.4 = (bf16[2,26,32,512]{3,2,1,0:T(8,128)(2,1)}, bf16[2,26,32,512]{3,2,1,0:T(8,128)(2,1)}, u32[]{:S(2)}, u32[]{:S(2)}) collective-permute-start(bf16[2,26,32,512]{3,2,1,0:T(8,128)(2,1)} %broadcast_select_fusion.6), channel_id=1, source_target_pairs={{0,1},{1,0},{2,3},{3,2},{4,5},{5,4},{6,7},{7,6},{8,9},{9,8},{10,11... | collective-permute-start | bytes 5111816 | tf_op jit(solution)/shard_map/ppermute | solution.py:24
  52.5 33.0 %collective-permute-start.7 = (bf16[9,128,512]{2,1,0:T(8,128)(2,1)}, bf16[9,128,512]{2,1,0:T(8,128)(2,1)}, u32[]{:S(2)}, u32[]{:S(2)}) collective-permute-start(bf16[9,128,512]{2,1,0:T(8,128)(2,1)} %collective-permute-done), channel_id=1, source_target_pairs={{2,4},{4,6},{3,5},{5,7},{10,12},{12,14},{11,13},{13,15},{18,20},{2... | collective-permute-start | bytes 3538952 | tf_op jit(solution)/shard_map/ppermute | solution.py:276
  54.3 37.0 %collective-permute-start.8 = (bf16[9,128,512]{2,1,0:T(8,128)(2,1)}, bf16[9,128,512]{2,1,0:T(8,128)(2,1)}, u32[]{:S(2)}, u32[]{:S(2)}) collective-permute-start(bf16[9,128,512]{2,1,0:T(8,128)(2,1)} %collective-permute-done.1), channel_id=1, source_target_pairs={{2,0},{4,2},{3,1},{5,3},{10,8},{12,10},{11,9},{13,11},{18,16},{20,... | collective-permute-start | bytes 3538952 | tf_op jit(solution)/shard_map/ppermute | solution.py:277
  62.2 29.2 %collective-permute-start.5 = (bf16[9,128,512]{2,1,0:T(8,128)(2,1)}, bf16[9,128,512]{2,1,0:T(8,128)(2,1)}, u32[]{:S(2)}, u32[]{:S(2)}) collective-permute-start(bf16[9,128,512]{2,1,0:T(8,128)(2,1)} %broadcast_select_fusion.12), channel_id=1, source_target_pairs={{0,8},{8,0},{16,24},{24,16},{1,9},{9,1},{17,25},{25,17},{2,10},{10... | collective-permute-start | bytes 3538952 | tf_op jit(solution)/shard_map/ppermute | solution.py:24
  63.7 28.4 %collective-permute-start.6 = (bf16[9,128,512]{2,1,0:T(8,128)(2,1)}, bf16[9,128,512]{2,1,0:T(8,128)(2,1)}, u32[]{:S(2)}, u32[]{:S(2)}) collective-permute-start(bf16[9,128,512]{2,1,0:T(8,128)(2,1)} %broadcast_select_fusion.12), channel_id=1, source_target_pairs={{0,16},{8,24},{16,0},{24,8},{1,17},{9,25},{17,1},{25,9},{2,18},{10... | collective-permute-start | bytes 3538952 | tf_op jit(solution)/shard_map/ppermute | solution.py:24
  92.6 7.8 %collective-permute-start.9 = (f32[8,64]{0,1:T(8,128)S(1)}, f32[8,64]{0,1:T(8,128)S(1)}, u32[]{:S(2)}, u32[]{:S(2)}) collective-permute-start(f32[8,64]{0,1:T(8,128)S(1)} %copy.187), channel_id=1, source_target_pairs={{0,8},{8,0},{16,24},{24,16},{1,9},{9,1},{17,25},{25,17},{2,10},{10... | collective-permute-start | bytes 6152 | tf_op jit(solution)/shard_map/ppermute | solution.py:24
  93.4 60.4 %collective-permute-start.13 = (bf16[9,128,512]{2,1,0:T(8,128)(2,1)}, bf16[9,128,512]{2,1,0:T(8,128)(2,1)}, u32[]{:S(2)}, u32[]{:S(2)}) collective-permute-start(bf16[9,128,512]{2,1,0:T(8,128)(2,1)} %collective-permute-done.7), channel_id=1, source_target_pairs={{4,6},{5,7},{12,14},{13,15},{20,22},{21,23},{28,30},{29,31}} | collective-permute-start | bytes 3538952 | tf_op jit(solution)/shard_map/ppermute | solution.py:276
  95.1 58.7 %collective-permute-start.14 = (bf16[9,128,512]{2,1,0:T(8,128)(2,1)}, bf16[9,128,512]{2,1,0:T(8,128)(2,1)}, u32[]{:S(2)}, u32[]{:S(2)}) collective-permute-start(bf16[9,128,512]{2,1,0:T(8,128)(2,1)} %collective-permute-done.8), channel_id=1, source_target_pairs={{2,0},{3,1},{10,8},{11,9},{18,16},{19,17},{26,24},{27,25}} | collective-permute-start | bytes 3538952 | tf_op jit(solution)/shard_map/ppermute | solution.py:277
  100.5 4.0 collective-permute-start.10
  104.5 49.3 %collective-permute-start.11 = (bf16[9,192,512]{2,1,0:T(8,128)(2,1)}, bf16[9,192,512]{2,1,0:T(8,128)(2,1)}, u32[]{:S(2)}, u32[]{:S(2)}) collective-permute-start(bf16[9,192,512]{2,1,0:T(8,128)(2,1)} %get-tuple-element.119), channel_id=1, source_target_pairs={{0,8},{8,0},{16,24},{24,16},{1,9},{9,1},{17,25},{25,17},{2,10},{10... | collective-permute-start | bytes 5308424 | tf_op jit(solution)/shard_map/ppermute | solution.py:24
  105.7 48.1 %collective-permute-start.12 = (bf16[9,192,512]{2,1,0:T(8,128)(2,1)}, bf16[9,192,512]{2,1,0:T(8,128)(2,1)}, u32[]{:S(2)}, u32[]{:S(2)}) collective-permute-start(bf16[9,192,512]{2,1,0:T(8,128)(2,1)} %get-tuple-element.120), channel_id=1, source_target_pairs={{0,16},{8,24},{16,0},{24,8},{1,17},{9,25},{17,1},{25,9},{2,18},{10... | collective-permute-start | bytes 5308424 | tf_op jit(solution)/shard_map/ppermute | solution.py:24
  161.8 41.9 %collective-permute-start.16 = (bf16[9,192,512]{2,1,0:T(8,128)(2,1)S(1)}, bf16[9,192,512]{2,1,0:T(8,128)(2,1)S(1)}, u32[]{:S(2)}, u32[]{:S(2)}) collective-permute-start(bf16[9,192,512]{2,1,0:T(8,128)(2,1)S(1)} %get-tuple-element.131), channel_id=1, source_target_pairs={{0,8},{8,0},{16,24},{24,16},{1,9},{9,1},{17,25},{25,17},{2,10},{10... | collective-permute-start | bytes 5308424 | tf_op jit(solution)/shard_map/ppermute | solution.py:24
  163.3 40.6 %collective-permute-start.17 = (bf16[9,192,512]{2,1,0:T(8,128)(2,1)S(1)}, bf16[9,192,512]{2,1,0:T(8,128)(2,1)S(1)}, u32[]{:S(2)}, u32[]{:S(2)}) collective-permute-start(bf16[9,192,512]{2,1,0:T(8,128)(2,1)S(1)} %get-tuple-element.132), channel_id=1, source_target_pairs={{0,16},{8,24},{16,0},{24,8},{1,17},{9,25},{17,1},{25,9},{2,18},{10... | collective-permute-start | bytes 5308424 | tf_op jit(solution)/shard_map/ppermute | solution.py:24
  164.8 38.9 %collective-permute-start.18 = (bf16[1664,512]{1,0:T(8,128)(2,1)S(1)}, bf16[1664,512]{1,0:T(8,128)(2,1)S(1)}, u32[]{:S(2)}, u32[]{:S(2)}) collective-permute-start(bf16[1664,512]{1,0:T(8,128)(2,1)S(1)} %get-tuple-element.133), channel_id=1, source_target_pairs={{0,2},{2,0},{4,6},{6,4},{1,3},{3,1},{5,7},{7,5},{8,10},{10,8},{12,... | collective-permute-start | bytes 5111816 | tf_op jit(solution)/shard_map/ppermute | solution.py:24
  204.9 14.7 %collective-permute-start.19 = (bf16[9,64,512]{2,1,0:T(8,128)(2,1)S(1)}, bf16[9,64,512]{2,1,0:T(8,128)(2,1)S(1)}, u32[]{:S(2)}, u32[]{:S(2)}) collective-permute-start(bf16[9,64,512]{2,1,0:T(8,128)(2,1)S(1)} %get-tuple-element.141), channel_id=1, source_target_pairs={{0,8},{8,0},{16,24},{24,16},{1,9},{9,1},{17,25},{25,17},{2,10},{10... | collective-permute-start | bytes 1769480 | tf_op jit(solution)/shard_map/ppermute | solution.py:24
  205.6 14.0 %collective-permute-start.20 = (bf16[9,64,512]{2,1,0:T(8,128)(2,1)S(1)}, bf16[9,64,512]{2,1,0:T(8,128)(2,1)S(1)}, u32[]{:S(2)}, u32[]{:S(2)}) collective-permute-start(bf16[9,64,512]{2,1,0:T(8,128)(2,1)S(1)} %get-tuple-element.142), channel_id=1, source_target_pairs={{0,16},{8,24},{16,0},{24,8},{1,17},{9,25},{17,1},{25,9},{2,18},{10... | collective-permute-start | bytes 1769480 | tf_op jit(solution)/shard_map/ppermute | solution.py:24
  234.9 3.8 collective-permute-start.21
  242.2 1.2 collective-permute-start.22
  243.5 3.7 collective-permute-start.23
  247.2 4.4 collective-permute-start.24
  251.6 3.7 collective-permute-start.25
  255.3 4.5 collective-permute-start.26
  262.9 1.2 collective-permute-start.27
  264.2 3.7 collective-permute-start.28
  267.9 3.7 collective-permute-start.29
  271.5 3.6 collective-permute-start.30
  275.1 4.5 collective-permute-start.31
  282.9 8.0 %collective-permute-start.35 = (bf16[1,32,512]{2,1,0:T(8,128)(2,1)S(1)}, bf16[1,32,512]{2,1,0:T(8,128)(2,1)S(1)}, u32[]{:S(2)}, u32[]{:S(2)}) collective-permute-start(bf16[1,32,512]{2,1,0:T(8,128)(2,1)S(1)} %get-tuple-element.430), channel_id=1, source_target_pairs={{2,0},{4,2},{6,4},{3,1},{5,3},{7,5},{10,8},{12,10},{14,12},{11,9},... | collective-permute-start | bytes 98312 | tf_op jit(solution)/shard_map/ppermute | solution.py:401
  284.2 6.7 %collective-permute-start.34 = (bf16[1,32,512]{2,1,0:T(8,128)(2,1)S(1)}, bf16[1,32,512]{2,1,0:T(8,128)(2,1)S(1)}, u32[]{:S(2)}, u32[]{:S(2)}) collective-permute-start(bf16[1,32,512]{2,1,0:T(8,128)(2,1)S(1)} %get-tuple-element.429), channel_id=1, source_target_pairs={{0,2},{2,4},{4,6},{1,3},{3,5},{5,7},{8,10},{10,12},{12,14},{9,11},... | collective-permute-start | bytes 98312 | tf_op jit(solution)/shard_map/ppermute | solution.py:400
  293.0 7.0 %collective-permute-start.36 = (bf16[26,32,512]{2,1,0:T(8,128)(2,1)}, bf16[26,32,512]{2,1,0:T(8,128)(2,1)}, u32[]{:S(2)}, u32[]{:S(2)}) collective-permute-start(bf16[26,32,512]{2,1,0:T(8,128)(2,1)} %pad_maximum_fusion.31), channel_id=1, source_target_pairs={{0,1},{1,0},{2,3},{3,2},{4,5},{5,4},{6,7},{7,6},{8,9},{9,8},{10,11... | collective-permute-start | bytes 2555912 | tf_op jit(solution)/shard_map/ppermute | solution.py:24
  296.8 34.6 %collective-permute-start.32 = (bf16[24,32,512]{2,1,0:T(8,128)(2,1)}, bf16[24,32,512]{2,1,0:T(8,128)(2,1)}, u32[]{:S(2)}, u32[]{:S(2)}) collective-permute-start(bf16[24,32,512]{2,1,0:T(8,128)(2,1)} %bitcast.63), channel_id=1, source_target_pairs={{0,2},{2,0},{4,6},{6,4},{1,3},{3,1},{5,7},{7,5},{8,10},{10,8},{12,... | collective-permute-start | bytes 2359304 | tf_op jit(solution)/shard_map/ppermute | solution.py:24
  299.8 31.6 %collective-permute-start.33 = (f32[513,150]{0,1:T(8,128)}, f32[513,150]{0,1:T(8,128)}, u32[]{:S(2)}, u32[]{:S(2)}) collective-permute-start(f32[513,150]{0,1:T(8,128)} %pad_maximum_fusion.33), channel_id=1, source_target_pairs={{0,1},{1,0},{2,3},{3,2},{4,5},{5,4},{6,7},{7,6},{8,9},{9,8},{10,11... | collective-permute-start | bytes 923408 | tf_op jit(solution)/shard_map/ppermute | solution.py:24
  331.3 2.5 collective-permute-start.37
  331.7 143.2 %reduce-scatter.12.cloned.1.call-start = ((), (), s32[]{:S(2)}) async-start(), calls=%async_computation.6 | async-start | bytes 1179648 | tf_op jit(solution)/shard_map/reduce_scatter | solution.py:787
  364.6 32.0 %collective-permute-start.38 = (bf16[9,128,512]{2,1,0:T(8,128)(2,1)}, bf16[9,128,512]{2,1,0:T(8,128)(2,1)}, u32[]{:S(2)}, u32[]{:S(2)}) collective-permute-start(bf16[9,128,512]{2,1,0:T(8,128)(2,1)} %pad_maximum_fusion.25), channel_id=1, source_target_pairs={{0,8},{8,0},{16,24},{24,16},{1,9},{9,1},{17,25},{25,17},{2,10},{10... | collective-permute-start | bytes 3538952 | tf_op jit(solution)/shard_map/ppermute | solution.py:24
  366.1 30.6 %collective-permute-start.39 = (bf16[9,128,512]{2,1,0:T(8,128)(2,1)}, bf16[9,128,512]{2,1,0:T(8,128)(2,1)}, u32[]{:S(2)}, u32[]{:S(2)}) collective-permute-start(bf16[9,128,512]{2,1,0:T(8,128)(2,1)} %pad_maximum_fusion.26), channel_id=1, source_target_pairs={{0,16},{8,24},{16,0},{24,8},{1,17},{9,25},{17,1},{25,9},{2,18},{10... | collective-permute-start | bytes 3538952 | tf_op jit(solution)/shard_map/ppermute | solution.py:24
  367.8 28.8 %collective-permute-start.40 = (f32[513,150]{0,1:T(8,128)S(1)}, f32[513,150]{0,1:T(8,128)}, u32[]{:S(2)}, u32[]{:S(2)}) collective-permute-start(f32[513,150]{0,1:T(8,128)S(1)} %fusion.313), channel_id=1, source_target_pairs={{0,2},{2,0},{4,6},{6,4},{1,3},{3,1},{5,7},{7,5},{8,10},{10,8},{12,... | collective-permute-start | bytes 923408 | tf_op jit(solution)/shard_map/ppermute | solution.py:24
  368.2 4.6 collective-permute-start.41
  402.5 56.7 %collective-permute-start.42 = (bf16[2,768,512]{2,1,0:T(8,128)(2,1)}, bf16[2,768,512]{2,1,0:T(8,128)(2,1)}, u32[]{:S(2)}, u32[]{:S(2)}) collective-permute-start(bf16[2,768,512]{2,1,0:T(8,128)(2,1)} %pad_maximum_fusion.17), channel_id=1, source_target_pairs={{0,1},{1,0},{2,3},{3,2},{4,5},{5,4},{6,7},{7,6},{8,9},{9,8},{10,11... | collective-permute-start | bytes 4718600 | tf_op jit(solution)/shard_map/ppermute | solution.py:24
  406.6 38.7 %collective-permute-start.43 = (bf16[9,64,512]{2,1,0:T(8,128)(2,1)}, bf16[9,64,512]{2,1,0:T(8,128)(2,1)}, u32[]{:S(2)}, u32[]{:S(2)}) collective-permute-start(bf16[9,64,512]{2,1,0:T(8,128)(2,1)} %get-tuple-element.342), channel_id=1, source_target_pairs={{0,16},{8,24},{16,0},{24,8},{1,17},{9,25},{17,1},{25,9},{2,18},{10... | collective-permute-start | bytes 1769480 | tf_op jit(solution)/shard_map/ppermute | solution.py:24
  407.8 37.4 %collective-permute-start.44 = (bf16[9,64,512]{2,1,0:T(8,128)(2,1)}, bf16[9,64,512]{2,1,0:T(8,128)(2,1)}, u32[]{:S(2)}, u32[]{:S(2)}) collective-permute-start(bf16[9,64,512]{2,1,0:T(8,128)(2,1)} %get-tuple-element.341), channel_id=1, source_target_pairs={{0,8},{8,0},{16,24},{24,16},{1,9},{9,1},{17,25},{25,17},{2,10},{10... | collective-permute-start | bytes 1769480 | tf_op jit(solution)/shard_map/ppermute | solution.py:24
  410.3 35.0 %collective-permute-start.45 = (f32[513,150]{0,1:T(8,128)}, f32[513,150]{0,1:T(8,128)}, u32[]{:S(2)}, u32[]{:S(2)}) collective-permute-start(f32[513,150]{0,1:T(8,128)} %add.561), channel_id=1, source_target_pairs={{0,4},{2,6},{4,0},{6,2},{1,5},{3,7},{5,1},{7,3},{8,12},{10,14},{12... | collective-permute-start | bytes 923408 | tf_op jit(solution)/shard_map/ppermute | solution.py:24
  440.7 155.0 %all-reduce.2.cloned.1.call-start = ((), (), s32[]{:S(2)}) async-start(), calls=%async_computation.4 | async-start | bytes 2097152 | tf_op jit(solution)/shard_map/psum | solution.py:862
  448.3 40.0 %collective-permute-start.46 = (bf16[9,128,512]{2,1,0:T(8,128)(2,1)}, bf16[9,128,512]{2,1,0:T(8,128)(2,1)}, u32[]{:S(2)}, u32[]{:S(2)}) collective-permute-start(bf16[9,128,512]{2,1,0:T(8,128)(2,1)} %pad_maximum_fusion.27), channel_id=1, source_target_pairs={{0,8},{8,0},{16,24},{24,16},{1,9},{9,1},{17,25},{25,17},{2,10},{10... | collective-permute-start | bytes 3538952 | tf_op jit(solution)/shard_map/ppermute | solution.py:24
  450.9 37.5 %collective-permute-start.47 = (bf16[9,128,512]{2,1,0:T(8,128)(2,1)}, bf16[9,128,512]{2,1,0:T(8,128)(2,1)}, u32[]{:S(2)}, u32[]{:S(2)}) collective-permute-start(bf16[9,128,512]{2,1,0:T(8,128)(2,1)} %pad_maximum_fusion.28), channel_id=1, source_target_pairs={{0,16},{8,24},{16,0},{24,8},{1,17},{9,25},{17,1},{25,9},{2,18},{10... | collective-permute-start | bytes 3538952 | tf_op jit(solution)/shard_map/ppermute | solution.py:24
  453.5 34.8 %collective-permute-start.48 = (f32[513,150]{0,1:T(8,128)}, f32[513,150]{0,1:T(8,128)}, u32[]{:S(2)}, u32[]{:S(2)}) collective-permute-start(f32[513,150]{0,1:T(8,128)} %add.562), channel_id=1, source_target_pairs={{0,8},{8,0},{16,24},{24,16},{1,9},{9,1},{17,25},{25,17},{2,10},{10... | collective-permute-start | bytes 923408 | tf_op jit(solution)/shard_map/ppermute | solution.py:24
  457.8 73.6 %collective-permute-start.54 = (bf16[9,128,512]{2,1,0:T(8,128)(2,1)}, bf16[9,128,512]{2,1,0:T(8,128)(2,1)}, u32[]{:S(2)}, u32[]{:S(2)}) collective-permute-start(bf16[9,128,512]{2,1,0:T(8,128)(2,1)} %pad_maximum_fusion.29), channel_id=1, source_target_pairs={{0,4},{2,6},{4,0},{6,2},{1,5},{3,7},{5,1},{7,3},{8,12},{10,14},{12... | collective-permute-start | bytes 3538952 | tf_op jit(solution)/shard_map/ppermute | solution.py:24
  476.3 8.1 %collective-permute-start.49 = (f32[8,64]{0,1:T(8,128)S(1)}, f32[8,64]{0,1:T(8,128)S(1)}, u32[]{:S(2)}, u32[]{:S(2)}) collective-permute-start(f32[8,64]{0,1:T(8,128)S(1)} %copy.204), channel_id=1, source_target_pairs={{0,8},{8,0},{16,24},{24,16},{1,9},{9,1},{17,25},{25,17},{2,10},{10... | collective-permute-start | bytes 6152 | tf_op jit(solution)/shard_map/ppermute | solution.py:24
  484.4 3.9 collective-permute-start.50
  491.5 5.3 collective-permute-start.51
  491.5 39.9 %collective-permute-start.52 = (bf16[9,64,512]{2,1,0:T(8,128)(2,1)}, bf16[9,64,512]{2,1,0:T(8,128)(2,1)S(1)}, u32[]{:S(2)}, u32[]{:S(2)}) collective-permute-start(bf16[9,64,512]{2,1,0:T(8,128)(2,1)} %get-tuple-element.184), channel_id=1, source_target_pairs={{0,16},{8,24},{16,0},{24,8},{1,17},{9,25},{17,1},{25,9},{2,18},{10... | collective-permute-start | bytes 1769480 | tf_op jit(solution)/shard_map/ppermute | solution.py:24
  492.3 39.1 %collective-permute-start.53 = (bf16[9,64,512]{2,1,0:T(8,128)(2,1)}, bf16[9,64,512]{2,1,0:T(8,128)(2,1)}, u32[]{:S(2)}, u32[]{:S(2)}) collective-permute-start(bf16[9,64,512]{2,1,0:T(8,128)(2,1)} %get-tuple-element.185), channel_id=1, source_target_pairs={{0,8},{8,0},{16,24},{24,16},{1,9},{9,1},{17,25},{25,17},{2,10},{10... | collective-permute-start | bytes 1769480 | tf_op jit(solution)/shard_map/ppermute | solution.py:24
  494.9 36.6 %collective-permute-start.55 = (f32[513,150]{0,1:T(8,128)S(1)}, f32[513,150]{0,1:T(8,128)}, u32[]{:S(2)}, u32[]{:S(2)}) collective-permute-start(f32[513,150]{0,1:T(8,128)S(1)} %add.582), channel_id=1, source_target_pairs={{0,16},{8,24},{16,0},{24,8},{1,17},{9,25},{17,1},{25,9},{2,18},{10... | collective-permute-start | bytes 923408 | tf_op jit(solution)/shard_map/ppermute | solution.py:24
  534.4 20.4 %collective-permute-start.56 = (bf16[9,64,512]{2,1,0:T(8,128)(2,1)S(1)}, bf16[9,64,512]{2,1,0:T(8,128)(2,1)S(1)}, u32[]{:S(2)}, u32[]{:S(2)}) collective-permute-start(bf16[9,64,512]{2,1,0:T(8,128)(2,1)S(1)} %get-tuple-element.328), channel_id=1, source_target_pairs={{0,8},{8,0},{16,24},{24,16},{1,9},{9,1},{17,25},{25,17},{2,10},{10... | collective-permute-start | bytes 1769480 | tf_op jit(solution)/shard_map/ppermute | solution.py:24
  534.5 20.4 %collective-permute-start.57 = (bf16[9,64,512]{2,1,0:T(8,128)(2,1)S(1)}, bf16[9,64,512]{2,1,0:T(8,128)(2,1)}, u32[]{:S(2)}, u32[]{:S(2)}) collective-permute-start(bf16[9,64,512]{2,1,0:T(8,128)(2,1)S(1)} %get-tuple-element.327), channel_id=1, source_target_pairs={{0,16},{8,24},{16,0},{24,8},{1,17},{9,25},{17,1},{25,9},{2,18},{10... | collective-permute-start | bytes 1769480 | tf_op jit(solution)/shard_map/ppermute | solution.py:24
  557.7 3.6 collective-permute-start.58
  559.1 37.0 %collective-permute-start.59 = (bf16[9,128,512]{2,1,0:T(8,128)(2,1)}, bf16[9,128,512]{2,1,0:T(8,128)(2,1)S(1)}, u32[]{:S(2)}, u32[]{:S(2)}) collective-permute-start(bf16[9,128,512]{2,1,0:T(8,128)(2,1)} %get-tuple-element.196), channel_id=1, source_target_pairs={{0,16},{8,24},{16,0},{24,8},{1,17},{9,25},{17,1},{25,9},{2,18},{10... | collective-permute-start | bytes 3538952 | tf_op jit(solution)/shard_map/ppermute | solution.py:24
  560.5 36.8 %collective-permute-start.60 = (bf16[9,128,512]{2,1,0:T(8,128)(2,1)}, bf16[9,128,512]{2,1,0:T(8,128)(2,1)}, u32[]{:S(2)}, u32[]{:S(2)}) collective-permute-start(bf16[9,128,512]{2,1,0:T(8,128)(2,1)} %get-tuple-element.197), channel_id=1, source_target_pairs={{0,8},{8,0},{16,24},{24,16},{1,9},{9,1},{17,25},{25,17},{2,10},{10... | collective-permute-start | bytes 3538952 | tf_op jit(solution)/shard_map/ppermute | solution.py:24
  (145 other events, 1725.3 us)
Sparse Core Ops, SparseCore 0:
  43.3 32.0 reduce-scatter.9
  331.8 32.5 reduce-scatter.7
  440.8 33.9 reduce-scatter.11
  531.5 64.1 all-reduce.1

commit v3 on v2

--- a/solution.py
+++ b/solution.py
@@ -233,6 +233,84 @@
     )(wide, *weight, keeps, *extra)
 
 
+def weight_slot(sides, wides, marker=None):
+    _, cells, block = sides.shape
+    mid = wides.shape[1] // 3
+
+    def body(side_ref, wide_ref, *rest):
+        o_ref = rest[-1]
+        terms = lax.dot_general(
+            side_ref[0], wide_ref[...], contract_first, preferred_element_type=f32
+        )
+        for j in range(3):
+            o_ref[j] = terms[:, j * mid : (j + 1) * mid].astype(bf16)
+
+    extra = [] if marker is None else [marker]
+    return pl.pallas_call(
+        body,
+        grid=(3,),
+        in_specs=[
+            pl.BlockSpec((1, cells, block), lambda a: (a, 0, 0)),
+            pl.BlockSpec((cells, 3 * mid), lambda a: (0, 0), pipeline_mode=pl.Buffered(1)),
+        ]
+        + [pl.BlockSpec(memory_space=pl.ANY)] * len(extra),
+        out_specs=pl.BlockSpec((3, block, mid), lambda a: (a, 0, 0)),
+        out_shape=jax.ShapeDtypeStruct((9, block, mid), bf16),
+        compiler_params=pltpu.CompilerParams(vmem_limit_bytes=52 << 20),
+        cost_estimate=small_cost,
+    )(sides, wides, *extra)
+
+
+def weight_sums(sides, wides, marker=None):
+    _, cells, _ = sides.shape
+    mid = wides.shape[1] // 3
+    if cells * mid <= 3072 * 512:
+        return weight_slot(sides, wides, marker)
+    return jnp.stack(
+        [
+            dot(sides[a], wides[:, j * mid : (j + 1) * mid], contract_first).astype(bf16)
+            for a in range(3)
+            for j in range(3)
+        ]
+    )
+
+
+def pool_back(grads, projections, limits, shares, pooled, joined):
+    scales, wide, deep = projections.shape
+    cells, bins = pooled.shape
+    _, more = grads.shape
+    block = wide // 4
+
+    def body(grad_ref, w_ref, share_ref, pool_ref, join_ref, o_ref):
+        lane = lax.broadcasted_iota(jnp.int32, (deep, more), 1)
+        grad = grad_ref[...].astype(f32)
+        total = 0.0
+        for s in range(scales):
+            inside = (lane >= limits[s]) & (lane < limits[s + 1])
+            part = jnp.where(inside, grad, 0.0).astype(bf16)
+            total = total + jnp.dot(w_ref[s], part, preferred_element_type=f32)
+        value = (total[:, :bins] * share_ref[...]).astype(bf16)
+        o_ref[...] = join_ref[...].astype(f32) + lax.dot_general(
+            pool_ref[...], value, contract_last, preferred_element_type=f32
+        )
+
+    return pl.pallas_call(
+        body,
+        grid=(4,),
+        in_specs=[
+            pl.BlockSpec((deep, more), lambda c: (0, 0)),
+            pl.BlockSpec((scales, block, deep), lambda c: (0, c, 0)),
+            pl.BlockSpec((1, bins), lambda c: (0, 0)),
+            pl.BlockSpec((cells, bins), lambda c: (0, 0)),
+            pl.BlockSpec((cells, block), lambda c: (0, c)),
+        ],
+        out_specs=pl.BlockSpec((cells, block), lambda c: (0, c)),
+        out_shape=jax.ShapeDtypeStruct((cells, wide), f32),
+        compiler_params=pltpu.CompilerParams(vmem_limit_bytes=40 << 20),
+        cost_estimate=small_cost,
+    )(grads, projections, shares, pooled, joined)
+
+
 def silu_slope(value):
     sigmoid_value = jax.nn.sigmoid(value)
     return sigmoid_value * (1.0 + value * (1.0 - sigmoid_value))
@@ -380,13 +458,23 @@
 
     def gathered(self, got):
         half = self.half
+        own, near = self.own, self.next
         parts = [
-            (self.own[0], self.own[1]),
-            (self.next[0], got[1][:, :half]),
-            (got[0][:, :half], self.next[1]),
-            (got[0][:, half:], got[1][:, half:]),
+            (0, 0, own[0]),
+            (0, 1, own[1]),
+            (1, 0, near[0]),
+            (2, 1, near[1]),
+            (2, 0, got[0][:, :half]),
+            (3, 0, got[0][:, half:]),
+            (1, 1, got[1][:, :half]),
+            (3, 1, got[1][:, half:]),
         ]
-        return place_images([jnp.concatenate(part, axis=1) for part in parts], f32)
+        taps, _, mid = self.x.shape
+        whole = jnp.zeros((taps, 8 * half, mid), f32)
+        for j, side, part in parts:
+            at = (self.me ^ j) * 2 * half + side * half
+            whole = lax.dynamic_update_slice_in_dim(whole, part.astype(f32), at, 1)
+        return whole
 
 
 def join_cols(mine, others, axis):
@@ -633,11 +721,15 @@
             got, hold = weight_phase(more=more, hold=[hidden_strip])
             if got:
                 feature_exts[step] = got[0]
-            (hidden_strip,) = weight_plan(hold)
+            if len(weights) == row_count - 2:
+                hidden_strip, mean_moves = weight_plan(hold + [local_means.astype(bf16)])
+            else:
+                (hidden_strip,) = weight_plan(hold)
         hidden_strip = conv_slot(cat_wide, slot, weights[slot], keeps, hidden_strip, width)
     for step in range(1, depth):
         if step not in feature_exts:
             feature_exts[step] = swap(sends[step - 1], "row", step)
+    own_means = lax.psum_scatter(mean_moves, ("row", "col"), scatter_dimension=1, tiled=True)
     hidden_strip = hidden_strip.reshape(tile_h, width, mid)
 
     def cells_of(step):
@@ -668,40 +760,6 @@
         jnp.stack([jnp.sum(grad_before * normed_mid, axis=0), jnp.sum(grad_before, axis=0)]),
         everywhere,
     )
-    conv_gain_grad, conv_bias_grad = mid_grads[0], mid_grads[1]
-    background = ("col", "row", "img")
-    class_chain = Chain(
-        jnp.concatenate(
-            [
-                dot(act_mid, grad_logits, contract_first),
-                jnp.sum(grad_logits.astype(f32), axis=0, keepdims=True),
-            ],
-            axis=0,
-        ),
-        background,
-    )
-    grad_hidden = (
-        conv_gain
-        * inverse_mid
-        * (grad_before - conv_bias_grad / all_cells - normed_mid * conv_gain_grad / all_cells)
-    ).astype(bf16)
-
-    def pair_strip(mine):
-        return [swap(mine, "col", step) for step in range(1, col_count)]
-
-    grad_hidden, mean_moves = tie(grad_hidden, local_means.astype(bf16))
-    own_means = lax.psum_scatter(mean_moves, ("row", "col"), scatter_dimension=1, tiled=True)
-    grad_tile = grad_hidden.reshape(tile_h, tile_w, mid)
-    hops = [swap(grad_tile, "row", step) for step in range(1, depth)]
-    grad_ext = row_halo(grad_tile)
-    grad_ext = join_cols(grad_ext, pair_strip(grad_ext), 1)
-    grad_strip = grad_ext[1:-1]
-    grad_ext = grad_ext.reshape(1, ext_cells, mid)
-    own_wide = shifted(grad_ext, canvas_box, top - 1, width, reverse=True)[0]
-
-    def input_grads(slot, marker=None):
-        return grad_slot(own_wide, weights[slot], keeps, width, marker)
-
     low_zero = jnp.zeros((), bf16)
     lower_half = row < depth
     up_exts = [choose([ups[r] for r in range(depth)], place)] + [
@@ -728,8 +786,42 @@
             lines.append(jnp.concatenate(pieces, axis=0))
         sides.append(lines)
 
-    def phase(flights, hold=()):
-        sent = class_chain.send()
+    mid_grads, home_side, *lines = tie(mid_grads, jnp.stack(sides[1]), *sides[0])
+    sides = [lines]
+    conv_gain_grad, conv_bias_grad = mid_grads[0], mid_grads[1]
+    background = ("img", "row", "col")
+    class_chain = Chain(
+        jnp.concatenate(
+            [
+                dot(act_mid, grad_logits, contract_first),
+                jnp.sum(grad_logits.astype(f32), axis=0, keepdims=True),
+            ],
+            axis=0,
+        ),
+        background,
+    )
+    grad_hidden = (
+        conv_gain
+        * inverse_mid
+        * (grad_before - conv_bias_grad / all_cells - normed_mid * conv_gain_grad / all_cells)
+    ).astype(bf16)
+
+    def pair_strip(mine):
+        return [swap(mine, "col", step) for step in range(1, col_count)]
+
+    grad_tile = grad_hidden.reshape(tile_h, tile_w, mid)
+    hops = [swap(grad_tile, "row", step) for step in range(1, depth)]
+    grad_ext = row_halo(grad_tile)
+    grad_ext = join_cols(grad_ext, pair_strip(grad_ext), 1)
+    grad_strip = grad_ext[1:-1]
+    grad_ext = grad_ext.reshape(1, ext_cells, mid)
+    own_wide = shifted(grad_ext, canvas_box, top - 1, width, reverse=True)[0]
+
+    def input_grads(slot, marker=None):
+        return grad_slot(own_wide, weights[slot], keeps, width, marker)
+
+    def phase(flights, hold=(), chain=True):
+        sent = class_chain.send() if chain else []
         got = tie(*flights, *sent, *hold)
         class_chain.receive(got[len(flights) : len(flights) + len(sent)])
         return got[: len(flights)], got[len(flights) + len(sent) :]
@@ -739,9 +831,10 @@
         places=jnp.zeros((1,), jnp.int32), out_blocks=depth,
     )
     held = [input_grads(slot) for slot in range(depth)]
-    hops, held = phase(hops, held + [wides, *sides[0], *sides[1]])
+    hops += [swap(own_means, "img", 1), swap(own_means, "img", 2)]
+    hops, held = phase(hops, held + [wides])
+    *hops, means_one, means_two = hops
     cat_grads, wides = held[:depth], held[depth]
-    sides = [held[depth + 1 : depth + 4], held[depth + 4 :]]
     for k, tile_there in enumerate(hops):
         strip = join_cols(tile_there, pair_strip(tile_there), 1)
         wides = shifted(
@@ -761,14 +854,28 @@
             ]
         )
 
+    class_sent = class_chain.send()
     away = ImageSum(weight_grads(0))
-    sends, marker = mark(*away.first_sends())
+    (*sends, class_got), marker = mark(*away.first_sends(), *class_sent)
+    class_chain.receive([class_got])
     flights = away.first(sends)
+    flights.append(swap(means_one, "img", 2))
+    home = weight_sums(home_side, wides, marker)
+    got, (home,) = phase(flights, [home])
+    home = ImageSum(home)
+    means = [own_means, means_one, means_two, got.pop()]
+    sends, marker = mark(*away.second_sends(got))
+    flights = away.second(sends)
     held = [input_grads(slot, marker) for slot in range(depth, row_count)]
-    got, held = phase(flights, held + [own_means, wides])
-    cat_grads += held[:-2]
-    own_means, wides = held[-2:]
-    flights = away.second(away.second_sends(got))
+    got, held = phase(flights, held)
+    cat_grads += held
+    *sends, far_own, far_next = tie(*home.first_sends(), *away.reduced(got))
+    got, (far_next,) = phase(
+        home.first(sends) + [swap(far_own, "row", depth)], [far_next]
+    )
+    crossed = [got.pop()]
+    sends, second_mark = mark(*home.second_sends(got))
+    flights = home.second(sends) + [swap(far_next, "row", depth)]
     by_row = [choose(cat_grads, row ^ r) for r in range(row_count)]
     spread_strip = lax.slice_in_dim(spread_ext, width, width + strip_cells, axis=1)
     grad_bins_local = jnp.zeros((branch_width, bins), f32)
@@ -780,20 +887,13 @@
         at = lax.rem(first, branch_width)
         old = lax.dynamic_slice_in_dim(grad_bins_local, at, block, 0)
         grad_bins_local = lax.dynamic_update_slice_in_dim(grad_bins_local, old + terms, at, 0)
-    wides, grad_bins_local = tie(wides, grad_bins_local)
-    got, (home,) = phase(flights, [weight_grads(1)])
-    home = ImageSum(home)
-    crossing = [swap(jnp.concatenate(away.reduced(got), axis=1), "row", depth)]
     grad_bins = lax.psum_scatter(
-        grad_bins_local, ("row", "col"), scatter_dimension=0, tiled=True
-    )
-    grad_act = grad_bins * silu_slope(before)
+        grad_bins_local.astype(bf16), ("row", "col"), scatter_dimension=0, tiled=True
+    ).astype(f32)
+    grad_act = (grad_bins + second_mark[0, 0]) * silu_slope(before)
     branch_sums = butterfly(
         jnp.concatenate([by_scale(grad_act * normed), by_scale(grad_act)], axis=0), ("img",)
     )
-    got, (branch_sums,) = phase(home.first(home.first_sends()), [branch_sums])
-    sends, second_mark = mark(*home.second_sends(got))
-    flights = home.second(sends)
     grad_pre = (
         gain_part
         * inverse_bins
@@ -803,39 +903,6 @@
             - normed * to_bins(branch_sums[:4] / counts)
         )
     ).astype(bf16)
-    got, _ = phase(flights + crossing)
-    home_own = home.reduced(got[:2])
-    crossed = [got[2][:, : home.half], got[2][:, home.half :]]
-    home_own = [add_low(a, b) for a, b in zip(home_own, crossed)]
-    got, _ = phase(home.third(home_own))
-    sends, fourth_mark = mark(*home.fourth_sends(got))
-    got = home.fourth(sends)
-    while class_chain.todo:
-        phase([])
-    class_w_grad, class_bias_grad = class_chain.value[:mid], class_chain.value[mid]
-    gathered = lax.all_gather(
-        jnp.concatenate([grad_pre.astype(f32), branch_sums.T], axis=1) + second_mark[0, 0],
-        ("row", "col"), axis=0, tiled=True,
-    )
-    grad_pre = gathered[:, :bins].astype(bf16)
-    branch_all = gathered[:, bins:].T
-    branch_gain_grad, branch_bias_grad = branch_all[:4], branch_all[4:]
-
-    late_pre = (gathered[:, :bins] + fourth_mark[0, 0]).astype(bf16)
-    weight_terms, bin_grads = [], []
-    for position in range(4):
-        span = slice(limits[position], limits[position + 1])
-        weight_terms.append(
-            dot(own_means[span], grad_pre[:, span], (((0,), (1,)), ((), ())))
-        )
-        bin_grads.append(
-            dot(
-                late_pre[:, span], branch_projection_weight[position], (((0,), (1,)), ((), ()))
-            )
-        )
-    bin_grads = (jnp.concatenate(bin_grads, axis=0) / sizes[:, None]).astype(bf16)
-    grad_pool = dot(pooling, bin_grads, contract_first)
-
     own_features = [
         by_row[r].reshape(tile_h, width, block) for r in range(feature_rows)
     ]
@@ -857,11 +924,44 @@
     joined = jnp.concatenate(
         [by_block[c][r] for r in range(feature_rows) for c in range(col_count)], axis=1
     )
-    feature_grad = (joined.astype(f32) + grad_pool).reshape(1, tile_h, tile_w, channels_in)
-
-    branch_w_grad = lax.psum(jnp.stack(weight_terms).astype(bf16), "img")
-    branch_w_grad, *got = tie(branch_w_grad, *got)
-    branch_w_grad = branch_w_grad.astype(f32)
+    by_scales = jnp.asarray(table[:, 0][None, :] == np.arange(4)[:, None], bf16)
+    means = [
+        jnp.concatenate([part * line[:, None] for line in by_scales], axis=1) for part in means
+    ]
+    sums = branch_sums.T
+    high = sums.astype(bf16)
+    middle = (sums - high.astype(f32)).astype(bf16)
+    low = (sums - high.astype(f32) - middle.astype(f32)).astype(bf16)
+    piece = jnp.concatenate([grad_pre, high, middle, low], axis=1)
+    flights += [swap(piece, "img", 1), swap(piece, "img", 2)]
+    pooled = jnp.transpose(pooling)
+    got, (joined, pooled, *means) = phase(flights, [joined, pooled, *means], chain=False)
+    *got, piece_one, piece_two = got
+    home_own = home.reduced(got[:2])
+    crossed.append(got[2])
+    home_own = [add_low(a, b) for a, b in zip(home_own, crossed)]
+    got, _ = phase(home.third(home_own) + [swap(piece_one, "img", 2)])
+    packed = jnp.stack([piece, piece_one, piece_two, got.pop()])
+    sends = home.fourth_sends(got)
+    sends, fourth_mark = mark(*sends, *home.own, *home.next)
+    home.own, home.next = sends[2:4], sends[4:]
+    got = home.fourth(sends)
+    while class_chain.todo:
+        phase([])
+    class_w_grad, class_bias_grad = class_chain.value[:mid], class_chain.value[mid]
+    gathered = lax.all_gather(
+        packed + fourth_mark[0, 0].astype(bf16), ("row", "col"), axis=1, tiled=True
+    )
+    ends = gathered[0, :, bins:].astype(f32)
+    branch_all = (ends[:, :8] + ends[:, 8:16] + ends[:, 16:]).T
+    branch_gain_grad, branch_bias_grad = branch_all[:4], branch_all[4:]
+    branch_w_grad = sum(
+        dot(means[k], gathered[k, :, :bins], (((0,), (1,)), ((), ()))) for k in range(images)
+    ).reshape(4, -1, branch_width)
+    feature_grad = pool_back(
+        gathered[0], branch_projection_weight, limits, 1.0 / sizes[None], pooled, joined
+    ).reshape(1, tile_h, tile_w, channels_in)
+    feature_grad, *got = tie(feature_grad, *got)
     conv_w_grad = home.gathered(got)
     conv_w_grad = jnp.transpose(conv_w_grad, (1, 0, 2))
     return (

time: 624 us -> 613 us (0.982)
  Pallas kernels: 112 us -> 143 us
  blocking collectives: 55.7 us -> 25.1 us
  matrix products: 80.6 us -> 53.1 us
  local copies, waits for them, and re-layouts: 79.8 us -> 61.8 us
  waiting for transfers between devices: 101 us -> 116 us
  other arithmetic: 101 us -> 112 us
  starting transfers between devices: 67.9 us -> 75.5 us
    ppermute x51 -> x59, waiting for transfers between devices: 50.1 us -> 88.9 us  [swap(): return lax.ppermute(value, axis, [(i, i ^ step) for i in range(count)])]
    all_gather x1 -> x0, blocking collectives: 30.7 us -> none  [on_device(): lax.all_gather(jnp.concatenate([grad_pre.astype(f32), branch_sums.T], axi...]
    pallas_call x0 -> x2, Pallas kernels: none -> 30.1 us  [the longest x1 21 us: weight_slot(): pl.pallas_call(body, grid=(3,), in_specs=[pl.BlockSpec((1, cells, block),...]
    dot_general x40 -> x26, matrix products: 80.6 us -> 53.1 us  [dot(): return lax.dot_general(a, b, dims, preferred_element_type=f32)]
    psum x1 -> x0, waiting for transfers between devices: 23.8 us -> none  [on_device(): branch_w_grad = lax.psum(jnp.stack(weight_terms).astype(bf16), 'img')]
    reduce_scatter x1 -> x2, waiting for transfers between devices: 13.9 us -> 0.01 us  [the longest x1 0.01 us: on_device(): lax.psum_scatter(pre_local, ('row', 'col'), scatter_dimension=0, tiled=True)]
    unnamed x293 -> x313, local copies, waits for them, and re-layouts: 32.3 us -> 18.7 us
    all_gather x0 -> x1, waiting for transfers between devices: none -> 10.9 us  [on_device(): lax.all_gather(packed + fourth_mark[0, 0].astype(bf16), ('row', 'col'), a...]
  transfers between devices with their start and end apart: 65 -> 73, of which waited for: 27 -> 23; matrix products, arithmetic and copies ran while one was open for 32% -> 28% of each run, Pallas kernels for 16% -> 22%
where the time goes in v3:
time: 613 us; the launch traced here: 603 us
  Pallas kernels  143 us (23%)
  waiting for transfers between devices  116 us (19%)
  other arithmetic  112 us (18%)
  starting transfers between devices  75.5 us (12%)
  local copies, waits for them, and re-layouts  61.8 us (10%)
  matrix products  53.1 us (9%)
  blocking collectives  25.1 us (4%)
  between operations  17.2 us (3%)
    ppermute x59, waiting for transfers between devices, swap(): return lax.ppermute(value, axis, [(i, i ^ step) for i in range(count)])  88.9 us
    dot_general x26, matrix products, dot(): return lax.dot_general(a, b, dims, preferred_element_type=f32)  53.1 us
    ppermute x59, starting transfers between devices, swap(): return lax.ppermute(value, axis, [(i, i ^ step) for i in range(count)])  48.7 us
    pallas_call x4, Pallas kernels, conv_slot(): pl.pallas_call(body, grid=(cells // chunk,), in_specs=[pl.BlockSpec((1, e...  46.5 us
    pallas_call x5, Pallas kernels, shifted(): pl.pallas_call(body, grid_spec=pltpu.PrefetchScalarGridSpec(num_scalar_pr...  34 us
    pallas_call x4, Pallas kernels, grad_slot(): pl.pallas_call(body, grid=(cells // chunk,), in_specs=[pl.BlockSpec((ext,...  32.2 us
    all_gather x1, blocking collectives, on_device(): lax.all_gather((jax.nn.silu(before) + waiting['mark'][0, 0]).astype(bf16)...  25.1 us
    pallas_call x1, Pallas kernels, weight_slot(): pl.pallas_call(body, grid=(3,), in_specs=[pl.BlockSpec((1, cells, block),...  21 us
  transfers between devices with their start and end apart: 73, of which 23 were waited for; matrix products, arithmetic and copies ran while one was open for 28% of the time, Pallas kernels for 22%

profile of v3, /device:TPU:0, one launch (start us, length us, event | category | flops | bytes accessed | tf_op | source)
XLA Modules:
  0.0 603.1 jit_solution(17595254356452776983)
XLA Ops:
  7.4 2.4 dynamic-slice_bitcast_fusion.2
  9.8 6.0 collective-permute-start
  20.0 5.8 collective-permute-start.2
  26.5 3.9 divide_convert_fusion
  30.5 3.5 fusion.75
  34.0 2.5 fusion.152
  36.6 2.5 fusion.155
  39.1 2.5 fusion.158
  43.6 4.6 collective-permute-done.3
  57.1 2.4 broadcast_select_fusion.12
  67.8 4.6 fusion.207
  72.7 9.0 %shard_map.375.rest_0_ = bf16[4,1664,1536]{2,1,0:T(8,128)(2,1)} custom-call(s32[2]{0:T(128)S(1)} %get-tuple-element.533.place_ref, s32[1]{0:T(128)} %bitcast.22.first_ref, s32[8,4]{1,0:T(8,128)S(1)} %copy.154.box_ref, bf16[2,1664,512]{2,1,0:T(8,128)(2,1)} %bitcast.276), custom_call_target="tpu_custom_call" | custom-call | flops 1024 | bytes 1024 | tf_op jit(solution)/shard_map/pallas_call | solution.py:129
  81.8 10.2 %collective-permute-done.8 = bf16[9,128,512]{2,1,0:T(8,128)(2,1)} collective-permute-done((bf16[9,128,512]{2,1,0:T(8,128)(2,1)}, bf16[9,128,512]{2,1,0:T(8,128)(2,1)}, u32[]{:S(2)}, u32[]{:S(2)}) %collective-permute-start.8) | collective-permute-done | bytes 1179680 | tf_op jit(solution)/shard_map/ppermute | solution.py:355
  103.9 2.2 pad_maximum_fusion.9
  112.6 25.1 %all_gather.6 = bf16[512,400]{1,0:T(8,128)(2,1)S(1)} all-gather(bf16[64,400]{1,0:T(8,128)(2,1)S(1)} %get-tuple-element.350), channel_id=1, replica_groups=mesh['img'=4,'row'=4,'col'=2] {'row','col'}, dimensions={0}, use_global_device_ids=true | all-gather | bytes 460800 | tf_op jit(solution)/shard_map/all_gather | solution.py:667
  137.7 2.8 convolution_convert_fusion.1
  140.6 2.8 convolution_convert_fusion.2
  145.4 9.5 %shard_map.376.x_ref = bf16[4,1664,1536]{2,1,0:T(8,128)(2,1)} custom-call(s32[2]{0:T(128)S(1)} %get-tuple-element.532.place_ref, s32[1]{0:T(128)} %bitcast.22.first_ref, s32[8,4]{1,0:T(8,128)S(1)} %copy.154.box_ref, bf16[2,1664,512]{2,1,0:T(8,128)(2,1)} %pad_maximum_fusion.3.x_ref, ...), custom_call_target="tpu_custom_call", output_to_operand_aliasing={{}: (4, {})} | custom-call | flops 1024 | bytes 1024 | tf_op jit(solution)/shard_map/pallas_call | solution.py:129
  167.9 10.3 %shard_map.377.rest_4_ = f32[1536,512]{1,0:T(8,128)S(1)} custom-call(bf16[4,1664,1536]{2,1,0:T(8,128)(2,1)} %shard_map.376.x_ref, bf16[3,512,512]{2,1,0:T(8,128)(2,1)S(1)} %copy-done.26, bf16[3,512,512]{2,1,0:T(8,128)(2,1)S(1)} %copy-done.24, bf16[3,512,512]{2,1,0:T(8,128)(2,1)S(1)} %copy-done.22, f32[3,1536,1]{2,1,0:T(8,128)S(1)} %add_convert_fusion.rest_3_), custom_call_target="tpu_custom_call" | custom-call | flops 1024 | bytes 1024 | tf_op jit(solution)/shard_map/pallas_call | solution.py:177
  182.2 12.1 %shard_map.378.rest_4_ = f32[1536,512]{1,0:T(8,128)S(1)} custom-call(bf16[4,1664,1536]{2,1,0:T(8,128)(2,1)} %shard_map.376.x_ref, bf16[3,512,512]{2,1,0:T(8,128)(2,1)S(1)} %get-tuple-element.442.rest_0_, bf16[3,512,512]{2,1,0:T(8,128)(2,1)S(1)} %get-tuple-element.441.rest_1_, ...), custom_call_target="tpu_custom_call", output_to_operand_aliasing={{}: (5, {})} | custom-call | flops 1024 | bytes 1024 | tf_op jit(solution)/shard_map/pallas_call | solution.py:177
  196.2 8.3 %collective-permute-done.18 = bf16[1664,512]{1,0:T(8,128)(2,1)} collective-permute-done((bf16[1664,512]{1,0:T(8,128)(2,1)}, bf16[1664,512]{1,0:T(8,128)(2,1)}, u32[]{:S(2)}, u32[]{:S(2)}) %collective-permute-start.18) | collective-permute-done | bytes 1703968 | tf_op jit(solution)/shard_map/ppermute | solution.py:24
  208.8 12.1 %shard_map.379.rest_4_ = f32[1536,512]{1,0:T(8,128)S(1)} custom-call(bf16[4,1664,1536]{2,1,0:T(8,128)(2,1)} %shard_map.376.x_ref, bf16[3,512,512]{2,1,0:T(8,128)(2,1)S(1)} %get-tuple-element.433.rest_0_, bf16[3,512,512]{2,1,0:T(8,128)(2,1)S(1)} %get-tuple-element.432.rest_1_, ...), custom_call_target="tpu_custom_call", output_to_operand_aliasing={{}: (5, {})} | custom-call | flops 1024 | bytes 1024 | tf_op jit(solution)/shard_map/pallas_call | solution.py:177
  221.5 12.1 %shard_map.380 = f32[1536,512]{1,0:T(8,128)S(1)} custom-call(bf16[4,1664,1536]{2,1,0:T(8,128)(2,1)} %shard_map.376.x_ref, bf16[3,512,512]{2,1,0:T(8,128)(2,1)S(1)} %get-tuple-element.430.rest_0_, bf16[3,512,512]{2,1,0:T(8,128)(2,1)S(1)} %get-tuple-element.429.rest_1_, ...), custom_call_target="tpu_custom_call", output_to_operand_aliasing={{}: (5, {})} | custom-call | flops 1024 | bytes 1024 | tf_op jit(solution)/shard_map/pallas_call | solution.py:177
  233.9 4.0 convolution_convert_fusion
  240.3 4.2 slice_select_fusion.7
  246.1 2.2 broadcast_select_fusion.1
  252.2 3.6 collective-permute-done.25
  256.2 4.1 collective-permute-done.26
  266.1 4.5 pad_maximum_fusion.side_ref
  280.1 2.3 collective-permute-done.31
  286.3 4.5 collective-permute-start.36
  294.6 2.3 collective-permute-start.32
  298.8 2.4 broadcast_select_fusion.14
  304.5 5.2 shard_map.381
  309.8 2.4 copy-done.2
  312.2 8.0 %shard_map.382 = bf16[1536,512]{1,0:T(8,128)(2,1)S(1)} custom-call(bf16[1664,1536]{1,0:T(8,128)(2,1)S(1)} %bitcast.254, bf16[3,512,512]{2,1,0:T(8,128)(2,1)S(1)} %copy-done.27, bf16[3,512,512]{2,1,0:T(8,128)(2,1)S(1)} %copy-done.25, bf16[3,512,512]{2,1,0:T(8,128)(2,1)S(1)} %copy-done.23, f32[3,1536,1]{2,1,0:T(8,128)S(1)} %add_convert_fusion.rest_3_), custom_call_target="tpu_custom_call" | custom-call | flops 1024 | bytes 1024 | tf_op jit(solution)/shard_map/pallas_call | solution.py:220
  320.3 8.0 %shard_map.383 = bf16[1536,512]{1,0:T(8,128)(2,1)S(1)} custom-call(bf16[1664,1536]{1,0:T(8,128)(2,1)S(1)} %bitcast.255, bf16[3,512,512]{2,1,0:T(8,128)(2,1)S(1)} %copy-done.17, bf16[3,512,512]{2,1,0:T(8,128)(2,1)S(1)} %copy-done.21, bf16[3,512,512]{2,1,0:T(8,128)(2,1)S(1)} %copy-done.19, f32[3,1536,1]{2,1,0:T(8,128)S(1)} %add_convert_fusion.rest_3_), custom_call_target="tpu_custom_call" | custom-call | flops 1024 | bytes 1024 | tf_op jit(solution)/shard_map/pallas_call | solution.py:220
  329.5 4.9 shard_map.384.rest_0_
  338.8 5.3 shard_map.385
  344.1 3.9 fusion.141
  370.9 3.6 multiply_convert_fusion.1
  376.6 21.0 %shard_map.386 = bf16[9,512,512]{2,1,0:T(8,128)(2,1)} custom-call(bf16[3,3072,512]{2,1,0:T(8,128)(2,1)} %pad_maximum_fusion.side_ref, bf16[3072,1536]{1,0:T(8,128)(2,1)} %bitcast.267, f32[8,128]{1,0:T(8,128)S(1)} %collective-permute-done.45.rest_0_), custom_call_target="tpu_custom_call" | custom-call | flops 1024 | bytes 1024 | tf_op jit(solution)/shard_map/pallas_call | solution.py:249
  397.6 3.3 collective-permute-done.43
  406.3 3.3 broadcast_multiply_fusion.15
  413.4 8.0 %shard_map.387 = bf16[1536,512]{1,0:T(8,128)(2,1)S(1)} custom-call(bf16[1664,1536]{1,0:T(8,128)(2,1)S(1)} %bitcast.258, bf16[3,512,512]{2,1,0:T(8,128)(2,1)S(1)} %copy-done.5, bf16[3,512,512]{2,1,0:T(8,128)(2,1)S(1)} %copy-done.15, bf16[3,512,512]{2,1,0:T(8,128)(2,1)S(1)} %copy-done.13, f32[3,1536,1]{2,1,0:T(8,128)S(1)} %add_convert_fusion.rest_3_, ...), custom_call_target="tpu_custom_call" | custom-call | flops 1024 | bytes 1024 | tf_op jit(solution)/shard_map/pallas_call | solution.py:220
  421.5 8.2 %shard_map.388 = bf16[1536,512]{1,0:T(8,128)(2,1)S(1)} custom-call(bf16[1664,1536]{1,0:T(8,128)(2,1)S(1)} %bitcast.259, bf16[3,512,512]{2,1,0:T(8,128)(2,1)S(1)} %copy-done.7, bf16[3,512,512]{2,1,0:T(8,128)(2,1)S(1)} %copy-done.11, bf16[3,512,512]{2,1,0:T(8,128)(2,1)S(1)} %copy-done.9, f32[3,1536,1]{2,1,0:T(8,128)S(1)} %add_convert_fusion.rest_3_, ...), custom_call_target="tpu_custom_call" | custom-call | flops 1024 | bytes 1024 | tf_op jit(solution)/shard_map/pallas_call | solution.py:220
  429.8 3.7 add_convert_fusion.9
  439.5 2.5 fusion.84
  442.0 2.5 select_select_fusion.1
  444.7 23.1 %collective-permute-done.52 = bf16[9,64,512]{2,1,0:T(8,128)(2,1)} collective-permute-done((bf16[9,64,512]{2,1,0:T(8,128)(2,1)}, bf16[9,64,512]{2,1,0:T(8,128)(2,1)}, u32[]{:S(2)}, u32[]{:S(2)}) %collective-permute-start.52) | collective-permute-done | bytes 589856 | tf_op jit(solution)/shard_map/ppermute | solution.py:24
  467.9 3.0 add_convert_fusion.7
  476.0 2.9 pad_maximum_fusion.28
  489.7 8.7 %collective-permute-done.60 = bf16[64,424]{1,0:T(8,128)(2,1)S(1)} collective-permute-done((bf16[64,424]{1,0:T(8,128)(2,1)S(1)}, bf16[64,424]{1,0:T(8,128)(2,1)S(1)}, u32[]{:S(2)}, u32[]{:S(2)}) %collective-permute-start.60) | collective-permute-done | bytes 54304 | tf_op jit(solution)/shard_map/ppermute | solution.py:24
  498.4 12.6 %collective-permute-done.59 = bf16[9,64,512]{2,1,0:T(8,128)(2,1)S(1)} collective-permute-done((bf16[9,64,512]{2,1,0:T(8,128)(2,1)S(1)}, bf16[9,64,512]{2,1,0:T(8,128)(2,1)S(1)}, u32[]{:S(2)}, u32[]{:S(2)}) %collective-permute-start.59) | collective-permute-done | bytes 589856 | tf_op jit(solution)/shard_map/ppermute | solution.py:24
  511.0 2.4 add_convert_fusion.1
  516.2 14.3 %collective-permute-done.65 = bf16[64,424]{1,0:T(8,128)(2,1)S(1)} collective-permute-done((bf16[64,424]{1,0:T(8,128)(2,1)S(1)}, bf16[64,424]{1,0:T(8,128)(2,1)S(1)}, u32[]{:S(2)}, u32[]{:S(2)}) %collective-permute-start.65) | collective-permute-done | bytes 54304 | tf_op jit(solution)/shard_map/ppermute | solution.py:24
  543.5 4.9 broadcast_in_dim.129
  553.2 10.9 %all-gather.2.cloned.1.call-done = bf16[4,512,424]{2,1,0:T(8,128)(2,1)} async-done(((bf16[4,64,424]{2,1,0:T(8,128)(2,1)}), bf16[4,512,424]{2,1,0:T(8,128)(2,1)}) %all-gather.2.cloned.1.call-update) | async-done | bytes 1736720 | tf_op jit(solution)/shard_map/all_gather | solution.py:952
  565.2 3.4 copy-done.28
  569.7 9.1 %shard_map.389 = f32[768,2048]{1,0:T(8,128)} custom-call(bf16[512,424]{1,0:T(8,128)(2,1)S(1)} %slice_bitcast_fusion.18.grad_ref, bf16[4,2048,512]{2,1,0:T(8,128)(2,1)S(1)} %copy-done.28, f32[1,400]{1,0:T(1,128)S(1)} %bitcast.265, bf16[768,400]{1,0:T(8,128)(2,1)S(1)} %copy-done.35, bf16[768,2048]{1,0:T(8,128)(2,1)S(1)} %pad_maximum_fusion.7.join_ref), custom_call_target="tpu_custom_call" | custom-call | flops 1024 | bytes 1024 | tf_op jit(solution)/shard_map/pallas_call | solution.py:297
  581.5 2.2 convert_dynamic-update-slice_fusion.3
  583.8 2.2 convert_dynamic-update-slice_fusion.2
  586.0 2.4 convert_dynamic-update-slice_fusion.1
  588.4 2.2 convert_dynamic-update-slice_fusion
  (653 shorter events, 196.3 us)
Async XLA Ops:
  7.3 74.5 %reduce-scatter.4.cloned.1.call-start = ((), (), s32[]{:S(2)}) async-start(), calls=%async_computation.3 | async-start | bytes 1179648 | tf_op jit(solution)/shard_map/reduce_scatter | solution.py:638
  9.8 44.1 %collective-permute-start = (bf16[9,128,512]{2,1,0:T(8,128)(2,1)}, bf16[9,128,512]{2,1,0:T(8,128)(2,1)}, u32[]{:S(2)}, u32[]{:S(2)}) collective-permute-start(bf16[9,128,512]{2,1,0:T(8,128)(2,1)} %dynamic-slice_bitcast_fusion.2), channel_id=1, source_target_pairs={{0,2},{2,4},{4,6},{1,3},{3,5},{5,7},{8,10},{10,12},{12,14},{9,11},... | collective-permute-start | bytes 3538952 | tf_op jit(solution)/shard_map/ppermute | solution.py:354
  15.8 38.1 %collective-permute-start.1 = (bf16[9,128,512]{2,1,0:T(8,128)(2,1)}, bf16[9,128,512]{2,1,0:T(8,128)(2,1)}, u32[]{:S(2)}, u32[]{:S(2)}) collective-permute-start(bf16[9,128,512]{2,1,0:T(8,128)(2,1)} %dynamic-slice_bitcast_fusion.2), channel_id=1, source_target_pairs={{2,0},{4,2},{6,4},{3,1},{5,3},{7,5},{10,8},{12,10},{14,12},{11,9},... | collective-permute-start | bytes 3538952 | tf_op jit(solution)/shard_map/ppermute | solution.py:355
  18.7 29.5 %collective-permute-start.3 = (bf16[1,32,2048]{2,1,0:T(8,128)(2,1)}, bf16[1,32,2048]{2,1,0:T(8,128)(2,1)}, u32[]{:S(2)}, u32[]{:S(2)}) collective-permute-start(bf16[1,32,2048]{2,1,0:T(8,128)(2,1)} %get-tuple-element.389), channel_id=1, source_target_pairs={{2,0},{4,2},{6,4},{3,1},{5,3},{7,5},{10,8},{12,10},{14,12},{11,9},... | collective-permute-start | bytes 393224 | tf_op jit(solution)/shard_map/ppermute | solution.py:489
  20.0 28.2 %collective-permute-start.2 = (bf16[1,32,2048]{2,1,0:T(8,128)(2,1)S(1)}, bf16[1,32,2048]{2,1,0:T(8,128)(2,1)}, u32[]{:S(2)}, u32[]{:S(2)}) collective-permute-start(bf16[1,32,2048]{2,1,0:T(8,128)(2,1)S(1)} %get-tuple-element.388), channel_id=1, source_target_pairs={{0,2},{2,4},{4,6},{1,3},{3,5},{5,7},{8,10},{10,12},{12,14},{9,11},... | collective-permute-start | bytes 393224 | tf_op jit(solution)/shard_map/ppermute | solution.py:488
  43.3 258.0 %reduce-scatter.6.cloned.1.call-start = ((), (), s32[]{:S(2)}) async-start(), calls=%async_computation.4 | async-start | bytes 1843200 | tf_op jit(solution)/shard_map/reduce_scatter | solution.py:732
  51.3 8.2 %collective-permute-start.4 = (bf16[2,26,32,512]{3,2,1,0:T(8,128)(2,1)}, bf16[2,26,32,512]{3,2,1,0:T(8,128)(2,1)}, u32[]{:S(2)}, u32[]{:S(2)}) collective-permute-start(bf16[2,26,32,512]{3,2,1,0:T(8,128)(2,1)} %broadcast_select_fusion.6), channel_id=1, source_target_pairs={{0,1},{1,0},{2,3},{3,2},{4,5},{5,4},{6,7},{7,6},{8,9},{9,8},{10,11... | collective-permute-start | bytes 5111816 | tf_op jit(solution)/shard_map/ppermute | solution.py:24
  53.9 27.9 %collective-permute-start.7 = (bf16[9,128,512]{2,1,0:T(8,128)(2,1)}, bf16[9,128,512]{2,1,0:T(8,128)(2,1)}, u32[]{:S(2)}, u32[]{:S(2)}) collective-permute-start(bf16[9,128,512]{2,1,0:T(8,128)(2,1)} %collective-permute-done), channel_id=1, source_target_pairs={{2,4},{4,6},{3,5},{5,7},{10,12},{12,14},{11,13},{13,15},{18,20},{2... | collective-permute-start | bytes 3538952 | tf_op jit(solution)/shard_map/ppermute | solution.py:354
  55.8 36.2 %collective-permute-start.8 = (bf16[9,128,512]{2,1,0:T(8,128)(2,1)}, bf16[9,128,512]{2,1,0:T(8,128)(2,1)}, u32[]{:S(2)}, u32[]{:S(2)}) collective-permute-start(bf16[9,128,512]{2,1,0:T(8,128)(2,1)} %collective-permute-done.1), channel_id=1, source_target_pairs={{2,0},{4,2},{3,1},{5,3},{10,8},{12,10},{11,9},{13,11},{18,16},{20,... | collective-permute-start | bytes 3538952 | tf_op jit(solution)/shard_map/ppermute | solution.py:355
  63.6 28.7 %collective-permute-start.5 = (bf16[9,128,512]{2,1,0:T(8,128)(2,1)}, bf16[9,128,512]{2,1,0:T(8,128)(2,1)}, u32[]{:S(2)}, u32[]{:S(2)}) collective-permute-start(bf16[9,128,512]{2,1,0:T(8,128)(2,1)} %broadcast_select_fusion.12), channel_id=1, source_target_pairs={{0,8},{8,0},{16,24},{24,16},{1,9},{9,1},{17,25},{25,17},{2,10},{10... | collective-permute-start | bytes 3538952 | tf_op jit(solution)/shard_map/ppermute | solution.py:24
  65.1 28.4 %collective-permute-start.6 = (bf16[9,128,512]{2,1,0:T(8,128)(2,1)}, bf16[9,128,512]{2,1,0:T(8,128)(2,1)}, u32[]{:S(2)}, u32[]{:S(2)}) collective-permute-start(bf16[9,128,512]{2,1,0:T(8,128)(2,1)} %broadcast_select_fusion.12), channel_id=1, source_target_pairs={{0,16},{8,24},{16,0},{24,8},{1,17},{9,25},{17,1},{25,9},{2,18},{10... | collective-permute-start | bytes 3538952 | tf_op jit(solution)/shard_map/ppermute | solution.py:24
  94.9 7.4 %collective-permute-start.9 = (f32[8,64]{0,1:T(8,128)S(1)}, f32[8,64]{0,1:T(8,128)S(1)}, u32[]{:S(2)}, u32[]{:S(2)}) collective-permute-start(f32[8,64]{0,1:T(8,128)S(1)} %copy.156), channel_id=1, source_target_pairs={{0,8},{8,0},{16,24},{24,16},{1,9},{9,1},{17,25},{25,17},{2,10},{10... | collective-permute-start | bytes 6152 | tf_op jit(solution)/shard_map/ppermute | solution.py:24
  95.5 59.4 %collective-permute-start.13 = (bf16[9,128,512]{2,1,0:T(8,128)(2,1)}, bf16[9,128,512]{2,1,0:T(8,128)(2,1)}, u32[]{:S(2)}, u32[]{:S(2)}) collective-permute-start(bf16[9,128,512]{2,1,0:T(8,128)(2,1)} %collective-permute-done.7), channel_id=1, source_target_pairs={{4,6},{5,7},{12,14},{13,15},{20,22},{21,23},{28,30},{29,31}} | collective-permute-start | bytes 3538952 | tf_op jit(solution)/shard_map/ppermute | solution.py:354
  97.1 57.8 %collective-permute-start.14 = (bf16[9,128,512]{2,1,0:T(8,128)(2,1)}, bf16[9,128,512]{2,1,0:T(8,128)(2,1)}, u32[]{:S(2)}, u32[]{:S(2)}) collective-permute-start(bf16[9,128,512]{2,1,0:T(8,128)(2,1)} %collective-permute-done.8), channel_id=1, source_target_pairs={{2,0},{3,1},{10,8},{11,9},{18,16},{19,17},{26,24},{27,25}} | collective-permute-start | bytes 3538952 | tf_op jit(solution)/shard_map/ppermute | solution.py:355
  102.3 4.0 collective-permute-start.10
  106.3 48.6 %collective-permute-start.11 = (bf16[9,192,512]{2,1,0:T(8,128)(2,1)}, bf16[9,192,512]{2,1,0:T(8,128)(2,1)}, u32[]{:S(2)}, u32[]{:S(2)}) collective-permute-start(bf16[9,192,512]{2,1,0:T(8,128)(2,1)} %get-tuple-element.137), channel_id=1, source_target_pairs={{0,8},{8,0},{16,24},{24,16},{1,9},{9,1},{17,25},{25,17},{2,10},{10... | collective-permute-start | bytes 5308424 | tf_op jit(solution)/shard_map/ppermute | solution.py:24
  107.8 47.1 %collective-permute-start.12 = (bf16[9,192,512]{2,1,0:T(8,128)(2,1)}, bf16[9,192,512]{2,1,0:T(8,128)(2,1)S(1)}, u32[]{:S(2)}, u32[]{:S(2)}) collective-permute-start(bf16[9,192,512]{2,1,0:T(8,128)(2,1)} %get-tuple-element.138), channel_id=1, source_target_pairs={{0,16},{8,24},{16,0},{24,8},{1,17},{9,25},{17,1},{25,9},{2,18},{10... | collective-permute-start | bytes 5308424 | tf_op jit(solution)/shard_map/ppermute | solution.py:24
  162.4 42.1 %collective-permute-start.16 = (bf16[9,192,512]{2,1,0:T(8,128)(2,1)S(1)}, bf16[9,192,512]{2,1,0:T(8,128)(2,1)S(1)}, u32[]{:S(2)}, u32[]{:S(2)}) collective-permute-start(bf16[9,192,512]{2,1,0:T(8,128)(2,1)S(1)} %get-tuple-element.149), channel_id=1, source_target_pairs={{0,8},{8,0},{16,24},{24,16},{1,9},{9,1},{17,25},{25,17},{2,10},{10... | collective-permute-start | bytes 5308424 | tf_op jit(solution)/shard_map/ppermute | solution.py:24
  163.9 40.6 %collective-permute-start.17 = (bf16[9,192,512]{2,1,0:T(8,128)(2,1)S(1)}, bf16[9,192,512]{2,1,0:T(8,128)(2,1)S(1)}, u32[]{:S(2)}, u32[]{:S(2)}) collective-permute-start(bf16[9,192,512]{2,1,0:T(8,128)(2,1)S(1)} %get-tuple-element.150), channel_id=1, source_target_pairs={{0,16},{8,24},{16,0},{24,8},{1,17},{9,25},{17,1},{25,9},{2,18},{10... | collective-permute-start | bytes 5308424 | tf_op jit(solution)/shard_map/ppermute | solution.py:24
  165.3 39.2 %collective-permute-start.18 = (bf16[1664,512]{1,0:T(8,128)(2,1)}, bf16[1664,512]{1,0:T(8,128)(2,1)}, u32[]{:S(2)}, u32[]{:S(2)}) collective-permute-start(bf16[1664,512]{1,0:T(8,128)(2,1)} %get-tuple-element.151), channel_id=1, source_target_pairs={{0,2},{2,0},{4,6},{6,4},{1,3},{3,1},{5,7},{7,5},{8,10},{10,8},{12,... | collective-permute-start | bytes 5111816 | tf_op jit(solution)/shard_map/ppermute | solution.py:24
  204.8 16.5 %collective-permute-start.19 = (bf16[9,64,512]{2,1,0:T(8,128)(2,1)S(1)}, bf16[9,64,512]{2,1,0:T(8,128)(2,1)S(1)}, u32[]{:S(2)}, u32[]{:S(2)}) collective-permute-start(bf16[9,64,512]{2,1,0:T(8,128)(2,1)S(1)} %get-tuple-element.159), channel_id=1, source_target_pairs={{0,8},{8,0},{16,24},{24,16},{1,9},{9,1},{17,25},{25,17},{2,10},{10... | collective-permute-start | bytes 1769480 | tf_op jit(solution)/shard_map/ppermute | solution.py:24
  205.4 15.8 %collective-permute-start.20 = (bf16[9,64,512]{2,1,0:T(8,128)(2,1)S(1)}, bf16[9,64,512]{2,1,0:T(8,128)(2,1)S(1)}, u32[]{:S(2)}, u32[]{:S(2)}) collective-permute-start(bf16[9,64,512]{2,1,0:T(8,128)(2,1)S(1)} %get-tuple-element.160), channel_id=1, source_target_pairs={{0,16},{8,24},{16,0},{24,8},{1,17},{9,25},{17,1},{25,9},{2,18},{10... | collective-permute-start | bytes 1769480 | tf_op jit(solution)/shard_map/ppermute | solution.py:24
  233.8 4.4 collective-permute-start.21
  239.8 4.8 collective-permute-start.22
  244.5 228.0 %reduce-scatter.8.cloned.1.call-start = ((), (), s32[]{:S(2)}) async-start(), calls=%async_computation.5 | async-start | bytes 589824 | tf_op jit(solution)/shard_map/reduce_scatter | solution.py:890
  244.6 3.7 collective-permute-start.23
  252.0 3.8 collective-permute-start.25
  255.8 4.5 collective-permute-start.26
  264.6 5.9 collective-permute-start.28
  277.9 4.5 collective-permute-start.31
  285.0 5.8 collective-permute-start.37
  286.3 6.1 %collective-permute-start.36 = (bf16[1,32,512]{2,1,0:T(8,128)(2,1)S(1)}, bf16[1,32,512]{2,1,0:T(8,128)(2,1)S(1)}, u32[]{:S(2)}, u32[]{:S(2)}) collective-permute-start(bf16[1,32,512]{2,1,0:T(8,128)(2,1)S(1)} %get-tuple-element.453), channel_id=1, source_target_pairs={{0,2},{2,4},{4,6},{1,3},{3,5},{5,7},{8,10},{10,12},{12,14},{9,11},... | collective-permute-start | bytes 98312 | tf_op jit(solution)/shard_map/ppermute | solution.py:488
  294.6 4.2 collective-permute-start.38
  294.6 39.8 %collective-permute-start.32 = (bf16[24,32,512]{2,1,0:T(8,128)(2,1)}, bf16[24,32,512]{2,1,0:T(8,128)(2,1)}, u32[]{:S(2)}, u32[]{:S(2)}) collective-permute-start(bf16[24,32,512]{2,1,0:T(8,128)(2,1)} %bitcast.67), channel_id=1, source_target_pairs={{0,2},{2,0},{4,6},{6,4},{1,3},{3,1},{5,7},{7,5},{8,10},{10,8},{12,... | collective-permute-start | bytes 2359304 | tf_op jit(solution)/shard_map/ppermute | solution.py:24
  298.2 36.2 %collective-permute-start.35 = (f32[513,150]{0,1:T(8,128)}, f32[513,150]{0,1:T(8,128)}, u32[]{:S(2)}, u32[]{:S(2)}) collective-permute-start(f32[513,150]{0,1:T(8,128)} %pad_maximum_fusion.32), channel_id=1, source_target_pairs={{0,8},{8,0},{16,24},{24,16},{1,9},{9,1},{17,25},{25,17},{2,10},{10... | collective-permute-start | bytes 923408 | tf_op jit(solution)/shard_map/ppermute | solution.py:24
  301.3 33.1 %collective-permute-start.33 = (bf16[400,256]{1,0:T(8,128)(2,1)}, bf16[400,256]{1,0:T(8,128)(2,1)}, u32[]{:S(2)}, u32[]{:S(2)}) collective-permute-start(bf16[400,256]{1,0:T(8,128)(2,1)} %reduce-scatter.6.cloned.1.call-done), channel_id=1, source_target_pairs={{0,8},{8,0},{16,24},{24,16},{1,9},{9,1},{17,25},{25,17},{2,10},{10... | collective-permute-start | bytes 614408 | tf_op jit(solution)/shard_map/ppermute | solution.py:24
  302.6 31.8 %collective-permute-start.34 = (bf16[400,256]{1,0:T(8,128)(2,1)}, bf16[400,256]{1,0:T(8,128)(2,1)}, u32[]{:S(2)}, u32[]{:S(2)}) collective-permute-start(bf16[400,256]{1,0:T(8,128)(2,1)} %reduce-scatter.6.cloned.1.call-done), channel_id=1, source_target_pairs={{0,16},{8,24},{16,0},{24,8},{1,17},{9,25},{17,1},{25,9},{2,18},{10... | collective-permute-start | bytes 614408 | tf_op jit(solution)/shard_map/ppermute | solution.py:24
  335.6 32.2 %collective-permute-start.40 = (f32[513,150]{0,1:T(8,128)S(1)}, f32[513,150]{0,1:T(8,128)S(1)}, u32[]{:S(2)}, u32[]{:S(2)}) collective-permute-start(f32[513,150]{0,1:T(8,128)S(1)} %fusion.202), channel_id=1, source_target_pairs={{0,16},{8,24},{16,0},{24,8},{1,17},{9,25},{17,1},{25,9},{2,18},{10... | collective-permute-start | bytes 923408 | tf_op jit(solution)/shard_map/ppermute | solution.py:24
  367.8 33.1 %collective-permute-start.41 = (bf16[9,128,512]{2,1,0:T(8,128)(2,1)}, bf16[9,128,512]{2,1,0:T(8,128)(2,1)}, u32[]{:S(2)}, u32[]{:S(2)}) collective-permute-start(bf16[9,128,512]{2,1,0:T(8,128)(2,1)} %pad_maximum_fusion.20), channel_id=1, source_target_pairs={{0,8},{8,0},{16,24},{24,16},{1,9},{9,1},{17,25},{25,17},{2,10},{10... | collective-permute-start | bytes 3538952 | tf_op jit(solution)/shard_map/ppermute | solution.py:24
  368.5 32.4 %collective-permute-start.42 = (bf16[9,128,512]{2,1,0:T(8,128)(2,1)}, bf16[9,128,512]{2,1,0:T(8,128)(2,1)}, u32[]{:S(2)}, u32[]{:S(2)}) collective-permute-start(bf16[9,128,512]{2,1,0:T(8,128)(2,1)} %pad_maximum_fusion.21), channel_id=1, source_target_pairs={{0,16},{8,24},{16,0},{24,8},{1,17},{9,25},{17,1},{25,9},{2,18},{10... | collective-permute-start | bytes 3538952 | tf_op jit(solution)/shard_map/ppermute | solution.py:24
  370.1 30.9 %collective-permute-start.44 = (f32[513,150]{0,1:T(8,128)S(1)}, f32[513,150]{0,1:T(8,128)S(1)}, u32[]{:S(2)}, u32[]{:S(2)}) collective-permute-start(f32[513,150]{0,1:T(8,128)S(1)} %add.573), channel_id=1, source_target_pairs={{0,2},{2,0},{4,6},{6,4},{1,3},{3,1},{5,7},{7,5},{8,10},{10,8},{12,... | collective-permute-start | bytes 923408 | tf_op jit(solution)/shard_map/ppermute | solution.py:24
  374.5 26.4 %collective-permute-start.43 = (bf16[400,256]{1,0:T(8,128)(2,1)}, bf16[400,256]{1,0:T(8,128)(2,1)S(1)}, u32[]{:S(2)}, u32[]{:S(2)}) collective-permute-start(bf16[400,256]{1,0:T(8,128)(2,1)} %collective-permute-done.33), channel_id=1, source_target_pairs={{0,16},{8,24},{16,0},{24,8},{1,17},{9,25},{17,1},{25,9},{2,18},{10... | collective-permute-start | bytes 614408 | tf_op jit(solution)/shard_map/ppermute | solution.py:24
  402.9 26.9 %collective-permute-start.46 = (bf16[9,64,512]{2,1,0:T(8,128)(2,1)S(1)}, bf16[9,64,512]{2,1,0:T(8,128)(2,1)S(1)}, u32[]{:S(2)}, u32[]{:S(2)}) collective-permute-start(bf16[9,64,512]{2,1,0:T(8,128)(2,1)S(1)} %get-tuple-element.188), channel_id=1, source_target_pairs={{0,16},{8,24},{16,0},{24,8},{1,17},{9,25},{17,1},{25,9},{2,18},{10... | collective-permute-start | bytes 1769480 | tf_op jit(solution)/shard_map/ppermute | solution.py:24
  404.4 25.4 %collective-permute-start.47 = (bf16[9,64,512]{2,1,0:T(8,128)(2,1)S(1)}, bf16[9,64,512]{2,1,0:T(8,128)(2,1)S(1)}, u32[]{:S(2)}, u32[]{:S(2)}) collective-permute-start(bf16[9,64,512]{2,1,0:T(8,128)(2,1)S(1)} %get-tuple-element.189), channel_id=1, source_target_pairs={{0,8},{8,0},{16,24},{24,16},{1,9},{9,1},{17,25},{25,17},{2,10},{10... | collective-permute-start | bytes 1769480 | tf_op jit(solution)/shard_map/ppermute | solution.py:24
  405.8 23.9 %collective-permute-start.48 = (f32[513,150]{0,1:T(8,128)S(1)}, f32[513,150]{0,1:T(8,128)S(1)}, u32[]{:S(2)}, u32[]{:S(2)}) collective-permute-start(f32[513,150]{0,1:T(8,128)S(1)} %add.578), channel_id=1, source_target_pairs={{0,4},{2,6},{4,0},{6,2},{1,5},{3,7},{5,1},{7,3},{8,12},{10,14},{12... | collective-permute-start | bytes 923408 | tf_op jit(solution)/shard_map/ppermute | solution.py:24
  406.2 5.3 collective-permute-start.49
  433.5 34.4 %collective-permute-start.50 = (bf16[9,128,512]{2,1,0:T(8,128)(2,1)}, bf16[9,128,512]{2,1,0:T(8,128)(2,1)}, u32[]{:S(2)}, u32[]{:S(2)}) collective-permute-start(bf16[9,128,512]{2,1,0:T(8,128)(2,1)} %get-tuple-element.199), channel_id=1, source_target_pairs={{0,8},{8,0},{16,24},{24,16},{1,9},{9,1},{17,25},{25,17},{2,10},{10... | collective-permute-start | bytes 3538952 | tf_op jit(solution)/shard_map/ppermute | solution.py:24
  434.2 33.6 %collective-permute-start.51 = (bf16[9,128,512]{2,1,0:T(8,128)(2,1)}, bf16[9,128,512]{2,1,0:T(8,128)(2,1)}, u32[]{:S(2)}, u32[]{:S(2)}) collective-permute-start(bf16[9,128,512]{2,1,0:T(8,128)(2,1)} %get-tuple-element.200), channel_id=1, source_target_pairs={{0,16},{8,24},{16,0},{24,8},{1,17},{9,25},{17,1},{25,9},{2,18},{10... | collective-permute-start | bytes 3538952 | tf_op jit(solution)/shard_map/ppermute | solution.py:24
  434.8 33.0 %collective-permute-start.52 = (bf16[9,64,512]{2,1,0:T(8,128)(2,1)}, bf16[9,64,512]{2,1,0:T(8,128)(2,1)}, u32[]{:S(2)}, u32[]{:S(2)}) collective-permute-start(bf16[9,64,512]{2,1,0:T(8,128)(2,1)} %get-tuple-element.201), channel_id=1, source_target_pairs={{0,4},{2,6},{4,0},{6,2},{1,5},{3,7},{5,1},{7,3},{8,12},{10,14},{12... | collective-permute-start | bytes 1769480 | tf_op jit(solution)/shard_map/ppermute | solution.py:24
  437.7 7.0 %collective-permute-start.53 = (f32[513,150]{0,1:T(8,128)}, f32[513,150]{0,1:T(8,128)}, u32[]{:S(2)}, u32[]{:S(2)}) collective-permute-start(f32[513,150]{0,1:T(8,128)} %add.586), channel_id=1, source_target_pairs={{0,1},{1,0},{2,3},{3,2},{4,5},{5,4},{6,7},{7,6},{8,9},{9,8},{10,11... | collective-permute-start | bytes 923408 | tf_op jit(solution)/shard_map/ppermute | solution.py:24
  441.9 122.1 %all-gather.2.cloned.1.call-start = ((), (), s32[]{:S(2)}) async-start(), calls=%async_computation.6 | async-start | bytes 2359296 | tf_op jit(solution)/shard_map/all_gather | solution.py:952
  471.1 14.7 %collective-permute-start.62 = (bf16[2,768,512]{2,1,0:T(8,128)(2,1)S(1)}, bf16[2,768,512]{2,1,0:T(8,128)(2,1)}, u32[]{:S(2)}, u32[]{:S(2)}) collective-permute-start(bf16[2,768,512]{2,1,0:T(8,128)(2,1)S(1)} %pad_maximum_fusion.16), channel_id=1, source_target_pairs={{0,1},{1,0},{2,3},{3,2},{4,5},{5,4},{6,7},{7,6},{8,9},{9,8},{10,11... | collective-permute-start | bytes 4718600 | tf_op jit(solution)/shard_map/ppermute | solution.py:24
  474.6 4.3 collective-permute-start.55
  479.0 4.6 collective-permute-start.56
  482.1 16.3 %collective-permute-start.57 = (bf16[9,64,512]{2,1,0:T(8,128)(2,1)S(1)}, bf16[9,64,512]{2,1,0:T(8,128)(2,1)S(1)}, u32[]{:S(2)}, u32[]{:S(2)}) collective-permute-start(bf16[9,64,512]{2,1,0:T(8,128)(2,1)S(1)} %copy-done.84), channel_id=1, source_target_pairs={{0,16},{8,24},{16,0},{24,8},{1,17},{9,25},{17,1},{25,9},{2,18},{10... | collective-permute-start | bytes 1769480 | tf_op jit(solution)/shard_map/ppermute | solution.py:24
  482.6 15.8 %collective-permute-start.58 = (bf16[9,64,512]{2,1,0:T(8,128)(2,1)S(1)}, bf16[9,64,512]{2,1,0:T(8,128)(2,1)S(1)}, u32[]{:S(2)}, u32[]{:S(2)}) collective-permute-start(bf16[9,64,512]{2,1,0:T(8,128)(2,1)S(1)} %copy-done.83), channel_id=1, source_target_pairs={{0,8},{8,0},{16,24},{24,16},{1,9},{9,1},{17,25},{25,17},{2,10},{10... | collective-permute-start | bytes 1769480 | tf_op jit(solution)/shard_map/ppermute | solution.py:24
  483.6 27.4 %collective-permute-start.59 = (bf16[9,64,512]{2,1,0:T(8,128)(2,1)S(1)}, bf16[9,64,512]{2,1,0:T(8,128)(2,1)S(1)}, u32[]{:S(2)}, u32[]{:S(2)}) collective-permute-start(bf16[9,64,512]{2,1,0:T(8,128)(2,1)S(1)} %copy-done.82), channel_id=1, source_target_pairs={{0,4},{2,6},{4,0},{6,2},{1,5},{3,7},{5,1},{7,3},{8,12},{10,14},{12... | collective-permute-start | bytes 1769480 | tf_op jit(solution)/shard_map/ppermute | solution.py:24
  484.6 13.8 %collective-permute-start.60 = (bf16[64,424]{1,0:T(8,128)(2,1)S(1)}, bf16[64,424]{1,0:T(8,128)(2,1)S(1)}, u32[]{:S(2)}, u32[]{:S(2)}) collective-permute-start(bf16[64,424]{1,0:T(8,128)(2,1)S(1)} %pad_maximum_fusion.33), channel_id=1, source_target_pairs={{0,8},{8,0},{16,24},{24,16},{1,9},{9,1},{17,25},{25,17},{2,10},{10... | collective-permute-start | bytes 162824 | tf_op jit(solution)/shard_map/ppermute | solution.py:24
  485.7 12.7 %collective-permute-start.61 = (bf16[64,424]{1,0:T(8,128)(2,1)S(1)}, bf16[64,424]{1,0:T(8,128)(2,1)S(1)}, u32[]{:S(2)}, u32[]{:S(2)}) collective-permute-start(bf16[64,424]{1,0:T(8,128)(2,1)S(1)} %pad_maximum_fusion.33), channel_id=1, source_target_pairs={{0,16},{8,24},{16,0},{24,8},{1,17},{9,25},{17,1},{25,9},{2,18},{10... | collective-permute-start | bytes 162824 | tf_op jit(solution)/shard_map/ppermute | solution.py:24
  513.4 17.2 %collective-permute-start.63 = (bf16[9,64,512]{2,1,0:T(8,128)(2,1)S(1)}, bf16[9,64,512]{2,1,0:T(8,128)(2,1)S(1)}, u32[]{:S(2)}, u32[]{:S(2)}) collective-permute-start(bf16[9,64,512]{2,1,0:T(8,128)(2,1)S(1)} %get-tuple-element.231), channel_id=1, source_target_pairs={{0,8},{8,0},{16,24},{24,16},{1,9},{9,1},{17,25},{25,17},{2,10},{10... | collective-permute-start | bytes 1769480 | tf_op jit(solution)/shard_map/ppermute | solution.py:24
  514.2 16.4 %collective-permute-start.64 = (bf16[9,64,512]{2,1,0:T(8,128)(2,1)S(1)}, bf16[9,64,512]{2,1,0:T(8,128)(2,1)S(1)}, u32[]{:S(2)}, u32[]{:S(2)}) collective-permute-start(bf16[9,64,512]{2,1,0:T(8,128)(2,1)S(1)} %get-tuple-element.232), channel_id=1, source_target_pairs={{0,16},{8,24},{16,0},{24,8},{1,17},{9,25},{17,1},{25,9},{2,18},{10... | collective-permute-start | bytes 1769480 | tf_op jit(solution)/shard_map/ppermute | solution.py:24
  515.6 14.9 %collective-permute-start.65 = (bf16[64,424]{1,0:T(8,128)(2,1)S(1)}, bf16[64,424]{1,0:T(8,128)(2,1)S(1)}, u32[]{:S(2)}, u32[]{:S(2)}) collective-permute-start(bf16[64,424]{1,0:T(8,128)(2,1)S(1)} %collective-permute-done.60), channel_id=1, source_target_pairs={{0,16},{8,24},{16,0},{24,8},{1,17},{9,25},{17,1},{25,9},{2,18},{10... | collective-permute-start | bytes 162824 | tf_op jit(solution)/shard_map/ppermute | solution.py:24
  540.8 37.9 %collective-permute-start.67 = (bf16[9,128,512]{2,1,0:T(8,128)(2,1)}, bf16[9,128,512]{2,1,0:T(8,128)(2,1)}, u32[]{:S(2)}, u32[]{:S(2)}) collective-permute-start(bf16[9,128,512]{2,1,0:T(8,128)(2,1)} %pad_maximum_fusion.24), channel_id=1, source_target_pairs={{0,16},{8,24},{16,0},{24,8},{1,17},{9,25},{17,1},{25,9},{2,18},{10... | collective-permute-start | bytes 3538952 | tf_op jit(solution)/shard_map/ppermute | solution.py:24
  542.2 36.5 %collective-permute-start.68 = (bf16[9,128,512]{2,1,0:T(8,128)(2,1)}, bf16[9,128,512]{2,1,0:T(8,128)(2,1)}, u32[]{:S(2)}, u32[]{:S(2)}) collective-permute-start(bf16[9,128,512]{2,1,0:T(8,128)(2,1)} %pad_maximum_fusion.25), channel_id=1, source_target_pairs={{0,8},{8,0},{16,24},{24,16},{1,9},{9,1},{17,25},{25,17},{2,10},{10... | collective-permute-start | bytes 3538952 | tf_op jit(solution)/shard_map/ppermute | solution.py:24
  (165 other events, 1823.1 us)
Sparse Core Ops, SparseCore 0:
  43.4 32.0 reduce-scatter.3
  244.6 32.8 reduce-scatter.5
  442.1 30.3 reduce-scatter.7
  536.2 27.8 all-gather.1

commit v4 on v3

--- a/solution.py
+++ b/solution.py
@@ -233,46 +233,59 @@
     )(wide, *weight, keeps, *extra)
 
 
-def weight_slot(sides, wides, marker=None):
+def weight_sums(sides, own, others, width, marker=None):
     _, cells, block = sides.shape
-    mid = wides.shape[1] // 3
-
-    def body(side_ref, wide_ref, *rest):
+    mid = own.shape[1] // 3
+    strips = 1 + len(others)
+    strip = cells // strips
+
+    if cells * mid > 3072 * 512:
+        parts = [own[width : width + strip], *others]
+        return jnp.stack(
+            [
+                sum(
+                    dot(
+                        sides[a, k * strip : (k + 1) * strip],
+                        parts[k][:, j * mid : (j + 1) * mid],
+                        contract_first,
+                    )
+                    for k in range(strips)
+                ).astype(bf16)
+                for a in range(3)
+                for j in range(3)
+            ]
+        )
+
+    def body(side_ref, own_ref, *rest):
         o_ref = rest[-1]
-        terms = lax.dot_general(
-            side_ref[0], wide_ref[...], contract_first, preferred_element_type=f32
-        )
+        terms = 0.0
+        for k in range(strips):
+            part = own_ref[width : width + strip, :] if k == 0 else rest[k - 1][...]
+            terms = terms + lax.dot_general(
+                side_ref[0, k * strip : (k + 1) * strip, :],
+                part,
+                contract_first,
+                preferred_element_type=f32,
+            )
         for j in range(3):
             o_ref[j] = terms[:, j * mid : (j + 1) * mid].astype(bf16)
 
+    once = pl.Buffered(1)
     extra = [] if marker is None else [marker]
     return pl.pallas_call(
         body,
         grid=(3,),
         in_specs=[
             pl.BlockSpec((1, cells, block), lambda a: (a, 0, 0)),
-            pl.BlockSpec((cells, 3 * mid), lambda a: (0, 0), pipeline_mode=pl.Buffered(1)),
+            pl.BlockSpec(own.shape, lambda a: (0, 0), pipeline_mode=once),
         ]
+        + [pl.BlockSpec((strip, 3 * mid), lambda a: (0, 0), pipeline_mode=once)] * len(others)
         + [pl.BlockSpec(memory_space=pl.ANY)] * len(extra),
         out_specs=pl.BlockSpec((3, block, mid), lambda a: (a, 0, 0)),
         out_shape=jax.ShapeDtypeStruct((9, block, mid), bf16),
-        compiler_params=pltpu.CompilerParams(vmem_limit_bytes=52 << 20),
+        compiler_params=pltpu.CompilerParams(vmem_limit_bytes=44 << 20),
         cost_estimate=small_cost,
-    )(sides, wides, *extra)
-
-
-def weight_sums(sides, wides, marker=None):
-    _, cells, _ = sides.shape
-    mid = wides.shape[1] // 3
-    if cells * mid <= 3072 * 512:
-        return weight_slot(sides, wides, marker)
-    return jnp.stack(
-        [
-            dot(sides[a], wides[:, j * mid : (j + 1) * mid], contract_first).astype(bf16)
-            for a in range(3)
-            for j in range(3)
-        ]
-    )
+    )(sides, own, *others, *extra)
 
 
 def pool_back(grads, projections, limits, shares, pooled, joined):
@@ -786,8 +799,7 @@
             lines.append(jnp.concatenate(pieces, axis=0))
         sides.append(lines)
 
-    mid_grads, home_side, *lines = tie(mid_grads, jnp.stack(sides[1]), *sides[0])
-    sides = [lines]
+    mid_grads, home_side, away_side = tie(mid_grads, jnp.stack(sides[1]), jnp.stack(sides[0]))
     conv_gain_grad, conv_bias_grad = mid_grads[0], mid_grads[1]
     background = ("img", "row", "col")
     class_chain = Chain(
@@ -826,41 +838,27 @@
         class_chain.receive(got[len(flights) : len(flights) + len(sent)])
         return got[: len(flights)], got[len(flights) + len(sent) :]
 
-    wides = shifted(
-        grad_strip.reshape(1, strip_cells, mid), canvas_box, top, width, reverse=True,
-        places=jnp.zeros((1,), jnp.int32), out_blocks=depth,
-    )
     held = [input_grads(slot) for slot in range(depth)]
     hops += [swap(own_means, "img", 1), swap(own_means, "img", 2)]
-    hops, held = phase(hops, held + [wides])
+    hops, cat_grads = phase(hops, held)
     *hops, means_one, means_two = hops
-    cat_grads, wides = held[:depth], held[depth]
+    cat_grads = list(cat_grads)
+    others = []
     for k, tile_there in enumerate(hops):
         strip = join_cols(tile_there, pair_strip(tile_there), 1)
-        wides = shifted(
-            strip.reshape(1, strip_cells, mid), canvas_box, (row ^ (k + 1)) * tile_h, width,
-            reverse=True, places=jnp.full((1,), k + 1, jnp.int32), out_blocks=depth, into=wides,
+        others.append(
+            shifted(
+                strip.reshape(1, strip_cells, mid), canvas_box, (row ^ (k + 1)) * tile_h, width,
+                reverse=True,
+            )[0]
         )
-    wides = wides.reshape(depth * strip_cells, 3 * mid)
-
-    def weight_grads(kind):
-        return jnp.stack(
-            [
-                dot(
-                    sides[kind][a], wides[:, j * mid : (j + 1) * mid], contract_first
-                ).astype(bf16)
-                for a in range(3)
-                for j in range(3)
-            ]
-        )
-
     class_sent = class_chain.send()
-    away = ImageSum(weight_grads(0))
+    away = ImageSum(weight_sums(away_side, own_wide, others, width))
     (*sends, class_got), marker = mark(*away.first_sends(), *class_sent)
     class_chain.receive([class_got])
     flights = away.first(sends)
     flights.append(swap(means_one, "img", 2))
-    home = weight_sums(home_side, wides, marker)
+    home = weight_sums(home_side, own_wide, others, width, marker)
     got, (home,) = phase(flights, [home])
     home = ImageSum(home)
     means = [own_means, means_one, means_two, got.pop()]
@@ -870,8 +868,9 @@
     got, held = phase(flights, held)
     cat_grads += held
     *sends, far_own, far_next = tie(*home.first_sends(), *away.reduced(got))
-    got, (far_next,) = phase(
-        home.first(sends) + [swap(far_own, "row", depth)], [far_next]
+    logits_out = logits.reshape(1, tile_h, tile_w, classes)
+    got, (far_next, logits_out, *means) = phase(
+        home.first(sends) + [swap(far_own, "row", depth)], [far_next, logits_out, *means]
     )
     crossed = [got.pop()]
     sends, second_mark = mark(*home.second_sends(got))
@@ -961,11 +960,11 @@
     feature_grad = pool_back(
         gathered[0], branch_projection_weight, limits, 1.0 / sizes[None], pooled, joined
     ).reshape(1, tile_h, tile_w, channels_in)
-    feature_grad, *got = tie(feature_grad, *got)
+    feature_grad, branch_w_grad, *got = tie(feature_grad, branch_w_grad, *got)
     conv_w_grad = home.gathered(got)
     conv_w_grad = jnp.transpose(conv_w_grad, (1, 0, 2))
     return (
-        logits.reshape(1, tile_h, tile_w, classes),
+        logits_out,
         feature_grad,
         branch_w_grad,
         branch_gain_grad,

time: 613 us -> 608 us (level)
  matrix products: 53.1 us -> 37.4 us
  Pallas kernels: 143 us -> 153 us
  local copies, waits for them, and re-layouts: 61.8 us -> 69.5 us
  waiting for transfers between devices: 116 us -> 109 us
    pallas_call x1 -> x2, Pallas kernels: 21 us -> 37.6 us  [weight_sums(): pl.pallas_call(body, grid=(3,), in_specs=[pl.BlockSpec((1, cells, block),...]
    dot_general x26 -> x17, matrix products: 53.1 us -> 37.4 us  [dot(): return lax.dot_general(a, b, dims, preferred_element_type=f32)]
    ppermute x59, waiting for transfers between devices: 88.9 us -> 80.3 us  [swap(): return lax.ppermute(value, axis, [(i, i ^ step) for i in range(count)])]
    unnamed x313 -> x289, local copies, waits for them, and re-layouts: 18.7 us -> 24.6 us
    pallas_call x5 -> x4, Pallas kernels: 34 us -> 28.7 us  [shifted(): pl.pallas_call(body, grid_spec=pltpu.PrefetchScalarGridSpec(num_scalar_pr...]
  transfers between devices with their start and end apart: 73 -> 73, of which waited for: 23 -> 23; matrix products, arithmetic and copies ran while one was open for 28% -> 27% of each run, Pallas kernels for 22% -> 24%
where the time goes in v4:
time: 608 us; the launch traced here: 597 us
  Pallas kernels  153 us (25%)
  other arithmetic  114 us (19%)
  waiting for transfers between devices  109 us (18%)
  starting transfers between devices  72.1 us (12%)
  local copies, waits for them, and re-layouts  69.5 us (11%)
  matrix products  37.4 us (6%)
  blocking collectives  25.3 us (4%)
  between operations  16.8 us (3%)
    ppermute x59, waiting for transfers between devices, swap(): return lax.ppermute(value, axis, [(i, i ^ step) for i in range(count)])  80.3 us
    pallas_call x4, Pallas kernels, conv_slot(): pl.pallas_call(body, grid=(cells // chunk,), in_specs=[pl.BlockSpec((1, e...  46.2 us
    ppermute x59, starting transfers between devices, swap(): return lax.ppermute(value, axis, [(i, i ^ step) for i in range(count)])  46.1 us
    pallas_call x2, Pallas kernels, weight_sums(): pl.pallas_call(body, grid=(3,), in_specs=[pl.BlockSpec((1, cells, block),...  37.6 us
    dot_general x17, matrix products, dot(): return lax.dot_general(a, b, dims, preferred_element_type=f32)  37.4 us
    pallas_call x4, Pallas kernels, grad_slot(): pl.pallas_call(body, grid=(cells // chunk,), in_specs=[pl.BlockSpec((ext,...  31.7 us
    pallas_call x4, Pallas kernels, shifted(): pl.pallas_call(body, grid_spec=pltpu.PrefetchScalarGridSpec(num_scalar_pr...  28.7 us
    all_gather x1, blocking collectives, on_device(): lax.all_gather((jax.nn.silu(before) + waiting['mark'][0, 0]).astype(bf16)...  25.3 us
  transfers between devices with their start and end apart: 73, of which 23 were waited for; matrix products, arithmetic and copies ran while one was open for 27% of the time, Pallas kernels for 24%

profile of v4, /device:TPU:0, one launch (start us, length us, event | category | flops | bytes accessed | tf_op | source)
XLA Modules:
  0.0 597.4 jit_solution(225677747010282598)
XLA Ops:
  7.4 2.4 dynamic-slice_bitcast_fusion.2
  9.8 5.9 collective-permute-start
  19.3 5.2 collective-permute-start.2
  25.2 3.9 divide_convert_fusion
  29.2 3.5 fusion.29
  32.7 2.5 fusion.52
  35.2 2.5 fusion.55
  37.8 2.5 fusion.58
  42.2 5.8 collective-permute-done.3
  57.6 2.5 broadcast_select_fusion.12
  68.5 4.6 fusion.107
  73.5 9.0 %shard_map.375.rest_0_ = bf16[4,1664,1536]{2,1,0:T(8,128)(2,1)} custom-call(s32[2]{0:T(128)S(1)} %get-tuple-element.539.place_ref, s32[1]{0:T(128)} %bitcast.22.first_ref, s32[8,4]{1,0:T(8,128)S(1)} %copy.149.box_ref, bf16[2,1664,512]{2,1,0:T(8,128)(2,1)} %bitcast.228), custom_call_target="tpu_custom_call" | custom-call | flops 1024 | bytes 1024 | tf_op jit(solution)/shard_map/pallas_call | solution.py:129
  82.5 9.4 %collective-permute-done.8 = bf16[9,128,512]{2,1,0:T(8,128)(2,1)} collective-permute-done((bf16[9,128,512]{2,1,0:T(8,128)(2,1)}, bf16[9,128,512]{2,1,0:T(8,128)(2,1)}, u32[]{:S(2)}, u32[]{:S(2)}) %collective-permute-start.8) | collective-permute-done | bytes 1179680 | tf_op jit(solution)/shard_map/ppermute | solution.py:368
  104.6 2.3 pad_maximum_fusion.6
  113.3 25.3 %all_gather.6 = bf16[512,400]{1,0:T(8,128)(2,1)S(1)} all-gather(bf16[64,400]{1,0:T(8,128)(2,1)S(1)} %get-tuple-element.356), channel_id=1, replica_groups=mesh['img'=4,'row'=4,'col'=2] {'row','col'}, dimensions={0}, use_global_device_ids=true | all-gather | bytes 460800 | tf_op jit(solution)/shard_map/all_gather | solution.py:680
  138.6 2.8 convolution_convert_fusion.1
  141.5 2.8 convolution_convert_fusion.2
  146.4 9.4 %shard_map.376.x_ref = bf16[4,1664,1536]{2,1,0:T(8,128)(2,1)} custom-call(s32[2]{0:T(128)S(1)} %get-tuple-element.538.place_ref, s32[1]{0:T(128)} %bitcast.22.first_ref, s32[8,4]{1,0:T(8,128)S(1)} %copy.149.box_ref, bf16[2,1664,512]{2,1,0:T(8,128)(2,1)} %pad_maximum_fusion.4.x_ref, ...), custom_call_target="tpu_custom_call", output_to_operand_aliasing={{}: (4, {})} | custom-call | flops 1024 | bytes 1024 | tf_op jit(solution)/shard_map/pallas_call | solution.py:129
  155.8 4.0 convolution_convert_fusion
  172.8 10.2 %shard_map.377.rest_4_ = f32[1536,512]{1,0:T(8,128)S(1)} custom-call(bf16[4,1664,1536]{2,1,0:T(8,128)(2,1)} %shard_map.376.x_ref, bf16[3,512,512]{2,1,0:T(8,128)(2,1)S(1)} %copy-done.30, bf16[3,512,512]{2,1,0:T(8,128)(2,1)S(1)} %copy-done.28, bf16[3,512,512]{2,1,0:T(8,128)(2,1)S(1)} %copy-done.26, f32[3,1536,1]{2,1,0:T(8,128)S(1)} %add_convert_fusion.rest_3_), custom_call_target="tpu_custom_call" | custom-call | flops 1024 | bytes 1024 | tf_op jit(solution)/shard_map/pallas_call | solution.py:177
  187.1 12.0 %shard_map.378.rest_4_ = f32[1536,512]{1,0:T(8,128)S(1)} custom-call(bf16[4,1664,1536]{2,1,0:T(8,128)(2,1)} %shard_map.376.x_ref, bf16[3,512,512]{2,1,0:T(8,128)(2,1)S(1)} %get-tuple-element.448.rest_0_, bf16[3,512,512]{2,1,0:T(8,128)(2,1)S(1)} %get-tuple-element.447.rest_1_, ...), custom_call_target="tpu_custom_call", output_to_operand_aliasing={{}: (5, {})} | custom-call | flops 1024 | bytes 1024 | tf_op jit(solution)/shard_map/pallas_call | solution.py:177
  201.1 8.4 %collective-permute-done.18 = bf16[1664,512]{1,0:T(8,128)(2,1)} collective-permute-done((bf16[1664,512]{1,0:T(8,128)(2,1)}, bf16[1664,512]{1,0:T(8,128)(2,1)}, u32[]{:S(2)}, u32[]{:S(2)}) %collective-permute-start.18) | collective-permute-done | bytes 1703968 | tf_op jit(solution)/shard_map/ppermute | solution.py:24
  213.8 12.0 %shard_map.379.rest_4_ = f32[1536,512]{1,0:T(8,128)S(1)} custom-call(bf16[4,1664,1536]{2,1,0:T(8,128)(2,1)} %shard_map.376.x_ref, bf16[3,512,512]{2,1,0:T(8,128)(2,1)S(1)} %get-tuple-element.439.rest_0_, bf16[3,512,512]{2,1,0:T(8,128)(2,1)S(1)} %get-tuple-element.438.rest_1_, ...), custom_call_target="tpu_custom_call", output_to_operand_aliasing={{}: (5, {})} | custom-call | flops 1024 | bytes 1024 | tf_op jit(solution)/shard_map/pallas_call | solution.py:177
  226.4 12.0 %shard_map.380 = f32[1536,512]{1,0:T(8,128)S(1)} custom-call(bf16[4,1664,1536]{2,1,0:T(8,128)(2,1)} %shard_map.376.x_ref, bf16[3,512,512]{2,1,0:T(8,128)(2,1)S(1)} %get-tuple-element.436.rest_0_, bf16[3,512,512]{2,1,0:T(8,128)(2,1)S(1)} %get-tuple-element.435.rest_1_, ...), custom_call_target="tpu_custom_call", output_to_operand_aliasing={{}: (5, {})} | custom-call | flops 1024 | bytes 1024 | tf_op jit(solution)/shard_map/pallas_call | solution.py:177
  240.7 4.1 slice_select_fusion.7
  244.8 2.5 fusion.103
  253.9 2.8 collective-permute-done.24
  256.9 3.4 collective-permute-done.25
  260.7 4.2 collective-permute-done.26
  267.5 4.5 pad_maximum_fusion.side_ref
  276.5 2.9 collective-permute-done.29
  279.6 3.4 collective-permute-done.30
  283.1 4.4 pad_maximum_fusion.1.side_ref
  289.9 4.5 collective-permute-start.32
  297.2 2.4 collective-permute-start.35
  306.7 5.4 shard_map.381
  312.2 2.4 copy-done.2
  314.6 7.9 %shard_map.382 = bf16[1536,512]{1,0:T(8,128)(2,1)S(1)} custom-call(bf16[1664,1536]{1,0:T(8,128)(2,1)S(1)} %bitcast.215, bf16[3,512,512]{2,1,0:T(8,128)(2,1)S(1)} %copy-done.31, bf16[3,512,512]{2,1,0:T(8,128)(2,1)S(1)} %copy-done.29, bf16[3,512,512]{2,1,0:T(8,128)(2,1)S(1)} %copy-done.27, f32[3,1536,1]{2,1,0:T(8,128)S(1)} %add_convert_fusion.rest_3_), custom_call_target="tpu_custom_call" | custom-call | flops 1024 | bytes 1024 | tf_op jit(solution)/shard_map/pallas_call | solution.py:220
  323.7 7.9 %shard_map.383 = bf16[1536,512]{1,0:T(8,128)(2,1)S(1)} custom-call(bf16[1664,1536]{1,0:T(8,128)(2,1)S(1)} %bitcast.216, bf16[3,512,512]{2,1,0:T(8,128)(2,1)S(1)} %copy-done.21, bf16[3,512,512]{2,1,0:T(8,128)(2,1)S(1)} %copy-done.25, bf16[3,512,512]{2,1,0:T(8,128)(2,1)S(1)} %copy-done.23, f32[3,1536,1]{2,1,0:T(8,128)S(1)} %add_convert_fusion.rest_3_), custom_call_target="tpu_custom_call" | custom-call | flops 1024 | bytes 1024 | tf_op jit(solution)/shard_map/pallas_call | solution.py:220
  337.1 4.8 shard_map.384
  342.0 2.3 copy-done.4
  344.3 18.6 %shard_map.385 = bf16[9,512,512]{2,1,0:T(8,128)(2,1)S(1)} custom-call(bf16[3,3072,512]{2,1,0:T(8,128)(2,1)} %pad_maximum_fusion.1.side_ref, bf16[1664,1536]{1,0:T(8,128)(2,1)} %bitcast.213, bf16[1536,1536]{1,0:T(8,128)(2,1)S(1)} %bitcast.223), custom_call_target="tpu_custom_call" | custom-call | flops 1024 | bytes 1024 | tf_op jit(solution)/shard_map/pallas_call | solution.py:275
  372.1 2.3 copy-done.5
  374.4 19.0 %shard_map.386 = bf16[9,512,512]{2,1,0:T(8,128)(2,1)S(1)} custom-call(bf16[3,3072,512]{2,1,0:T(8,128)(2,1)} %pad_maximum_fusion.side_ref, bf16[1664,1536]{1,0:T(8,128)(2,1)} %bitcast.214, bf16[1536,1536]{1,0:T(8,128)(2,1)S(1)} %bitcast.224, f32[8,128]{1,0:T(8,128)S(1)} %collective-permute-done.45.rest_1_), custom_call_target="tpu_custom_call" | custom-call | flops 1024 | bytes 1024 | tf_op jit(solution)/shard_map/pallas_call | solution.py:275
  395.7 5.5 collective-permute-done.43
  401.2 3.1 add_convert_fusion.12
  406.3 3.4 multiply_convert_fusion.1
  414.6 2.8 collective-permute-start.48
  422.5 7.9 %shard_map.387 = bf16[1536,512]{1,0:T(8,128)(2,1)S(1)} custom-call(bf16[1664,1536]{1,0:T(8,128)(2,1)S(1)} %bitcast.219, bf16[3,512,512]{2,1,0:T(8,128)(2,1)S(1)} %copy-done.9, bf16[3,512,512]{2,1,0:T(8,128)(2,1)S(1)} %copy-done.19, bf16[3,512,512]{2,1,0:T(8,128)(2,1)S(1)} %copy-done.17, f32[3,1536,1]{2,1,0:T(8,128)S(1)} %add_convert_fusion.rest_3_, ...), custom_call_target="tpu_custom_call" | custom-call | flops 1024 | bytes 1024 | tf_op jit(solution)/shard_map/pallas_call | solution.py:220
  430.4 8.1 %shard_map.388 = bf16[1536,512]{1,0:T(8,128)(2,1)S(1)} custom-call(bf16[1664,1536]{1,0:T(8,128)(2,1)S(1)} %bitcast.220, bf16[3,512,512]{2,1,0:T(8,128)(2,1)S(1)} %copy-done.11, bf16[3,512,512]{2,1,0:T(8,128)(2,1)S(1)} %copy-done.15, bf16[3,512,512]{2,1,0:T(8,128)(2,1)S(1)} %copy-done.13, f32[3,1536,1]{2,1,0:T(8,128)S(1)} %add_convert_fusion.rest_3_, ...), custom_call_target="tpu_custom_call" | custom-call | flops 1024 | bytes 1024 | tf_op jit(solution)/shard_map/pallas_call | solution.py:220
  438.6 4.2 add_convert_fusion.9
  447.3 2.6 fusion.38
  449.9 2.7 select_select_fusion.1
  455.5 22.6 %collective-permute-done.52 = bf16[9,64,512]{2,1,0:T(8,128)(2,1)} collective-permute-done((bf16[9,64,512]{2,1,0:T(8,128)(2,1)}, bf16[9,64,512]{2,1,0:T(8,128)(2,1)}, u32[]{:S(2)}, u32[]{:S(2)}) %collective-permute-start.52) | collective-permute-done | bytes 589856 | tf_op jit(solution)/shard_map/ppermute | solution.py:24
  478.1 3.1 add_convert_fusion.7
  483.3 2.6 broadcast_multiply_fusion.15
  493.3 5.2 collective-permute-done.55
  499.2 2.3 pad_maximum_fusion.29
  509.2 3.1 add_convert_fusion.1
  515.8 12.8 %collective-permute-done.65 = bf16[64,424]{1,0:T(8,128)(2,1)S(1)} collective-permute-done((bf16[64,424]{1,0:T(8,128)(2,1)S(1)}, bf16[64,424]{1,0:T(8,128)(2,1)S(1)}, u32[]{:S(2)}, u32[]{:S(2)}) %collective-permute-start.65) | collective-permute-done | bytes 54304 | tf_op jit(solution)/shard_map/ppermute | solution.py:24
  538.0 4.9 broadcast_in_dim.129
  547.6 12.3 %all-gather.2.cloned.1.call-done = bf16[4,512,424]{2,1,0:T(8,128)(2,1)} async-done(((bf16[4,64,424]{2,1,0:T(8,128)(2,1)}), bf16[4,512,424]{2,1,0:T(8,128)(2,1)}) %all-gather.2.cloned.1.call-update) | async-done | bytes 1736720 | tf_op jit(solution)/shard_map/all_gather | solution.py:951
  563.0 3.4 copy-done.33
  566.3 9.0 %shard_map.389 = f32[768,2048]{1,0:T(8,128)} custom-call(bf16[512,424]{1,0:T(8,128)(2,1)S(1)} %slice_bitcast_fusion.18.grad_ref, bf16[4,2048,512]{2,1,0:T(8,128)(2,1)S(1)} %copy-done.33, f32[1,400]{1,0:T(1,128)S(1)} %bitcast.227, bf16[768,400]{1,0:T(8,128)(2,1)S(1)} %copy-done.40, bf16[768,2048]{1,0:T(8,128)(2,1)S(1)} %copy-done.32), custom_call_target="tpu_custom_call" | custom-call | flops 1024 | bytes 1024 | tf_op jit(solution)/shard_map/pallas_call | solution.py:310
  (622 shorter events, 188.2 us)
Async XLA Ops:
  7.3 75.2 %reduce-scatter.4.cloned.1.call-start = ((), (), s32[]{:S(2)}) async-start(), calls=%async_computation.3 | async-start | bytes 1179648 | tf_op jit(solution)/shard_map/reduce_scatter | solution.py:651
  9.8 44.7 %collective-permute-start = (bf16[9,128,512]{2,1,0:T(8,128)(2,1)}, bf16[9,128,512]{2,1,0:T(8,128)(2,1)}, u32[]{:S(2)}, u32[]{:S(2)}) collective-permute-start(bf16[9,128,512]{2,1,0:T(8,128)(2,1)} %dynamic-slice_bitcast_fusion.2), channel_id=1, source_target_pairs={{0,2},{2,4},{4,6},{1,3},{3,5},{5,7},{8,10},{10,12},{12,14},{9,11},... | collective-permute-start | bytes 3538952 | tf_op jit(solution)/shard_map/ppermute | solution.py:367
  15.7 38.8 %collective-permute-start.1 = (bf16[9,128,512]{2,1,0:T(8,128)(2,1)}, bf16[9,128,512]{2,1,0:T(8,128)(2,1)}, u32[]{:S(2)}, u32[]{:S(2)}) collective-permute-start(bf16[9,128,512]{2,1,0:T(8,128)(2,1)} %dynamic-slice_bitcast_fusion.2), channel_id=1, source_target_pairs={{2,0},{4,2},{6,4},{3,1},{5,3},{7,5},{10,8},{12,10},{14,12},{11,9},... | collective-permute-start | bytes 3538952 | tf_op jit(solution)/shard_map/ppermute | solution.py:368
  18.0 30.1 %collective-permute-start.3 = (bf16[1,32,2048]{2,1,0:T(8,128)(2,1)S(1)}, bf16[1,32,2048]{2,1,0:T(8,128)(2,1)S(1)}, u32[]{:S(2)}, u32[]{:S(2)}) collective-permute-start(bf16[1,32,2048]{2,1,0:T(8,128)(2,1)S(1)} %get-tuple-element.395), channel_id=1, source_target_pairs={{2,0},{4,2},{6,4},{3,1},{5,3},{7,5},{10,8},{12,10},{14,12},{11,9},... | collective-permute-start | bytes 393224 | tf_op jit(solution)/shard_map/ppermute | solution.py:502
  19.3 28.8 %collective-permute-start.2 = (bf16[1,32,2048]{2,1,0:T(8,128)(2,1)S(1)}, bf16[1,32,2048]{2,1,0:T(8,128)(2,1)S(1)}, u32[]{:S(2)}, u32[]{:S(2)}) collective-permute-start(bf16[1,32,2048]{2,1,0:T(8,128)(2,1)S(1)} %get-tuple-element.394), channel_id=1, source_target_pairs={{0,2},{2,4},{4,6},{1,3},{3,5},{5,7},{8,10},{10,12},{12,14},{9,11},... | collective-permute-start | bytes 393224 | tf_op jit(solution)/shard_map/ppermute | solution.py:501
  41.9 262.0 %reduce-scatter.6.cloned.1.call-start = ((), (), s32[]{:S(2)}) async-start(), calls=%async_computation.4 | async-start | bytes 1843200 | tf_op jit(solution)/shard_map/reduce_scatter | solution.py:745
  51.9 8.1 %collective-permute-start.4 = (bf16[2,26,32,512]{3,2,1,0:T(8,128)(2,1)}, bf16[2,26,32,512]{3,2,1,0:T(8,128)(2,1)}, u32[]{:S(2)}, u32[]{:S(2)}) collective-permute-start(bf16[2,26,32,512]{3,2,1,0:T(8,128)(2,1)} %broadcast_select_fusion.6), channel_id=1, source_target_pairs={{0,1},{1,0},{2,3},{3,2},{4,5},{5,4},{6,7},{7,6},{8,9},{9,8},{10,11... | collective-permute-start | bytes 5111816 | tf_op jit(solution)/shard_map/ppermute | solution.py:24
  54.5 28.0 %collective-permute-start.7 = (bf16[9,128,512]{2,1,0:T(8,128)(2,1)}, bf16[9,128,512]{2,1,0:T(8,128)(2,1)}, u32[]{:S(2)}, u32[]{:S(2)}) collective-permute-start(bf16[9,128,512]{2,1,0:T(8,128)(2,1)} %collective-permute-done), channel_id=1, source_target_pairs={{2,4},{4,6},{3,5},{5,7},{10,12},{12,14},{11,13},{13,15},{18,20},{2... | collective-permute-start | bytes 3538952 | tf_op jit(solution)/shard_map/ppermute | solution.py:367
  56.3 35.6 %collective-permute-start.8 = (bf16[9,128,512]{2,1,0:T(8,128)(2,1)}, bf16[9,128,512]{2,1,0:T(8,128)(2,1)}, u32[]{:S(2)}, u32[]{:S(2)}) collective-permute-start(bf16[9,128,512]{2,1,0:T(8,128)(2,1)} %collective-permute-done.1), channel_id=1, source_target_pairs={{2,0},{4,2},{3,1},{5,3},{10,8},{12,10},{11,9},{13,11},{18,16},{20,... | collective-permute-start | bytes 3538952 | tf_op jit(solution)/shard_map/ppermute | solution.py:368
  64.3 28.7 %collective-permute-start.5 = (bf16[9,128,512]{2,1,0:T(8,128)(2,1)}, bf16[9,128,512]{2,1,0:T(8,128)(2,1)}, u32[]{:S(2)}, u32[]{:S(2)}) collective-permute-start(bf16[9,128,512]{2,1,0:T(8,128)(2,1)} %broadcast_select_fusion.12), channel_id=1, source_target_pairs={{0,8},{8,0},{16,24},{24,16},{1,9},{9,1},{17,25},{25,17},{2,10},{10... | collective-permute-start | bytes 3538952 | tf_op jit(solution)/shard_map/ppermute | solution.py:24
  65.8 28.4 %collective-permute-start.6 = (bf16[9,128,512]{2,1,0:T(8,128)(2,1)}, bf16[9,128,512]{2,1,0:T(8,128)(2,1)}, u32[]{:S(2)}, u32[]{:S(2)}) collective-permute-start(bf16[9,128,512]{2,1,0:T(8,128)(2,1)} %broadcast_select_fusion.12), channel_id=1, source_target_pairs={{0,16},{8,24},{16,0},{24,8},{1,17},{9,25},{17,1},{25,9},{2,18},{10... | collective-permute-start | bytes 3538952 | tf_op jit(solution)/shard_map/ppermute | solution.py:24
  95.6 7.4 %collective-permute-start.9 = (f32[8,64]{0,1:T(8,128)S(1)}, f32[8,64]{0,1:T(8,128)S(1)}, u32[]{:S(2)}, u32[]{:S(2)}) collective-permute-start(f32[8,64]{0,1:T(8,128)S(1)} %copy.151), channel_id=1, source_target_pairs={{0,8},{8,0},{16,24},{24,16},{1,9},{9,1},{17,25},{25,17},{2,10},{10... | collective-permute-start | bytes 6152 | tf_op jit(solution)/shard_map/ppermute | solution.py:24
  96.1 63.7 %collective-permute-start.13 = (bf16[9,128,512]{2,1,0:T(8,128)(2,1)}, bf16[9,128,512]{2,1,0:T(8,128)(2,1)}, u32[]{:S(2)}, u32[]{:S(2)}) collective-permute-start(bf16[9,128,512]{2,1,0:T(8,128)(2,1)} %collective-permute-done.7), channel_id=1, source_target_pairs={{4,6},{5,7},{12,14},{13,15},{20,22},{21,23},{28,30},{29,31}} | collective-permute-start | bytes 3538952 | tf_op jit(solution)/shard_map/ppermute | solution.py:367
  97.8 62.0 %collective-permute-start.14 = (bf16[9,128,512]{2,1,0:T(8,128)(2,1)}, bf16[9,128,512]{2,1,0:T(8,128)(2,1)}, u32[]{:S(2)}, u32[]{:S(2)}) collective-permute-start(bf16[9,128,512]{2,1,0:T(8,128)(2,1)} %collective-permute-done.8), channel_id=1, source_target_pairs={{2,0},{3,1},{10,8},{11,9},{18,16},{19,17},{26,24},{27,25}} | collective-permute-start | bytes 3538952 | tf_op jit(solution)/shard_map/ppermute | solution.py:368
  103.0 4.0 collective-permute-start.10
  107.0 52.8 %collective-permute-start.11 = (bf16[9,192,512]{2,1,0:T(8,128)(2,1)}, bf16[9,192,512]{2,1,0:T(8,128)(2,1)}, u32[]{:S(2)}, u32[]{:S(2)}) collective-permute-start(bf16[9,192,512]{2,1,0:T(8,128)(2,1)} %get-tuple-element.140), channel_id=1, source_target_pairs={{0,8},{8,0},{16,24},{24,16},{1,9},{9,1},{17,25},{25,17},{2,10},{10... | collective-permute-start | bytes 5308424 | tf_op jit(solution)/shard_map/ppermute | solution.py:24
  108.5 51.3 %collective-permute-start.12 = (bf16[9,192,512]{2,1,0:T(8,128)(2,1)}, bf16[9,192,512]{2,1,0:T(8,128)(2,1)S(1)}, u32[]{:S(2)}, u32[]{:S(2)}) collective-permute-start(bf16[9,192,512]{2,1,0:T(8,128)(2,1)} %get-tuple-element.141), channel_id=1, source_target_pairs={{0,16},{8,24},{16,0},{24,8},{1,17},{9,25},{17,1},{25,9},{2,18},{10... | collective-permute-start | bytes 5308424 | tf_op jit(solution)/shard_map/ppermute | solution.py:24
  167.3 42.2 %collective-permute-start.16 = (bf16[9,192,512]{2,1,0:T(8,128)(2,1)S(1)}, bf16[9,192,512]{2,1,0:T(8,128)(2,1)S(1)}, u32[]{:S(2)}, u32[]{:S(2)}) collective-permute-start(bf16[9,192,512]{2,1,0:T(8,128)(2,1)S(1)} %get-tuple-element.152), channel_id=1, source_target_pairs={{0,8},{8,0},{16,24},{24,16},{1,9},{9,1},{17,25},{25,17},{2,10},{10... | collective-permute-start | bytes 5308424 | tf_op jit(solution)/shard_map/ppermute | solution.py:24
  168.7 40.7 %collective-permute-start.17 = (bf16[9,192,512]{2,1,0:T(8,128)(2,1)S(1)}, bf16[9,192,512]{2,1,0:T(8,128)(2,1)S(1)}, u32[]{:S(2)}, u32[]{:S(2)}) collective-permute-start(bf16[9,192,512]{2,1,0:T(8,128)(2,1)S(1)} %get-tuple-element.153), channel_id=1, source_target_pairs={{0,16},{8,24},{16,0},{24,8},{1,17},{9,25},{17,1},{25,9},{2,18},{10... | collective-permute-start | bytes 5308424 | tf_op jit(solution)/shard_map/ppermute | solution.py:24
  170.2 39.2 %collective-permute-start.18 = (bf16[1664,512]{1,0:T(8,128)(2,1)}, bf16[1664,512]{1,0:T(8,128)(2,1)}, u32[]{:S(2)}, u32[]{:S(2)}) collective-permute-start(bf16[1664,512]{1,0:T(8,128)(2,1)} %get-tuple-element.154), channel_id=1, source_target_pairs={{0,2},{2,0},{4,6},{6,4},{1,3},{3,1},{5,7},{7,5},{8,10},{10,8},{12,... | collective-permute-start | bytes 5111816 | tf_op jit(solution)/shard_map/ppermute | solution.py:24
  209.7 16.4 %collective-permute-start.19 = (bf16[9,64,512]{2,1,0:T(8,128)(2,1)S(1)}, bf16[9,64,512]{2,1,0:T(8,128)(2,1)S(1)}, u32[]{:S(2)}, u32[]{:S(2)}) collective-permute-start(bf16[9,64,512]{2,1,0:T(8,128)(2,1)S(1)} %get-tuple-element.162), channel_id=1, source_target_pairs={{0,8},{8,0},{16,24},{24,16},{1,9},{9,1},{17,25},{25,17},{2,10},{10... | collective-permute-start | bytes 1769480 | tf_op jit(solution)/shard_map/ppermute | solution.py:24
  210.4 15.8 %collective-permute-start.20 = (bf16[9,64,512]{2,1,0:T(8,128)(2,1)S(1)}, bf16[9,64,512]{2,1,0:T(8,128)(2,1)S(1)}, u32[]{:S(2)}, u32[]{:S(2)}) collective-permute-start(bf16[9,64,512]{2,1,0:T(8,128)(2,1)S(1)} %get-tuple-element.163), channel_id=1, source_target_pairs={{0,16},{8,24},{16,0},{24,8},{1,17},{9,25},{17,1},{25,9},{2,18},{10... | collective-permute-start | bytes 1769480 | tf_op jit(solution)/shard_map/ppermute | solution.py:24
  240.0 4.8 collective-permute-start.21
  244.8 243.6 %reduce-scatter.8.cloned.1.call-start = ((), (), s32[]{:S(2)}) async-start(), calls=%async_computation.5 | async-start | bytes 589824 | tf_op jit(solution)/shard_map/reduce_scatter | solution.py:889
  249.3 3.7 collective-permute-start.23
  253.0 3.7 collective-permute-start.24
  260.3 4.6 collective-permute-start.26
  267.4 4.6 collective-permute-start.27
  272.0 3.7 collective-permute-start.28
  283.0 4.5 collective-permute-start.31
  288.6 5.8 collective-permute-start.33
  289.9 6.1 %collective-permute-start.32 = (bf16[1,32,512]{2,1,0:T(8,128)(2,1)S(1)}, bf16[1,32,512]{2,1,0:T(8,128)(2,1)S(1)}, u32[]{:S(2)}, u32[]{:S(2)}) collective-permute-start(bf16[1,32,512]{2,1,0:T(8,128)(2,1)S(1)} %get-tuple-element.459), channel_id=1, source_target_pairs={{0,2},{2,4},{4,6},{1,3},{3,5},{5,7},{8,10},{10,12},{12,14},{9,11},... | collective-permute-start | bytes 98312 | tf_op jit(solution)/shard_map/ppermute | solution.py:501
  297.1 8.1 %collective-permute-start.34 = (bf16[26,32,512]{2,1,0:T(8,128)(2,1)}, bf16[26,32,512]{2,1,0:T(8,128)(2,1)}, u32[]{:S(2)}, u32[]{:S(2)}) collective-permute-start(bf16[26,32,512]{2,1,0:T(8,128)(2,1)} %pad_maximum_fusion.25), channel_id=1, source_target_pairs={{0,1},{1,0},{2,3},{3,2},{4,5},{5,4},{6,7},{7,6},{8,9},{9,8},{10,11... | collective-permute-start | bytes 2555912 | tf_op jit(solution)/shard_map/ppermute | solution.py:24
  297.2 35.6 %collective-permute-start.35 = (bf16[24,32,512]{2,1,0:T(8,128)(2,1)S(1)}, bf16[24,32,512]{2,1,0:T(8,128)(2,1)}, u32[]{:S(2)}, u32[]{:S(2)}) collective-permute-start(bf16[24,32,512]{2,1,0:T(8,128)(2,1)S(1)} %bitcast.231), channel_id=1, source_target_pairs={{0,2},{2,0},{4,6},{6,4},{1,3},{3,1},{5,7},{7,5},{8,10},{10,8},{12,... | collective-permute-start | bytes 2359304 | tf_op jit(solution)/shard_map/ppermute | solution.py:24
  302.5 30.2 %collective-permute-start.38 = (f32[513,150]{0,1:T(8,128)}, f32[513,150]{0,1:T(8,128)}, u32[]{:S(2)}, u32[]{:S(2)}) collective-permute-start(f32[513,150]{0,1:T(8,128)} %pad_maximum_fusion.30), channel_id=1, source_target_pairs={{0,8},{8,0},{16,24},{24,16},{1,9},{9,1},{17,25},{25,17},{2,10},{10... | collective-permute-start | bytes 923408 | tf_op jit(solution)/shard_map/ppermute | solution.py:24
  303.9 28.9 %collective-permute-start.36 = (bf16[400,256]{1,0:T(8,128)(2,1)}, bf16[400,256]{1,0:T(8,128)(2,1)}, u32[]{:S(2)}, u32[]{:S(2)}) collective-permute-start(bf16[400,256]{1,0:T(8,128)(2,1)} %reduce-scatter.6.cloned.1.call-done), channel_id=1, source_target_pairs={{0,8},{8,0},{16,24},{24,16},{1,9},{9,1},{17,25},{25,17},{2,10},{10... | collective-permute-start | bytes 614408 | tf_op jit(solution)/shard_map/ppermute | solution.py:24
  304.6 28.2 %collective-permute-start.37 = (bf16[400,256]{1,0:T(8,128)(2,1)}, bf16[400,256]{1,0:T(8,128)(2,1)}, u32[]{:S(2)}, u32[]{:S(2)}) collective-permute-start(bf16[400,256]{1,0:T(8,128)(2,1)} %reduce-scatter.6.cloned.1.call-done), channel_id=1, source_target_pairs={{0,16},{8,24},{16,0},{24,8},{1,17},{9,25},{17,1},{25,9},{2,18},{10... | collective-permute-start | bytes 614408 | tf_op jit(solution)/shard_map/ppermute | solution.py:24
  334.0 33.3 %collective-permute-start.40 = (f32[513,150]{0,1:T(8,128)S(1)}, f32[513,150]{0,1:T(8,128)S(1)}, u32[]{:S(2)}, u32[]{:S(2)}) collective-permute-start(f32[513,150]{0,1:T(8,128)S(1)} %fusion.102), channel_id=1, source_target_pairs={{0,16},{8,24},{16,0},{24,8},{1,17},{9,25},{17,1},{25,9},{2,18},{10... | collective-permute-start | bytes 923408 | tf_op jit(solution)/shard_map/ppermute | solution.py:24
  367.3 33.9 %collective-permute-start.41 = (bf16[9,128,512]{2,1,0:T(8,128)(2,1)}, bf16[9,128,512]{2,1,0:T(8,128)(2,1)}, u32[]{:S(2)}, u32[]{:S(2)}) collective-permute-start(bf16[9,128,512]{2,1,0:T(8,128)(2,1)} %pad_maximum_fusion.18), channel_id=1, source_target_pairs={{0,8},{8,0},{16,24},{24,16},{1,9},{9,1},{17,25},{25,17},{2,10},{10... | collective-permute-start | bytes 3538952 | tf_op jit(solution)/shard_map/ppermute | solution.py:24
  368.7 32.5 %collective-permute-start.42 = (bf16[9,128,512]{2,1,0:T(8,128)(2,1)}, bf16[9,128,512]{2,1,0:T(8,128)(2,1)}, u32[]{:S(2)}, u32[]{:S(2)}) collective-permute-start(bf16[9,128,512]{2,1,0:T(8,128)(2,1)} %pad_maximum_fusion.19), channel_id=1, source_target_pairs={{0,16},{8,24},{16,0},{24,8},{1,17},{9,25},{17,1},{25,9},{2,18},{10... | collective-permute-start | bytes 3538952 | tf_op jit(solution)/shard_map/ppermute | solution.py:24
  370.1 31.0 %collective-permute-start.44 = (f32[513,150]{0,1:T(8,128)S(1)}, f32[513,150]{0,1:T(8,128)S(1)}, u32[]{:S(2)}, u32[]{:S(2)}) collective-permute-start(f32[513,150]{0,1:T(8,128)S(1)} %add.573), channel_id=1, source_target_pairs={{0,2},{2,0},{4,6},{6,4},{1,3},{3,1},{5,7},{7,5},{8,10},{10,8},{12,... | collective-permute-start | bytes 923408 | tf_op jit(solution)/shard_map/ppermute | solution.py:24
  370.2 31.0 %collective-permute-start.43 = (bf16[400,256]{1,0:T(8,128)(2,1)}, bf16[400,256]{1,0:T(8,128)(2,1)}, u32[]{:S(2)}, u32[]{:S(2)}) collective-permute-start(bf16[400,256]{1,0:T(8,128)(2,1)} %collective-permute-done.36), channel_id=1, source_target_pairs={{0,16},{8,24},{16,0},{24,8},{1,17},{9,25},{17,1},{25,9},{2,18},{10... | collective-permute-start | bytes 614408 | tf_op jit(solution)/shard_map/ppermute | solution.py:24
  404.3 34.2 %collective-permute-start.46 = (bf16[9,64,512]{2,1,0:T(8,128)(2,1)}, bf16[9,64,512]{2,1,0:T(8,128)(2,1)}, u32[]{:S(2)}, u32[]{:S(2)}) collective-permute-start(bf16[9,64,512]{2,1,0:T(8,128)(2,1)} %get-tuple-element.189), channel_id=1, source_target_pairs={{0,16},{8,24},{16,0},{24,8},{1,17},{9,25},{17,1},{25,9},{2,18},{10... | collective-permute-start | bytes 1769480 | tf_op jit(solution)/shard_map/ppermute | solution.py:24
  405.7 32.9 %collective-permute-start.47 = (bf16[9,64,512]{2,1,0:T(8,128)(2,1)}, bf16[9,64,512]{2,1,0:T(8,128)(2,1)}, u32[]{:S(2)}, u32[]{:S(2)}) collective-permute-start(bf16[9,64,512]{2,1,0:T(8,128)(2,1)} %get-tuple-element.190), channel_id=1, source_target_pairs={{0,8},{8,0},{16,24},{24,16},{1,9},{9,1},{17,25},{25,17},{2,10},{10... | collective-permute-start | bytes 1769480 | tf_op jit(solution)/shard_map/ppermute | solution.py:24
  414.6 24.0 %collective-permute-start.48 = (f32[513,150]{0,1:T(8,128)S(1)}, f32[513,150]{0,1:T(8,128)S(1)}, u32[]{:S(2)}, u32[]{:S(2)}) collective-permute-start(f32[513,150]{0,1:T(8,128)S(1)} %add.579), channel_id=1, source_target_pairs={{0,4},{2,6},{4,0},{6,2},{1,5},{3,7},{5,1},{7,3},{8,12},{10,14},{12... | collective-permute-start | bytes 923408 | tf_op jit(solution)/shard_map/ppermute | solution.py:24
  442.8 35.3 %collective-permute-start.50 = (bf16[9,128,512]{2,1,0:T(8,128)(2,1)}, bf16[9,128,512]{2,1,0:T(8,128)(2,1)}, u32[]{:S(2)}, u32[]{:S(2)}) collective-permute-start(bf16[9,128,512]{2,1,0:T(8,128)(2,1)} %get-tuple-element.195), channel_id=1, source_target_pairs={{0,8},{8,0},{16,24},{24,16},{1,9},{9,1},{17,25},{25,17},{2,10},{10... | collective-permute-start | bytes 3538952 | tf_op jit(solution)/shard_map/ppermute | solution.py:24
  444.1 34.0 %collective-permute-start.51 = (bf16[9,128,512]{2,1,0:T(8,128)(2,1)}, bf16[9,128,512]{2,1,0:T(8,128)(2,1)}, u32[]{:S(2)}, u32[]{:S(2)}) collective-permute-start(bf16[9,128,512]{2,1,0:T(8,128)(2,1)} %get-tuple-element.196), channel_id=1, source_target_pairs={{0,16},{8,24},{16,0},{24,8},{1,17},{9,25},{17,1},{25,9},{2,18},{10... | collective-permute-start | bytes 3538952 | tf_op jit(solution)/shard_map/ppermute | solution.py:24
  444.8 33.3 %collective-permute-start.52 = (bf16[9,64,512]{2,1,0:T(8,128)(2,1)}, bf16[9,64,512]{2,1,0:T(8,128)(2,1)}, u32[]{:S(2)}, u32[]{:S(2)}) collective-permute-start(bf16[9,64,512]{2,1,0:T(8,128)(2,1)} %get-tuple-element.197), channel_id=1, source_target_pairs={{0,4},{2,6},{4,0},{6,2},{1,5},{3,7},{5,1},{7,3},{8,12},{10,14},{12... | collective-permute-start | bytes 1769480 | tf_op jit(solution)/shard_map/ppermute | solution.py:24
  445.3 10.1 %collective-permute-start.53 = (f32[513,150]{0,1:T(8,128)S(1)}, f32[513,150]{0,1:T(8,128)S(1)}, u32[]{:S(2)}, u32[]{:S(2)}) collective-permute-start(f32[513,150]{0,1:T(8,128)S(1)} %add.585), channel_id=1, source_target_pairs={{0,1},{1,0},{2,3},{3,2},{4,5},{5,4},{6,7},{7,6},{8,9},{9,8},{10,11... | collective-permute-start | bytes 923408 | tf_op jit(solution)/shard_map/ppermute | solution.py:24
  449.9 110.0 %all-gather.2.cloned.1.call-start = ((), (), s32[]{:S(2)}) async-start(), calls=%async_computation.6 | async-start | bytes 2359296 | tf_op jit(solution)/shard_map/all_gather | solution.py:951
  455.0 49.1 %collective-permute-start.62 = (bf16[2,768,512]{2,1,0:T(8,128)(2,1)}, bf16[2,768,512]{2,1,0:T(8,128)(2,1)S(1)}, u32[]{:S(2)}, u32[]{:S(2)}) collective-permute-start(bf16[2,768,512]{2,1,0:T(8,128)(2,1)} %pad_maximum_fusion.14), channel_id=1, source_target_pairs={{0,1},{1,0},{2,3},{3,2},{4,5},{5,4},{6,7},{7,6},{8,9},{9,8},{10,11... | collective-permute-start | bytes 4718600 | tf_op jit(solution)/shard_map/ppermute | solution.py:24
  481.3 27.9 %collective-permute-start.57 = (bf16[9,64,512]{2,1,0:T(8,128)(2,1)}, bf16[9,64,512]{2,1,0:T(8,128)(2,1)}, u32[]{:S(2)}, u32[]{:S(2)}) collective-permute-start(bf16[9,64,512]{2,1,0:T(8,128)(2,1)} %get-tuple-element.210), channel_id=1, source_target_pairs={{0,16},{8,24},{16,0},{24,8},{1,17},{9,25},{17,1},{25,9},{2,18},{10... | collective-permute-start | bytes 1769480 | tf_op jit(solution)/shard_map/ppermute | solution.py:24
  482.6 26.6 %collective-permute-start.58 = (bf16[9,64,512]{2,1,0:T(8,128)(2,1)}, bf16[9,64,512]{2,1,0:T(8,128)(2,1)}, u32[]{:S(2)}, u32[]{:S(2)}) collective-permute-start(bf16[9,64,512]{2,1,0:T(8,128)(2,1)} %get-tuple-element.211), channel_id=1, source_target_pairs={{0,8},{8,0},{16,24},{24,16},{1,9},{9,1},{17,25},{25,17},{2,10},{10... | collective-permute-start | bytes 1769480 | tf_op jit(solution)/shard_map/ppermute | solution.py:24
  483.2 26.0 %collective-permute-start.59 = (bf16[9,64,512]{2,1,0:T(8,128)(2,1)}, bf16[9,64,512]{2,1,0:T(8,128)(2,1)}, u32[]{:S(2)}, u32[]{:S(2)}) collective-permute-start(bf16[9,64,512]{2,1,0:T(8,128)(2,1)} %get-tuple-element.212), channel_id=1, source_target_pairs={{0,4},{2,6},{4,0},{6,2},{1,5},{3,7},{5,1},{7,3},{8,12},{10,14},{12... | collective-permute-start | bytes 1769480 | tf_op jit(solution)/shard_map/ppermute | solution.py:24
  483.2 4.7 collective-permute-start.54
  490.4 8.1 %collective-permute-start.55 = (f32[8,64]{0,1:T(8,128)S(1)}, f32[8,64]{0,1:T(8,128)S(1)}, u32[]{:S(2)}, u32[]{:S(2)}) collective-permute-start(f32[8,64]{0,1:T(8,128)S(1)} %copy.162), channel_id=1, source_target_pairs={{0,8},{8,0},{16,24},{24,16},{1,9},{9,1},{17,25},{25,17},{2,10},{10... | collective-permute-start | bytes 6152 | tf_op jit(solution)/shard_map/ppermute | solution.py:24
  498.5 3.9 collective-permute-start.56
  503.4 5.8 collective-permute-start.60
  504.1 5.1 collective-permute-start.61
  512.3 16.3 %collective-permute-start.63 = (bf16[9,64,512]{2,1,0:T(8,128)(2,1)S(1)}, bf16[9,64,512]{2,1,0:T(8,128)(2,1)S(1)}, u32[]{:S(2)}, u32[]{:S(2)}) collective-permute-start(bf16[9,64,512]{2,1,0:T(8,128)(2,1)S(1)} %get-tuple-element.237), channel_id=1, source_target_pairs={{0,8},{8,0},{16,24},{24,16},{1,9},{9,1},{17,25},{25,17},{2,10},{10... | collective-permute-start | bytes 1769480 | tf_op jit(solution)/shard_map/ppermute | solution.py:24
  513.8 14.9 %collective-permute-start.64 = (bf16[9,64,512]{2,1,0:T(8,128)(2,1)S(1)}, bf16[9,64,512]{2,1,0:T(8,128)(2,1)S(1)}, u32[]{:S(2)}, u32[]{:S(2)}) collective-permute-start(bf16[9,64,512]{2,1,0:T(8,128)(2,1)S(1)} %get-tuple-element.238), channel_id=1, source_target_pairs={{0,16},{8,24},{16,0},{24,8},{1,17},{9,25},{17,1},{25,9},{2,18},{10... | collective-permute-start | bytes 1769480 | tf_op jit(solution)/shard_map/ppermute | solution.py:24
  514.7 14.0 %collective-permute-start.65 = (bf16[64,424]{1,0:T(8,128)(2,1)S(1)}, bf16[64,424]{1,0:T(8,128)(2,1)S(1)}, u32[]{:S(2)}, u32[]{:S(2)}) collective-permute-start(bf16[64,424]{1,0:T(8,128)(2,1)S(1)} %collective-permute-done.60), channel_id=1, source_target_pairs={{0,16},{8,24},{16,0},{24,8},{1,17},{9,25},{17,1},{25,9},{2,18},{10... | collective-permute-start | bytes 162824 | tf_op jit(solution)/shard_map/ppermute | solution.py:24
  536.7 43.1 %collective-permute-start.67 = (bf16[9,128,512]{2,1,0:T(8,128)(2,1)}, bf16[9,128,512]{2,1,0:T(8,128)(2,1)}, u32[]{:S(2)}, u32[]{:S(2)}) collective-permute-start(bf16[9,128,512]{2,1,0:T(8,128)(2,1)} %pad_maximum_fusion.22), channel_id=1, source_target_pairs={{0,16},{8,24},{16,0},{24,8},{1,17},{9,25},{17,1},{25,9},{2,18},{10... | collective-permute-start | bytes 3538952 | tf_op jit(solution)/shard_map/ppermute | solution.py:24
  537.4 42.4 %collective-permute-start.68 = (bf16[9,128,512]{2,1,0:T(8,128)(2,1)}, bf16[9,128,512]{2,1,0:T(8,128)(2,1)}, u32[]{:S(2)}, u32[]{:S(2)}) collective-permute-start(bf16[9,128,512]{2,1,0:T(8,128)(2,1)} %pad_maximum_fusion.23), channel_id=1, source_target_pairs={{0,8},{8,0},{16,24},{24,16},{1,9},{9,1},{17,25},{25,17},{2,10},{10... | collective-permute-start | bytes 3538952 | tf_op jit(solution)/shard_map/ppermute | solution.py:24
  (153 other events, 1903.6 us)
Sparse Core Ops, SparseCore 0:
  42.0 31.9 reduce-scatter.3
  244.9 32.6 reduce-scatter.5
  450.0 30.9 reduce-scatter.7
  534.3 25.5 all-gather.1
